TPU v7x, 128 devices: a whole 4x4x4 slice. The times are simulated.
128 devices in a mesh: gx: 4 (over z), gy: 32 (over x, y, core).
Axes of the slice: x: 4, y: 4, z: 4, core: 2. Of those that a mesh axis runs over, the one named last changes fastest.
Arguments:
- positions: float32 [3, 2097152], P(None, ('gx', 'gy')), may hold values from -0.5 to 0.5, as said below
- charges: float32 [2097152], P(('gx', 'gy')), may hold values from -0.36 to 0.36
- near_leaves: int32 [16384, 27], P(('gx', 'gy')), may hold values from -1 to 16383, as said below
- near_offsets: int32 [16384, 27], P(('gx', 'gy')), may hold values from 0 to 26, as said below
- far_leaves: int32 [16384, 189], P(('gx', 'gy')), may hold values from -1 to 2175, as said below
- far_leaf_class: int32 [16384, 189], P(('gx', 'gy')), may hold values from 0 to 15
- leaf_plan: int32 [128, 128, 16], P(('gx', 'gy')), may hold values from -1 to 127, as said below
- far_parents: int32 [2048, 189], P(('gx', 'gy')), may hold values from -1 to 527, as said below
- far_parent_class: int32 [2048, 189], P(('gx', 'gy')), may hold values from 0 to 15
- parent_plan: int32 [128, 128, 4], P(('gx', 'gy')), may hold values from -1 to 15, as said below
- coarse_lists: int32 [32, 7], replicated, may hold values from 0 to 31, as said below
- coarse_class: int32 [32, 7], replicated, may hold values from 0 to 15
- up_shift: float32 [8, 286, 286], replicated, may hold values from -4 to 4
- down_shift: float32 [8, 286, 286], replicated, may hold values from -4 to 4
- far_shift: float32 [16, 286, 286], replicated, may hold values from -2 to 2
Outputs:
- potential: float32 [2097152], P(('gx', 'gy'))
Inputs may be any that keep to these rules, and one draw needn't show every extreme that they name: `positions`: each coordinate lies within half a leaf width of its leaf centre. `near_leaves`: entry 0 of every list is the leaf itself with offset class 13; the other entries name leaves at most 32 before the first leaf or after the last leaf of the list's own device; -1 pads a list's tail. `near_offsets`: entry 0 is 13. `leaf_plan`: row d, column o lists distinct local indices of leaves of device o that device d names, then -1; at most 16 a pair, reached in every draw; a device names none of its own. `far_leaves`: slots name only own leaves or filled entries of the device's row of leaf_plan; -1 pads a list's tail. `parent_plan`: as leaf_plan, for parent cells, at most 4 a pair, reached in every draw. `far_parents`: slots name only own parents or filled entries of the device's row of parent_plan; -1 pads a list's tail. `coarse_lists`: each row names distinct cells other than its own.
All inputs are finite; a program needn't handle non-finite values.
Results may differ from a plain program's by a relative error of at most 0.0003.
Values sent between devices are 32-bit elements; how exact they have to be, the bound alone decides.
No kernel may reach another device: no remote copies, remote signals or barrier semaphores. Data moves between devices by JAX's collectives and lax.ppermute only.
A program may use at most 192 MiB of HBM per device.

v0:
```python
import jax
import jax.numpy as jnp
import numpy as np
from jax import lax
from jax.sharding import PartitionSpec as P

ORDER = 10
RIM = 32


softening = 0.05
highest = lax.Precision.HIGHEST


def extended_2(x, sides, width):
    for axis, dim in sides:
        size, length = (lax.axis_size(axis), x.shape[dim])
        up = [(i, (i + 1) % size) for i in range(size - 1)]
        down = [(j, i) for i, j in up]
        last = lax.slice_in_dim(x, length - width, length, axis=dim)
        first = lax.slice_in_dim(x, 0, width, axis=dim)
        before = lax.ppermute(last, axis, up)
        after = lax.ppermute(first, axis, down)
        x = jnp.concatenate([before, x, after], axis=dim)
    return x


def exponents(order):
    entries = []
    for degree in range(order + 1):
        for first_power in range(degree, -1, -1):
            for second_power in range(degree - first_power, -1, -1):
                entries.append((first_power, second_power, degree - first_power - second_power))
    return np.array(entries, dtype=np.int32).T


def basis(coords):
    scaled = 2.0 * coords
    powers = [jnp.ones_like(scaled)]
    for degree in range(ORDER):
        powers.append(powers[-1] * scaled)
    stacked = jnp.stack(powers)
    exponent_table = exponents(ORDER)
    return (
        stacked[exponent_table[0], 0]
        * stacked[exponent_table[1], 1]
        * stacked[exponent_table[2], 2]
    )


def upward(children, up_shift):
    grouped = children.reshape(children.shape[0], -1, 8)
    return jnp.einsum("cab,bnc->an", up_shift, grouped, precision=highest)


def downward(parents, down_shift):
    spread = jnp.einsum("cab,bn->anc", down_shift, parents, precision=highest)
    return spread.reshape(spread.shape[0], -1)


def far_field(sources, slots, classes, far_shift, block):
    targets, list_width = slots.shape
    operator_count = far_shift.shape[0]

    def one_block(pieces):
        slot_block, class_block = pieces
        present = slot_block >= 0
        columns = sources[:, jnp.maximum(slot_block, 0)]
        selector = (
            (class_block[..., None] == jnp.arange(operator_count, dtype=jnp.int32))
            & present[..., None]
        ).astype(jnp.float32)
        grouped = jnp.einsum("ctk,tko->otc", columns, selector, precision=highest)
        return jnp.einsum("oac,otc->at", far_shift, grouped, precision=highest)

    if targets <= block:
        return one_block((slots, classes))
    results = lax.map(
        one_block, (slots.reshape(-1, block, list_width), classes.reshape(-1, block, list_width))
    )
    return jnp.moveaxis(results, 0, 1).reshape(sources.shape[0], targets)


def near_sum(sources, targets, source_index, present, near_leaves, near_offsets, target_ids):
    leaf_count, leaf_size = (targets.shape[1], targets.shape[2])
    diagonal = jnp.eye(leaf_size, dtype=bool)

    def add_slot(entry_slot, running):
        source_rows = lax.dynamic_index_in_dim(source_index, entry_slot, 1, keepdims=False)
        neighbour = lax.dynamic_index_in_dim(near_leaves, entry_slot, 1, keepdims=False)
        counted_slot = lax.dynamic_index_in_dim(present, entry_slot, 1, keepdims=False)
        offset_class = lax.dynamic_index_in_dim(near_offsets, entry_slot, 1, keepdims=False)
        gathered = sources[:, source_rows]
        shift_x = (offset_class // 9 - 1).astype(jnp.float32)
        shift_y = (offset_class // 3 % 3 - 1).astype(jnp.float32)
        shift_z = (offset_class % 3 - 1).astype(jnp.float32)
        step_x = gathered[0][:, None, :] + shift_x[:, None, None] - targets[0][:, :, None]
        step_y = gathered[1][:, None, :] + shift_y[:, None, None] - targets[1][:, :, None]
        step_z = gathered[2][:, None, :] + shift_z[:, None, None] - targets[2][:, :, None]
        squared = step_x * step_x + step_y * step_y + step_z * step_z + softening * softening
        itself = (neighbour == target_ids) & (offset_class == 13)
        counted = counted_slot[:, None, None] & jnp.logical_not(
            itself[:, None, None] & diagonal[None]
        )
        contributions = jnp.where(counted, gathered[3][:, None, :] * lax.rsqrt(squared), 0.0)
        return running + jnp.sum(contributions, axis=2)

    return lax.fori_loop(
        0, near_leaves.shape[1], add_slot, jnp.zeros((leaf_count, leaf_size), jnp.float32)
    )


def deliver(outgoing):
    return lax.all_to_all(outgoing, ("gx", "gy"), split_axis=1, concat_axis=1, tiled=True)


def per_device(
    positions,
    charges,
    near_leaves,
    near_offsets,
    far_leaves,
    far_leaf_class,
    leaf_plan,
    far_parents,
    far_parent_class,
    parent_plan,
    coarse_lists,
    coarse_class,
    up_shift,
    down_shift,
    far_shift,
):
    coef_count = up_shift.shape[1]
    leaf_count = near_leaves.shape[0]
    leaf_size = positions.shape[1] // leaf_count
    device = lax.axis_index(("gx", "gy"))
    leaf_basis = basis(positions)
    leaf_multipoles = (leaf_basis * charges).reshape(coef_count, leaf_count, leaf_size).sum(axis=2)
    parent_multipoles = upward(leaf_multipoles, up_shift)
    grand_multipoles = upward(parent_multipoles, up_shift)
    grand_count = grand_multipoles.shape[1]
    grand_ids = device * grand_count + jnp.arange(grand_count, dtype=jnp.int32)
    coarse_count = coarse_lists.shape[0]
    lifted = jnp.einsum("gab,bg->ag", up_shift[grand_ids % 8], grand_multipoles, precision=highest)
    member = (grand_ids[:, None] // 8 == jnp.arange(coarse_count, dtype=jnp.int32)[None, :]).astype(
        jnp.float32
    )
    coarse_multipoles = lax.psum(jnp.dot(lifted, member, precision=highest), ("gx", "gy"))
    coarse_locals = far_field(coarse_multipoles, coarse_lists, coarse_class, far_shift, 256)
    grand_locals = jnp.einsum(
        "gab,bg->ag", down_shift[grand_ids % 8], coarse_locals[:, grand_ids // 8], precision=highest
    )
    leaf_capacity = leaf_plan.shape[2]
    requests = lax.all_to_all(
        jnp.concatenate([leaf_plan, parent_plan], 2),
        ("gx", "gy"),
        split_axis=1,
        concat_axis=0,
        tiled=True,
    )
    asked = jnp.maximum(requests[:, 0, :], 0)
    outgoing = jnp.concatenate(
        [
            leaf_multipoles[:, asked[:, :leaf_capacity]],
            parent_multipoles[:, asked[:, leaf_capacity:]],
        ],
        2,
    )
    arrived = deliver(outgoing)
    leaf_sources = jnp.concatenate(
        [leaf_multipoles, arrived[:, :, :leaf_capacity].reshape(coef_count, -1)], 1
    )
    parent_sources = jnp.concatenate(
        [parent_multipoles, arrived[:, :, leaf_capacity:].reshape(coef_count, -1)], 1
    )
    parent_locals = downward(grand_locals, down_shift) + far_field(
        parent_sources, far_parents, far_parent_class, far_shift, 64
    )
    leaf_locals = downward(parent_locals, down_shift) + far_field(
        leaf_sources, far_leaves, far_leaf_class, far_shift, 64
    )
    far_values = jnp.einsum(
        "alp,al->lp",
        leaf_basis.reshape(coef_count, leaf_count, leaf_size),
        leaf_locals,
        precision=highest,
    )
    particle_data = jnp.concatenate([positions, charges[None]], 0).reshape(4, leaf_count, leaf_size)
    extended = extended_2(particle_data, ((("gx", "gy"), 1),), RIM)
    first_leaf = device * leaf_count
    present = near_leaves >= 0
    source_index = jnp.where(present, near_leaves - first_leaf + RIM, 0)
    target_ids = first_leaf + jnp.arange(leaf_count, dtype=jnp.int32)
    near_values = near_sum(
        extended, particle_data, source_index, present, near_leaves, near_offsets, target_ids
    )
    return (near_values + far_values).reshape(-1)


def solution(mesh):
    placed = (
        P(None, ("gx", "gy")),
        P(("gx", "gy")),
        P(("gx", "gy"), None),
        P(("gx", "gy"), None),
        P(("gx", "gy"), None),
        P(("gx", "gy"), None),
        P(("gx", "gy"), None, None),
        P(("gx", "gy"), None),
        P(("gx", "gy"), None),
        P(("gx", "gy"), None, None),
        P(),
        P(),
        P(),
        P(),
        P(),
    )
    return jax.shard_map(
        per_device, mesh=mesh, in_specs=placed, out_specs=P(("gx", "gy")), check_vma=False
    )
```

profile of v0, /device:TPU:1, one launch (start us, length us, event | category | flops | bytes accessed | tf_op | source)
XLA Modules:
  0.0 1314.4 jit_solution(2198373858361831574)
XLA Ops:
  1.6 12.0 all-to-all-start
  46.5 51.1 %gather_fusion.2 = f32[286,16384]{1,0:T(8,128)} fusion(f32[11,3,16384]{2,1,0:T(4,128)} %bitcast_dynamic-update-slice_fusion, s32[286]{0:T(512)S(1)} %copy-done.7), kind=kCustom, calls=%fused_computation.2 | custom fusion | bytes 37488880 | tf_op jit(solution)/shard_map/gather | solution.py:45
  97.7 51.0 %gather_fusion.3 = f32[286,16384]{1,0:T(8,128)} fusion(f32[11,3,16384]{2,1,0:T(4,128)} %bitcast_dynamic-update-slice_fusion, s32[286]{0:T(512)S(1)} %copy-done.6), kind=kCustom, calls=%fused_computation.3 | custom fusion | bytes 37488880 | tf_op jit(solution)/shard_map/gather | solution.py:46
  148.7 50.2 %gather_fusion.4 = f32[286,16384]{1,0:T(8,128)} fusion(f32[11,3,16384]{2,1,0:T(4,128)} %bitcast_dynamic-update-slice_fusion, s32[286]{0:T(512)S(1)} %copy-done.5), kind=kCustom, calls=%fused_computation.4 | custom fusion | bytes 37488880 | tf_op jit(solution)/shard_map/gather | solution.py:47
  198.9 18.1 %multiply_multiply_fusion = f32[286,16384]{1,0:T(8,128)S(1)} fusion(f32[286,16384]{1,0:T(8,128)} %gather_fusion.4, f32[286,16384]{1,0:T(8,128)} %gather_fusion.2, f32[286,16384]{1,0:T(8,128)} %gather_fusion.3), kind=kLoop, calls=%fused_computation.60 | loop fusion | flops 9371648 | bytes 74973184 | tf_op jit(solution)/shard_map/mul | solution.py:45
  217.0 7.5 copy.171
  224.5 17.7 %multiply_reduce_fusion = (f32[286,128]{1,0:T(8,128)}, f32[286,128,128]{2,1,0:T(8,128)}) fusion(f32[128,128]{1,0:T(8,128)S(1)} %bitcast.247, f32[288,128,128]{2,1,0:T(8,128)} %bitcast.227), kind=kLoop, calls=%fused_computation.61 | loop fusion | flops 9335040 | bytes 37698560 | tf_op jit(solution)/shard_map/reduce_sum | solution.py:139
  243.9 5.5 fusion.39
  249.5 3.9 fusion.52
  264.0 8.1 copy.146
  280.4 5.0 gather_fusion.5
  288.9 67.6 %psum.7 = f32[286,32]{0,1:T(8,128)} all-reduce(f32[286,32]{0,1:T(8,128)} %fusion.88), channel_id=1, replica_groups=mesh['gx'=4,'gy'=32] {'gx','gy'}, use_global_device_ids=true, to_apply=%region_4.5 | all-reduce | flops 9152 | bytes 73216 | tf_op jit(solution)/shard_map/psum | solution.py:149
  362.9 10.1 convolution_bitcast_fusion.1
  373.0 4.9 gather_fusion.8
  381.3 4.4 fusion.47
  391.3 10.0 gather_fusion.9
  401.3 4.7 pad_maximum_fusion
  406.0 7.4 all-to-all-start.1
  415.5 582.0 %while.28 = (s32[]{:T(128)}, f32[128,128]{1,0:T(8,128)}, pred[128,27]{0,1:T(8,128)(4,1)}, s32[128,27]{0,1:T(8,128)}, s32[128,27]{0,1:T(8,128)}, /*index=5*/s32[1...) while((s32[]{:T(128)}, f32[128,128]{1,0:T(8,128)}, ...), condition=%wide.region_2.3_spmd.clone, body=%wide.region_0.2_spmd.clone.sunk | while | flops 31544960 | bytes 2600203 | solution.py:108
  423.6 11.9 select_reduce_fusion.2
  445.1 11.9 select_reduce_fusion.2
  466.6 11.9 select_reduce_fusion.2
  488.1 11.9 select_reduce_fusion.2
  509.7 11.9 select_reduce_fusion.2
  531.2 11.9 select_reduce_fusion.2
  552.7 11.9 select_reduce_fusion.2
  574.2 11.9 select_reduce_fusion.2
  595.8 11.9 select_reduce_fusion.2
  617.3 11.9 select_reduce_fusion.2
  638.9 11.9 select_reduce_fusion.2
  660.4 11.9 select_reduce_fusion.2
  681.9 11.9 select_reduce_fusion.2
  703.5 11.9 select_reduce_fusion.2
  725.0 11.9 select_reduce_fusion.2
  746.5 11.9 select_reduce_fusion.2
  768.1 11.9 select_reduce_fusion.2
  789.7 11.9 select_reduce_fusion.2
  811.3 11.9 select_reduce_fusion.2
  832.9 11.9 select_reduce_fusion.2
  854.5 11.9 select_reduce_fusion.2
  876.1 11.9 select_reduce_fusion.2
  897.7 11.9 select_reduce_fusion.2
  919.3 11.9 select_reduce_fusion.2
  940.9 11.9 select_reduce_fusion.2
  962.5 11.9 select_reduce_fusion.2
  984.0 11.9 select_reduce_fusion.2
  1004.3 14.3 %gather_fusion.11 = f32[3024,286]{1,0:T(8,128)} fusion(f32[286,528]{0,1:T(8,128)} %pad_maximum_fusion.2, s32[3072]{0:T(1024)S(1)} %copy-done.14), kind=kCustom, calls=%fused_computation.11 | custom fusion | bytes 6931008 | tf_op jit(solution)/shard_map/gather | solution.py:68
  1018.6 5.6 copy.151
  1024.2 8.9 reshape.507
  1033.1 7.2 fusion.41
  1040.3 9.4 fusion.51
  1049.7 4.5 fusion.44
  1056.6 227.1 %while.27 = (s32[]{:T(128)}, f32[2,286,64]{1,2,0:T(8,128)}, s32[2,64,189]{2,1,0:T(8,128)}, s32[2,64,189]{2,1,0:T(8,128)}, f32[286,2176]{0,1:T(8,128)S(1)}, /*index=5*/f32[16,286,286]{2,1,0:T(8,128)}, s32[]{:T(128)}) while((s32[]{:T(128)}, f32[2,286,64]{1,2,0:T(8,128)}, s32[2,64,189]{2,1,0:T(8,128)}, s32[2,64,189]{2,1,0:T(8,128)}, ...), condition=%wide.region_6.7_spmd, body=%wide.region_5.6_spmd.sunk | while | flops 1669748352 | bytes 107328752 | solution.py:78
  1057.8 30.9 %gather_fusion = f32[12096,286]{1,0:T(8,128)} fusion(f32[286,2176]{0,1:T(8,128)S(1)} %get-tuple-element.655, s32[12288]{0:T(1024)S(1)} %pad_clamp_fusion.9), kind=kCustom, calls=%fused_computation.1.clone.1 | custom fusion | bytes 27724032 | tf_op jit(solution)/shard_map/while/body/eval_jaxpr/gather | solution.py:68
  1088.8 17.1 %copy.241 = f32[12096,286]{0,1:T(8,128)} copy(f32[12096,286]{1,0:T(8,128)} %gather_fusion) | data formatting | bytes 27675648 | tf_op jit(solution)/shard_map/while/body/eval_jaxpr/gather | solution.py:68
  1105.8 28.2 %reshape.545 = f32[64,189,286]{1,0,2:T(8,128)} reshape(f32[12096,286]{0,1:T(8,128)} %copy.241) | data formatting | bytes 27675648 | tf_op jit(solution)/shard_map/while/body/eval_jaxpr/gather | solution.py:68
  1134.9 25.2 %fusion.116 = f32[16,64,286]{2,0,1:T(8,128)S(1)} fusion(f32[286,64,189]{2,1,0:T(8,128)} %bitcast.224, s32[64,189]{1,0:T(8,128)S(1)} %dynamic-slice_bitcast_fusion.4, pred[64,189]{1,0:T(8,128)(4,1)S(1)} %compare_bitcast_fusion.2), kind=kOutput, calls=%fused_computation.18.clone.1 | convolution fusion | flops 664602624 | bytes 15069760 | tf_op jit(solution)/shard_map/while/body/eval_jaxpr/ctk,tko->otc/dot_general | solution.py:73
  1160.1 10.0 fusion.117
  1171.2 30.9 %gather_fusion = f32[12096,286]{1,0:T(8,128)} fusion(f32[286,2176]{0,1:T(8,128)S(1)} %get-tuple-element.655, s32[12288]{0:T(1024)S(1)} %pad_clamp_fusion.9), kind=kCustom, calls=%fused_computation.1.clone.1 | custom fusion | bytes 27724032 | tf_op jit(solution)/shard_map/while/body/eval_jaxpr/gather | solution.py:68
  1202.1 17.1 %copy.241 = f32[12096,286]{0,1:T(8,128)} copy(f32[12096,286]{1,0:T(8,128)} %gather_fusion) | data formatting | bytes 27675648 | tf_op jit(solution)/shard_map/while/body/eval_jaxpr/gather | solution.py:68
  1219.2 28.2 %reshape.545 = f32[64,189,286]{1,0,2:T(8,128)} reshape(f32[12096,286]{0,1:T(8,128)} %copy.241) | data formatting | bytes 27675648 | tf_op jit(solution)/shard_map/while/body/eval_jaxpr/gather | solution.py:68
  1248.3 25.2 %fusion.116 = f32[16,64,286]{2,0,1:T(8,128)S(1)} fusion(f32[286,64,189]{2,1,0:T(8,128)} %bitcast.224, s32[64,189]{1,0:T(8,128)S(1)} %dynamic-slice_bitcast_fusion.4, pred[64,189]{1,0:T(8,128)(4,1)S(1)} %compare_bitcast_fusion.2), kind=kOutput, calls=%fused_computation.18.clone.1 | convolution fusion | flops 664602624 | bytes 15069760 | tf_op jit(solution)/shard_map/while/body/eval_jaxpr/ctk,tko->otc/dot_general | solution.py:73
  1273.4 10.0 fusion.117
  1284.8 28.5 %fusion.29 = f32[128,1,128]{2,1,0:T(1,128)S(1)} fusion(f32[286,128,128]{2,1,0:T(8,128)} %get-tuple-element.481, f32[286,128,1]{0,1,2:T(8,128)S(1)} %bitcast.243), kind=kOutput, calls=%fused_computation.58 | convolution fusion | flops 56229888 | bytes 18955264 | tf_op jit(solution)/shard_map/alp,al->lp/dot_general | solution.py:183
  (438 shorter events, 350.0 us)
Async XLA Ops:
  0.0 373.0 %copy-start = (f32[8,286,286]{2,0,1:T(8,128)S(1)}, f32[8,286,286]{2,0,1:T(8,128)}, u32[]{:S(2)}) copy-start(f32[8,286,286]{2,0,1:T(8,128)} %param.38) | copy-start | bytes 7852420
  0.0 46.5 %copy-start.7 = (s32[286]{0:T(512)S(1)}, s32[286]{0:T(512)}, u32[]{:S(2)}) copy-start(s32[286]{0:T(512)} %constant.313) | copy-start | bytes 3436
  1.6 273.8 %all-to-all-start = ((s32[1,128,20]{2,0,1:T(1,128)}), s32[1,128,20]{2,0,1:T(1,128)}, u32[]{:S(2)}, u32[]{:S(2)}) async-start(s32[1,128,20]{2,0,1:T(1,128)} %copy.149), calls=%async_computation | async-start | bytes 131072 | tf_op jit(solution)/shard_map/all_to_all | solution.py:155
  14.6 0.7 copy-start.9
  16.6 396.8 %collective-permute-start = (f32[4,32,128]{2,1,0:T(8,128)}, f32[4,32,128]{2,1,0:T(8,128)}, u32[]{:S(2)}, u32[]{:S(2)}) collective-permute-start(f32[4,32,128]{2,1,0:T(8,128)} %get-tuple-element.482), channel_id=1, source_target_pairs={{0,1},{1,2},{2,3},{3,4},{4,5},{5,6},{6,7},{7,8},{8,9},{9,10},{10,1... | collective-permute-start | bytes 196616 | tf_op jit(solution)/shard_map/ppermute | solution.py:22
  20.2 393.3 %collective-permute-start.1 = (f32[4,32,128]{2,1,0:T(8,128)}, f32[4,32,128]{2,1,0:T(8,128)}, u32[]{:S(2)}, u32[]{:S(2)}) collective-permute-start(f32[4,32,128]{2,1,0:T(8,128)} %get-tuple-element.483), channel_id=1, source_target_pairs={{1,0},{2,1},{3,2},{4,3},{5,4},{6,5},{7,6},{8,7},{9,8},{10,9},{11,1... | collective-permute-start | bytes 196616 | tf_op jit(solution)/shard_map/ppermute | solution.py:23
  22.8 22.0 %copy-start.4 = (f32[3,16384]{1,0:T(4,128)S(1)}, f32[3,16384]{1,0:T(4,128)}, u32[]{:S(2)}) copy-start(f32[3,16384]{1,0:T(4,128)} %param.25) | copy-start | bytes 589828
  46.5 51.2 %copy-start.6 = (s32[286]{0:T(512)S(1)}, s32[286]{0:T(512)}, u32[]{:S(2)}) copy-start(s32[286]{0:T(512)} %constant.321) | copy-start | bytes 3436
  97.7 51.0 %copy-start.5 = (s32[286]{0:T(512)S(1)}, s32[286]{0:T(512)}, u32[]{:S(2)}) copy-start(s32[286]{0:T(512)} %constant.329) | copy-start | bytes 3436
  217.0 7.5 copy-start.11
  242.2 16.7 %copy-start.13 = (s32[128,27]{0,1:T(8,128)S(1)}, s32[128,27]{0,1:T(8,128)}, u32[]{:S(2)}) copy-start(s32[128,27]{0,1:T(8,128)} %param.27) | copy-start | bytes 41476
  243.9 5.6 copy-start.3
  272.1 13.3 %copy-start.16 = (f32[286,2,1]{0,1,2:T(2,128)S(1)}, f32[286,2,1]{0,1,2:T(2,128)}, u32[]{:S(2)}) copy-start(f32[286,2,1]{0,1,2:T(2,128)} %fusion.52) | copy-start | bytes 6868
  406.0 591.5 %all-to-all-start.1 = ((f32[286,128,20]{0,2,1:T(8,128)}), f32[286,128,20]{0,2,1:T(8,128)}, u32[]{:S(2)}, u32[]{:S(2)}) async-start(f32[286,128,20]{0,2,1:T(8,128)} %pad_maximum_fusion), calls=%async_computation.1 | async-start | bytes 9437184 | tf_op jit(solution)/shard_map/all_to_all | solution.py:114
  997.5 6.8 copy-start.14
  1024.2 8.9 copy-start.15
  1024.2 16.1 %copy-start.12 = (f32[286,2,8]{0,1,2:T(2,128)S(1)}, f32[286,2,8]{0,1,2:T(2,128)}, u32[]{:S(2)}) copy-start(f32[286,2,8]{0,1,2:T(2,128)} %fusion.47) | copy-start | bytes 54916
  1049.7 6.6 copy-start.2
  1105.8 28.2 %copy-start.8 = (s32[2,64,189]{2,1,0:T(8,128)S(1)}, s32[2,64,189]{2,1,0:T(8,128)}, u32[]{:S(2)}) copy-start(s32[2,64,189]{2,1,0:T(8,128)} %get-tuple-element.654) | copy-start | bytes 290308 | tf_op jit(solution)/shard_map/while
  1219.2 28.2 %copy-start.8 = (s32[2,64,189]{2,1,0:T(8,128)S(1)}, s32[2,64,189]{2,1,0:T(8,128)}, u32[]{:S(2)}) copy-start(s32[2,64,189]{2,1,0:T(8,128)} %get-tuple-element.654) | copy-start | bytes 290308 | tf_op jit(solution)/shard_map/while
  1284.8 28.6 %copy-start.10 = (f32[128,128]{1,0:T(8,128)S(1)}, f32[128,128]{1,0:T(8,128)}, u32[]{:S(2)}) copy-start(f32[128,128]{1,0:T(8,128)} %get-tuple-element.320) | copy-start | bytes 196612
  1284.8 29.2 %copy-start.1 = (f32[8,286,286]{2,0,1:T(8,128)S(1)}, f32[8,286,286]{2,0,1:T(8,128)}, u32[]{:S(2)}) copy-start(f32[8,286,286]{2,0,1:T(8,128)} %param.38) | copy-start | bytes 7852420
where the time goes:
time: 1330 us; the launch traced here: 1310 us
  local copies, waits for them, and re-layouts  562 us (42%)
  other arithmetic  507 us (38%)
  matrix products  151 us (11%)
  blocking collectives  67.6 us (5%)
  starting transfers between devices  24.8 us (2%)
    reduce_sum x27, other arithmetic, add_slot(): return running + jnp.sum(contributions, axis=2)  322 us
    gather x11, local copies, waits for them, and re-layouts, one_block(): columns = sources[:, jnp.maximum(slot_block, 0)]  186 us
    psum x1, blocking collectives, per_device(): lax.psum(jnp.dot(lifted, member, precision=highest), ('gx', 'gy'))  67.6 us
    gather x27, local copies, waits for them, and re-layouts, add_slot(): gathered = sources[:, source_rows]  66.1 us
    dot_general x4, matrix products, one_block(): grouped = jnp.einsum('ctk,tko->otc', columns, selector, precision=highest)  59.4 us
    gather x1, local copies, waits for them, and re-layouts, basis(): stacked[exponent_table[0], 0] * stacked[exponent_table[1], 1]  51.1 us
    gather x1, local copies, waits for them, and re-layouts, basis(): stacked[exponent_table[1], 1]  51 us
    gather x1, local copies, waits for them, and re-layouts, basis(): stacked[exponent_table[2], 2]  50.2 us
  transfers between devices with their start and end apart: 4, of which 0 were waited for; matrix products, arithmetic and copies ran while one was open for 69% of the time, Pallas kernels for 0%

commit v1 on v0

v1 whole, which is shorter than its diff:
```python
import jax
import jax.numpy as jnp
import numpy as np
from jax import lax
from jax.experimental import pallas as pl
from jax.experimental.pallas import tpu as pltpu
from jax.sharding import PartitionSpec as P

ORDER = 10
COEF = 286
RIM = 32
LEAF = 128
K_NEAR = 27
CAP_L = 16
CAP_P = 4
ROWS = 48
TARGETS = 160
GROUP = 8
SOFT = 0.05 * 0.05
AXES = ("gx", "gy")
F32 = jnp.float32
BF16 = jnp.bfloat16
VMEM = pl.BlockSpec(memory_space=pltpu.VMEM)
SMEM = pl.BlockSpec(memory_space=pltpu.SMEM)


def exponents(order):
    entries = []
    for degree in range(order + 1):
        for first_power in range(degree, -1, -1):
            for second_power in range(degree - first_power, -1, -1):
                entries.append((first_power, second_power, degree - first_power - second_power))
    return entries


INDEX = {powers: number for number, powers in enumerate(exponents(ORDER))}


def split(x):
    high = x.astype(BF16)
    return high, (x - high.astype(F32)).astype(BF16)


def nt(a, b):
    return lax.dot_general(a, b, (((1,), (1,)), ((), ())), preferred_element_type=F32)


def nn(a, b):
    return jnp.dot(a, b, preferred_element_type=F32)


def apply_operator(rows, operator):
    row_high, row_low = split(rows)
    high, low = split(operator)
    return nt(row_high, high) + (nt(row_low, high) + nt(row_high, low))


def joined(ref, rows):
    return jnp.concatenate([ref[h, rows, :] for h in range(3)], axis=1)[:, :COEF]


def upward_kernel(dev_ref, pos_ref, chg_ref, up_ref, lt_ref, pt_ref, lift_ref, moments, wide):
    x, y, z = [2.0 * pos_ref[d].T for d in range(3)]
    with_x = chg_ref[...].T
    z_powers = [None, z]
    for k in range(ORDER - 1):
        z_powers.append(z_powers[-1] * z)
    moments[COEF - 6 : 384, :] = jnp.zeros((384 - COEF + 6, LEAF), F32)
    for i in range(ORDER + 1):
        if i:
            with_x = with_x * x
        with_xy = with_x
        for j in range(ORDER + 1 - i):
            if j:
                with_xy = with_xy * y
            for k in range(ORDER + 1 - i - j):
                term = with_xy * z_powers[k] if k else with_xy
                a = INDEX[(i, j, k)]
                moments[a : a + 1, :] = jnp.sum(term, axis=0, keepdims=True)
    for h in range(3):
        lt_ref[h] = moments[128 * h : 128 * h + 128, :].T
    wide[...] = jnp.zeros_like(wide)
    total = jnp.zeros((16, COEF), F32)
    for c in range(8):
        total = total + apply_operator(joined(lt_ref, pl.ds(c, 16, stride=8)), up_ref[c])
    wide[:, :COEF] = total
    for h in range(3):
        pt_ref[h] = wide[:, 128 * h : 128 * h + 128]
    grand = jnp.zeros((2, COEF), F32)
    for c in range(8):
        rows = jnp.concatenate([wide[c : c + 1, :COEF], wide[8 + c : 9 + c, :COEF]], axis=0)
        grand = grand + apply_operator(rows, up_ref[c])
    first = lax.rem(2 * dev_ref[0], 8)
    lifted = apply_operator(grand[0:1], up_ref[first]) + apply_operator(grand[1:2], up_ref[first + 1])
    wide[0:1, :COEF] = lifted
    for h in range(3):
        lift_ref[h : h + 1, :] = wide[0:1, 128 * h : 128 * h + 128]


def pack_kernel(asked_ref, lt_ref, pt_ref, lift_ref, out_ref):
    lane = lax.broadcasted_iota(jnp.int32, (128, 128), 1)
    leaf_rows = jnp.concatenate([lt_ref[h] for h in range(3)], axis=1)
    parent_rows = jnp.concatenate([pt_ref[h] for h in range(3)], axis=1)
    parent_rows = jnp.concatenate([parent_rows, jnp.zeros((112, 384), F32)], axis=0)
    leaf_rows = jnp.concatenate(split(leaf_rows), axis=0)
    parent_rows = jnp.concatenate(split(parent_rows), axis=0)
    for q in range(5):
        tail = jnp.zeros((128, 128), F32)
        for p in range(4):
            j = 4 * q + p
            chosen = jnp.where(asked_ref[:, j : j + 1] == lane, 1.0, 0.0).astype(BF16)
            chosen = jnp.concatenate([chosen, chosen], axis=1)
            rows = nn(chosen, leaf_rows if q < 4 else parent_rows)
            out_ref[:, 2 * j, :] = rows[:, 0:128]
            out_ref[:, 2 * j + 1, :] = rows[:, 128:256]
            part = rows[:, 256:384]
            tail = tail + (pltpu.roll(part, 32 * p, 1) if p else part)
        out_ref[:, 40 + q, :] = tail
    for h in range(3):
        out_ref[:, 45 + h, :] = jnp.broadcast_to(lift_ref[h : h + 1, :], (128, 128))


def near_kernel(code_ref, count_ref, self_ref, own_ref, before_ref, after_ref, out_ref,
                eight, offsets, features, spread, sums, even, odd, plan_even, plan_odd):
    sub = lax.broadcasted_iota(jnp.int32, (8, 128), 0)
    zeros = jnp.zeros((8, 128), F32)
    eight[...] = jnp.zeros_like(eight)
    for d, row in ((0, 0), (1, 1), (2, 2), (3, 5)):
        eight[0:RIM, row, :] = before_ref[d]
        eight[RIM : RIM + LEAF, row, :] = own_ref[d]
        eight[RIM + LEAF : 2 * RIM + LEAF, row, :] = after_ref[d]
    for o in range(27):
        shift = (o // 9 - 1, o // 3 % 3 - 1, o % 3 - 1)
        table = jnp.where(sub == 3, SOFT, jnp.where(sub == 4, 1.0, zeros))
        for d in range(3):
            table = jnp.where(sub == d, -float(shift[d]), table)
        offsets[o] = table

    def thirds(v):
        high = v.astype(BF16).astype(F32)
        rest = v - high
        middle = rest.astype(BF16).astype(F32)
        return high, middle, rest - middle

    def norm(v):
        return jnp.sum(jnp.where(sub < 3, v * v, 0.0), axis=0, keepdims=True)

    def target(leaf, offset):
        v = eight[RIM + leaf] + offsets[offset]
        v = jnp.where(sub == 3, v + norm(v), v)
        high, middle, low = thirds(v)
        rows = jnp.concatenate([high, high, high, middle, middle, low], axis=0)
        rows = jnp.concatenate([rows, jnp.zeros((80, 128), F32)], axis=0)
        return rows.astype(BF16)

    def source(leaf):
        v = eight[leaf]
        v = jnp.where(sub < 3, -2.0 * v, jnp.where(sub == 3, 1.0, jnp.where(sub == 4, norm(v), 0.0)))
        high, middle, low = thirds(v)
        rows = jnp.concatenate([high, middle, low, high, middle, high], axis=0)
        rows = jnp.concatenate([rows, jnp.zeros((80, 128), F32)], axis=0)
        features[leaf] = rows.T.astype(BF16)
        charge = jnp.broadcast_to(eight[leaf, 5:6, :], (128, 128))
        spread[leaf] = charge.T

    def prepare(step, carry):
        for u in range(4):
            source(4 * step + u)
        return carry

    lax.fori_loop(0, (LEAF + 2 * RIM) // 4, prepare, 0)
    diagonal = lax.broadcasted_iota(jnp.int32, (128, 128), 0) == lax.broadcasted_iota(
        jnp.int32, (128, 128), 1
    )

    def own_leaf(step, carry):
        for u in range(4):
            leaf = 4 * step + u
            squared = nn(features[RIM + leaf], target(leaf, 13))
            terms = jnp.where(diagonal, 0.0, spread[RIM + leaf] * lax.rsqrt(squared))
            sums[leaf] = jnp.sum(terms.reshape(16, 8, 128), axis=0) * self_ref[leaf].astype(F32)
        return carry

    lax.fori_loop(0, LEAF // 4, own_leaf, 0)

    def produce(buffer, plan, state):
        leaf, entry = state
        for g in range(GROUP):
            done = entry >= count_ref[leaf]
            leaf = jnp.where(done, jnp.minimum(leaf + 1, LEAF), leaf)
            entry = jnp.where(done, 1, entry)
            code = code_ref[leaf * K_NEAR + entry]
            entry = entry + 1
            real = code >= 0
            code = jnp.maximum(code, 0)
            place = jnp.minimum(leaf, LEAF - 1)
            plan[g] = code // 32
            plan[GROUP + g] = place
            plan[2 * GROUP + g] = jnp.where(real, 1, 0)
            buffer[g] = nn(features[code // 32], target(place, lax.rem(code, 32)))
        return leaf, entry

    def consume(buffer, plan):
        for g in range(GROUP):
            terms = spread[plan[g]] * lax.rsqrt(buffer[g])
            place = plan[GROUP + g]
            part = jnp.sum(terms.reshape(16, 8, 128), axis=0)
            sums[place] = sums[place] + part * plan[2 * GROUP + g].astype(F32)

    state = produce(even, plan_even, (jnp.int32(0), jnp.int32(1)))

    def two_groups(step, state):
        state = produce(odd, plan_odd, state)
        consume(even, plan_even)
        state = produce(even, plan_even, state)
        consume(odd, plan_odd)
        return state

    total = count_ref[LEAF + 1]
    lax.fori_loop(0, (total + 2 * GROUP - 1) // (2 * GROUP), two_groups, state)
    out_ref[...] = jnp.sum(sums[...], axis=1)


def count_rows(code, low, rows):
    wide = lax.broadcasted_iota(jnp.int32, (rows, 256), 0) == code
    narrow = lax.broadcasted_iota(jnp.int32, (128, 256), 0) == low
    return nt(
        jnp.where(wide, 1.0, 0.0).astype(BF16), jnp.where(narrow, 1.0, 0.0).astype(BF16)
    ).astype(BF16)


def counts_kernel(leaf_ref, leaf_class_ref, parent_ref, parent_class_ref, s_ref, sp_ref,
                  code_scr, low_scr):
    code_scr[...] = jnp.full_like(code_scr, -1)
    low_scr[...] = jnp.full_like(low_scr, -1)

    def one_level(slot_ref, class_ref, cells, capacity, out_ref):
        slots = slot_ref[...]
        ghost = jnp.maximum(slots - cells, 0)
        own = slots < cells
        position = lax.rem(ghost, capacity)
        code = jnp.where(own, 0, 1 + position) * 16 + class_ref[...]
        code_scr[:, : slots.shape[1]] = jnp.where(slots < 0, -1, code)
        low_scr[:, : slots.shape[1]] = jnp.where(own, slots, lax.div(ghost, capacity))
        blocks = capacity + 1
        for t in range(16):
            table = count_rows(code_scr[t : t + 1, :], low_scr[t : t + 1, :], 16 * blocks)
            for b in range(blocks):
                out_ref[16 * t : 16 * t + 16, 128 * b : 128 * b + 128] = table[16 * b : 16 * b + 16]

    one_level(leaf_ref, leaf_class_ref, LEAF, CAP_L, s_ref)

    @pl.when(pl.program_id(0) == 0)
    def _():
        one_level(parent_ref, parent_class_ref, 16, CAP_P, sp_ref)


def far_kernel(dev_ref, lists_ref, class_ref, s_ref, sp_ref, lt_ref, pt_ref, arrived_ref, pos_ref,
               near_ref, down_hbm, far_hbm, out_ref,
               src, src_parent, grouped, locals_rows, wide, loc, result, down_ref, far_ref, sems):
    step = pl.program_id(0)
    lane = lax.broadcasted_iota(jnp.int32, (128, 128), 1)

    def place(ref, row, parts):
        count = parts[0].shape[0]
        (h0, l0), (h1, l1) = split(parts[0]), split(parts[1])
        tail = parts[2]
        high = tail.astype(BF16).astype(F32)
        low = pltpu.roll(tail - high, 32, 1)
        ref[row : row + count, 0:128] = h0
        ref[row : row + count, 128:256] = h1
        ref[row : row + count, 256:384] = l0
        ref[row : row + count, 384:512] = l1
        ref[row : row + count, 512:640] = (high + low).astype(BF16)

    def collect(product, row, count):
        grouped[0, pl.ds(row, count), :] = product[:, 0:128] + product[:, 256:384]
        grouped[1, pl.ds(row, count), :] = product[:, 128:256] + product[:, 384:512]
        tail = product[:, 512:640]
        grouped[2, pl.ds(row, count), :] = tail + pltpu.roll(tail, 96, 1)

    def arrived_tail(row, p):
        part = arrived_ref[:, row, :]
        part = pltpu.roll(part, 128 - 32 * p, 1) if p else part
        return jnp.where(lane < 32, part, 0.0)

    @pl.when(step == 0)
    def _():
        pltpu.make_async_copy(down_hbm, down_ref, sems.at[0]).start()
        pltpu.make_async_copy(far_hbm, far_ref, sems.at[1]).start()
        place(src, 0, [lt_ref[h] for h in range(3)])
        for c in range(CAP_L):
            place(
                src,
                128 * (c + 1),
                [arrived_ref[:, 2 * c, :], arrived_ref[:, 2 * c + 1, :], arrived_tail(40 + c // 4, c % 4)],
            )
        own = [jnp.concatenate([pt_ref[h], jnp.zeros((112, 128), F32)], axis=0) for h in range(3)]
        place(src_parent, 0, own)
        for c in range(CAP_P):
            place(
                src_parent,
                128 * (c + 1),
                [arrived_ref[:, 32 + 2 * c, :], arrived_ref[:, 33 + 2 * c, :], arrived_tail(44, c)],
            )
        collect(nn(sp_ref[...], src_parent[...]), 2048, 256)
        mine = dev_ref[0] // 4
        operator = lax.broadcasted_iota(jnp.int32, (16, 128), 0)
        cell = lax.broadcasted_iota(jnp.int32, (16, 128), 1) // 4
        chosen = jnp.zeros((16, 128), F32)
        for k in range(7):
            hit = (operator == class_ref[mine * 7 + k]) & (cell == lists_ref[mine * 7 + k])
            chosen = chosen + jnp.where(hit, 1.0, 0.0)
        chosen = chosen.astype(BF16)
        for h in range(3):
            high, low = split(arrived_ref[:, 45 + h, :])
            grouped[h, 2304:2320, :] = nn(chosen, high) + nn(chosen, low)
            grouped[h, 2320:2560, :] = jnp.zeros((240, 128), F32)

    collect(nn(s_ref[...], src[...]), pl.multiple_of(step * 256, 256), 256)

    @pl.when(step == 7)
    def _():
        pltpu.make_async_copy(far_hbm, far_ref, sems.at[1]).wait()
        total = jnp.zeros((TARGETS, COEF), F32)
        for o in range(16):
            total = total + apply_operator(
                joined(grouped, pl.ds(o, TARGETS, stride=16)), far_ref[o]
            )
        wide[...] = jnp.zeros_like(wide)
        wide[:, :COEF] = total
        for h in range(3):
            locals_rows[h] = wide[0:128, 128 * h : 128 * h + 128]
        pltpu.make_async_copy(down_hbm, down_ref, sems.at[0]).wait()
        first = lax.rem(2 * dev_ref[0], 8)
        coarse = wide[144:145, :COEF]
        grand = jnp.concatenate(
            [apply_operator(coarse, down_ref[first]), apply_operator(coarse, down_ref[first + 1])],
            axis=0,
        )
        for c in range(8):
            rows = apply_operator(grand, down_ref[c])
            wide[128 + c : 129 + c, :COEF] = wide[128 + c : 129 + c, :COEF] + rows[0:1]
            wide[136 + c : 137 + c, :COEF] = wide[136 + c : 137 + c, :COEF] + rows[1:2]
        parents = wide[128:144, :COEF]
        for c in range(8):
            wide[0:16, :COEF] = apply_operator(parents, down_ref[c])
            for h in range(3):
                rows = pl.ds(c, 16, stride=8)
                locals_rows[h, rows, :] = (
                    locals_rows[h, rows, :] + wide[0:16, 128 * h : 128 * h + 128]
                )
        for h in range(3):
            loc[128 * h : 128 * h + 128, :] = locals_rows[h].T
        x_all, y_all, z_all = [2.0 * pos_ref[d].T for d in range(3)]
        for part in range(2):
            piece = slice(64 * part, 64 * part + 64)
            x, y, z = x_all[piece], y_all[piece], z_all[piece]
            over_i = None
            for i in range(ORDER, -1, -1):
                over_j = None
                for j in range(ORDER - i, -1, -1):
                    over_k = None
                    for k in range(ORDER - i - j, -1, -1):
                        a = INDEX[(i, j, k)]
                        value = loc[a : a + 1, :]
                        over_k = value if over_k is None else over_k * z + value
                    over_j = over_k if over_j is None else over_j * y + over_k
                over_i = over_j if over_i is None else over_i * x + over_j
            result[piece, :] = over_i
        out_ref[...] = near_ref[...] + result[...].T


def cost(flops, moved):
    return pl.CostEstimate(flops=flops, bytes_accessed=moved, transcendentals=0)


def shape(*dims, dtype=F32):
    return jax.ShapeDtypeStruct(dims, dtype)


def limits(mib):
    return pltpu.CompilerParams(vmem_limit_bytes=mib * 1024 * 1024)


def upward_call(dev, pos, chg, up_shift):
    return pl.pallas_call(
        upward_kernel,
        out_shape=(shape(3, 128, 128), shape(3, 16, 128), shape(3, 128)),
        in_specs=[SMEM, VMEM, VMEM, VMEM],
        out_specs=(VMEM, VMEM, VMEM),
        scratch_shapes=[pltpu.VMEM((384, 128), F32), pltpu.VMEM((16, 384), F32)],
        compiler_params=limits(40),
        cost_estimate=cost(10**9, 3 * 10**6),
        name="upward",
    )(dev, pos, chg, up_shift)


def pack_call(asked, lt, pt, lift):
    return pl.pallas_call(
        pack_kernel,
        out_shape=shape(128, ROWS, 128),
        in_specs=[VMEM] * 4,
        out_specs=VMEM,
        compiler_params=limits(40),
        cost_estimate=cost(10**9, 4 * 10**6),
        name="pack",
    )(asked, lt, pt, lift)


def near_call(code, count, selves, own, before, after):
    return pl.pallas_call(
        near_kernel,
        out_shape=shape(128, 128),
        in_specs=[SMEM, SMEM, SMEM, VMEM, VMEM, VMEM],
        out_specs=VMEM,
        scratch_shapes=[
            pltpu.VMEM((LEAF + 2 * RIM, 8, 128), F32),
            pltpu.VMEM((27, 8, 128), F32),
            pltpu.VMEM((LEAF + 2 * RIM, 128, 128), BF16),
            pltpu.VMEM((LEAF + 2 * RIM, 128, 128), F32),
            pltpu.VMEM((LEAF, 8, 128), F32),
            pltpu.VMEM((GROUP, 128, 128), F32),
            pltpu.VMEM((GROUP, 128, 128), F32),
            pltpu.SMEM((3 * GROUP,), jnp.int32),
            pltpu.SMEM((3 * GROUP,), jnp.int32),
        ],
        compiler_params=limits(40),
        cost_estimate=cost(30 * 10**9, 10**6),
        name="near",
    )(code, count, selves, own, before, after)


def counts_call(far_leaves, far_leaf_class, far_parents, far_parent_class):
    width = far_leaves.shape[1]
    blocks = lambda i: (i, 0)
    whole = lambda i: (0, 0)
    return pl.pallas_call(
        counts_kernel,
        grid=(8,),
        out_shape=(shape(2048, 2176, dtype=BF16), shape(256, 640, dtype=BF16)),
        in_specs=[
            pl.BlockSpec((16, width), blocks),
            pl.BlockSpec((16, width), blocks),
            pl.BlockSpec((16, width), whole),
            pl.BlockSpec((16, width), whole),
        ],
        out_specs=(pl.BlockSpec((256, 2176), blocks), pl.BlockSpec((256, 640), whole)),
        scratch_shapes=[pltpu.VMEM((16, 256), jnp.int32), pltpu.VMEM((16, 256), jnp.int32)],
        compiler_params=limits(40),
        cost_estimate=cost(10 * 10**9, 9 * 10**6),
        name="counts",
    )(far_leaves, far_leaf_class, far_parents, far_parent_class)


def far_call(dev, lists, classes, s, sp, lt, pt, arrived, pos, near, down_shift, far_shift):
    def whole(*dims):
        return pl.BlockSpec(dims, lambda i: (0,) * len(dims))

    hbm = pl.BlockSpec(memory_space=pl.ANY)
    return pl.pallas_call(
        far_kernel,
        grid=(8,),
        out_shape=shape(128, 128),
        in_specs=[
            SMEM, SMEM, SMEM,
            pl.BlockSpec((256, 2176), lambda i: (i, 0)),
            whole(256, 640), whole(3, 128, 128), whole(3, 16, 128), whole(128, ROWS, 128),
            whole(3, 128, 128), whole(128, 128), hbm, hbm,
        ],
        out_specs=whole(128, 128),
        scratch_shapes=[
            pltpu.VMEM((2176, 640), BF16),
            pltpu.VMEM((640, 640), BF16),
            pltpu.VMEM((3, 16 * TARGETS, 128), F32),
            pltpu.VMEM((3, 128, 128), F32),
            pltpu.VMEM((TARGETS, 384), F32),
            pltpu.VMEM((384, 128), F32),
            pltpu.VMEM((128, 128), F32),
            pltpu.VMEM((8, COEF, COEF), F32),
            pltpu.VMEM((16, COEF, COEF), F32),
            pltpu.SemaphoreType.DMA((2,)),
        ],
        compiler_params=limits(48),
        cost_estimate=cost(10 * 10**9, 20 * 10**6),
        name="far",
    )(dev, lists, classes, s, sp, lt, pt, arrived, pos, near, down_shift, far_shift)


def near_lists(near_leaves, near_offsets, first_leaf):
    leaves = near_leaves.shape[0]
    present = near_leaves >= 0
    own = first_leaf + jnp.arange(leaves, dtype=jnp.int32)[:, None]
    itself = (near_leaves == own) & (near_offsets == 13)
    code = (near_leaves - first_leaf + RIM) * 32 + near_offsets
    code = jnp.where(present & jnp.logical_not(itself), code, -1)
    code = jnp.concatenate([code.reshape(-1), jnp.full((32,), -1, jnp.int32)])
    count = jnp.maximum(jnp.sum(present.astype(jnp.int32), axis=1), 2)
    selves = jnp.sum(itself.astype(jnp.int32), axis=1)
    extra = jnp.stack([jnp.int32(1 << 30), jnp.sum(count - 1)])
    return code, jnp.concatenate([count, extra]), selves


def per_device(
    positions,
    charges,
    near_leaves,
    near_offsets,
    far_leaves,
    far_leaf_class,
    leaf_plan,
    far_parents,
    far_parent_class,
    parent_plan,
    coarse_lists,
    coarse_class,
    up_shift,
    down_shift,
    far_shift,
):
    device = lax.axis_index(AXES)
    dev = device.reshape(1).astype(jnp.int32)
    plans = jnp.concatenate([leaf_plan[0], parent_plan[0]], 1)
    asked = lax.all_to_all(plans, AXES, split_axis=0, concat_axis=0, tiled=True)
    pos = positions.reshape(3, LEAF, 128)
    chg = charges.reshape(LEAF, 128)
    own = jnp.concatenate([pos, chg[None]], 0)
    size = lax.axis_size(AXES)
    up = [(i, i + 1) for i in range(size - 1)]
    down = [(j, i) for i, j in up]
    before = lax.ppermute(own[:, LEAF - RIM :], AXES, up)
    after = lax.ppermute(own[:, :RIM], AXES, down)
    lt, pt, lift = upward_call(dev, pos, chg, up_shift)
    outgoing = pack_call(asked, lt, pt, lift)
    arrived = lax.all_to_all(outgoing, AXES, split_axis=0, concat_axis=0, tiled=True)
    code, count, selves = near_lists(near_leaves, near_offsets, device * LEAF)
    near = near_call(code, count, selves, own, before, after)
    s, sp = counts_call(far_leaves, far_leaf_class, far_parents, far_parent_class)
    potential = far_call(
        dev, coarse_lists.reshape(-1), coarse_class.reshape(-1), s, sp, lt, pt, arrived, pos, near,
        down_shift, far_shift,
    )
    return potential.reshape(-1)


def solution(mesh):
    row = P(AXES, None)
    placed = (
        P(None, AXES), P(AXES), row, row, row, row, P(AXES, None, None), row, row,
        P(AXES, None, None), P(), P(), P(), P(), P(),
    )
    return jax.shard_map(
        per_device, mesh=mesh, in_specs=placed, out_specs=P(AXES), check_vma=False
    )
```

time: 1330 us -> 204 us (0.15); the launches traced: 1310 us -> 205 us
  local copies, waits for them, and re-layouts: 562 us -> 32.3 us
  other arithmetic: 507 us -> 6.45 us
  matrix products: 151 us -> 0 us
  Pallas kernels: 0 us -> 139 us
  blocking collectives: 67.6 us -> 0 us
    gather x47 -> x0, local copies, waits for them, and re-layouts: 430 us -> none  [the longest x11 186 us: one_block(): columns = sources[:, jnp.maximum(slot_block, 0)]]
    reduce_sum x28 -> x1, other arithmetic: 340 us -> 1.34 us  [near_lists(): selves = jnp.sum(itself.astype(jnp.int32), axis=1)]
    dot_general x16 -> x0, matrix products: 151 us -> none  [the longest x4 59.4 us: one_block(): grouped = jnp.einsum('ctk,tko->otc', columns, selector, precision=highest)]
    pallas_call x0 -> x5, Pallas kernels: none -> 139 us  [the longest x1 67.2 us: near_call(): pl.pallas_call(near_kernel, out_shape=shape(128, 128), in_specs=[SMEM, SM...]
    psum x1 -> x0, blocking collectives: 67.6 us -> none  [per_device(): lax.psum(jnp.dot(lifted, member, precision=highest), ('gx', 'gy'))]
    slice x29 -> x0, local copies, waits for them, and re-layouts: 51.8 us -> none  [the longest x27 47.3 us: add_slot(): gathered[3][:, None, :] * lax.rsqrt(squared)]
    add x82 -> x1, other arithmetic: 46.6 us -> 0.01 us  [near_lists(): own = first_leaf + jnp.arange(leaves, dtype=jnp.int32)[:, None]]
    sub x27 -> x0, local copies, waits for them, and re-layouts: 24.7 us -> none  [add_slot(): gathered[0][:, None, :] + shift_x[:, None, None] - targets[0][:, :, None]]
  transfers between devices with their start and end apart: 4 -> 4, of which waited for: 0 -> 0; matrix products, arithmetic and copies ran while one was open for 69% -> 12% of each run, Pallas kernels for 0% -> 42%
where the time goes in v1:
time: 204 us; the launch traced here: 205 us
  Pallas kernels  139 us (68%)
  local copies, waits for them, and re-layouts  32.3 us (16%)
  starting transfers between devices  27.3 us (13%)
  other arithmetic  6.45 us (3%)
    pallas_call x1, Pallas kernels, near_call(): pl.pallas_call(near_kernel, out_shape=shape(128, 128), in_specs=[SMEM, SM...  67.2 us
    pallas_call x1, Pallas kernels, far_call(): pl.pallas_call(far_kernel, grid=(8,), out_shape=shape(128, 128), in_specs...  52.8 us
    unnamed x50, local copies, waits for them, and re-layouts  30.4 us
    all_to_all x1, starting transfers between devices, per_device(): asked = lax.all_to_all(plans, AXES, split_axis=0, concat_axis=0, tiled=True)  11 us
    all_to_all x1, starting transfers between devices, per_device(): lax.all_to_all(outgoing, AXES, split_axis=0, concat_axis=0, tiled=True)  9.75 us
    pallas_call x1, Pallas kernels, upward_call(): pl.pallas_call(upward_kernel, out_shape=(shape(3, 128, 128), shape(3, 16,...  8 us
    pallas_call x1, Pallas kernels, counts_call(): pl.pallas_call(counts_kernel, grid=(8,), out_shape=(shape(2048, 2176, dty...  7.24 us
    ppermute x1, starting transfers between devices, per_device(): before = lax.ppermute(own[:, LEAF - RIM:], AXES, up)  4.58 us
  transfers between devices with their start and end apart: 4, of which 0 were waited for; matrix products, arithmetic and copies ran while one was open for 12% of the time, Pallas kernels for 42%

profile of v1, /device:TPU:1, one launch (start us, length us, event | category | flops | bytes accessed | tf_op | source)
XLA Modules:
  0.0 205.1 jit_solution(15803875767717272059)
XLA Ops:
  0.0 1.0 copy.44
  1.0 0.0 copy-start
  1.0 1.5 fusion.1
  2.4 4.6 %collective-permute-start = (f32[4,32,128]{2,1,0:T(8,128)}, f32[4,32,128]{2,1,0:T(8,128)}, u32[]{:S(2)}, u32[]{:S(2)}) collective-permute-start(f32[4,32,128]{2,1,0:T(8,128)} %get-tuple-element.18), channel_id=1, source_target_pairs={{0,1},{1,2},{2,3},{3,4},{4,5},{5,6},{6,7},{7,8},{8,9},{9,10},{10,1... | collective-permute-start | bytes 196616 | tf_op jit(solution)/shard_map/ppermute | solution.py:531
  7.0 1.9 collective-permute-start.1
  9.0 0.7 pad_add_fusion
  9.7 0.7 copy.38
  10.4 11.0 %all-to-all-start = ((s32[128,1,20]{2,1,0:T(1,128)}), s32[128,1,20]{2,1,0:T(1,128)}, u32[]{:S(2)}, u32[]{:S(2)}) async-start(s32[128,1,20]{2,1,0:T(1,128)} %bitcast.4), calls=%async_computation | async-start | bytes 131072 | tf_op jit(solution)/shard_map/all_to_all | solution.py:524
  21.4 1.6 pad_maximum_fusion.own_ref
  23.0 0.0 copy-done
  23.0 2.7 %copy.37.up_ref = f32[8,286,286]{2,1,0:T(8,128)S(1)} copy(f32[8,286,286]{2,0,1:T(8,128)} %param.27) | data formatting | bytes 5234944 | tf_op args[12]
  25.7 1.6 copy.35.leaf_ref
  27.3 1.6 copy.36.leaf_class_ref
  29.0 1.3 convert_reduce_fusion
  30.3 0.0 copy-start.6
  30.3 0.9 copy-done.6
  31.2 0.0 copy-start.7
  31.2 0.9 copy-done.7
  32.1 0.0 copy-start.13
  32.1 0.7 copy-done.13
  32.9 0.0 copy-start.14
  32.9 0.7 copy-done.14
  33.6 7.2 %counts.1 = (bf16[2048,2176]{1,0:T(8,128)(2,1)S(1)}, bf16[256,640]{1,0:T(8,128)(2,1)S(1)}) custom-call(s32[128,189]{1,0:T(8,128)S(1)} %copy-done.6, s32[128,189]{1,0:T(8,128)S(1)} %copy-done.7, s32[16,189]{1,0:T(8,128)S(1)} %copy-done.13, s32[16,189]{1,0:T(8,128)S(1)} %copy-done.14), custom_call_target="tpu_custom_call" | custom-call | flops 10000000000 | bytes 9000000 | tf_op jit(solution)/shard_map/counts/pallas_call | solution.py:438
  40.8 0.0 copy-start.15
  40.8 3.5 %copy-done.15 = bf16[2048,2176]{1,0:T(8,128)(2,1)} copy-done((bf16[2048,2176]{1,0:T(8,128)(2,1)}, bf16[2048,2176]{1,0:T(8,128)(2,1)S(1)}, u32[]{:S(2)}) %copy-start.15) | copy-done | bytes 8912920
  44.3 0.0 copy-done.1
  44.3 0.0 copy-done.4
  44.3 8.0 %upward.1 = (f32[3,128,128]{2,1,0:T(8,128)S(1)}, f32[3,16,128]{2,1,0:T(8,128)S(1)}, f32[3,128]{1,0:T(4,128)S(1)}) custom-call(s32[1]{0:T(128)} %bitcast.dev_ref, f32[3,128,128]{2,1,0:T(8,128)S(1)} %bitcast.15, f32[128,128]{1,0:T(8,128)S(1)} %bitcast.19, f32[8,286,286]{2,1,0:T(8,128)S(1)} %copy.37.up_ref), custom_call_target="tpu_custom_call" | custom-call | flops 1000000000 | bytes 3000000 | tf_op jit(solution)/shard_map/upward/pallas_call | solution.py:387
  52.3 0.0 copy-done.16
  52.3 0.0 copy-start.8
  52.3 0.7 copy-done.8
  53.0 0.6 copy-done.11
  53.6 0.8 copy.39
  54.4 0.2 reshape.33
  54.6 0.0 copy-start.18
  54.7 8.3 %copy.41.far_hbm = f32[16,286,286]{2,1,0:T(8,128)} copy(f32[16,286,286]{2,0,1:T(8,128)} %param.29) | data formatting | bytes 10469888 | tf_op args[14]
  62.9 0.0 copy-done.18
  62.9 0.0 copy-start.12
  62.9 2.4 %copy.40.down_hbm = f32[8,286,286]{2,1,0:T(8,128)} copy(f32[8,286,286]{2,0,1:T(8,128)S(1)} %copy-done.18) | data formatting | bytes 5234944 | tf_op args[13]
  65.4 0.0 copy-done.19
  65.4 0.1 copy.33
  65.5 0.1 reshape.29.lists_ref
  65.6 0.0 copy-done.20
  65.6 0.1 copy.34
  65.7 0.1 reshape.30.class_ref
  65.8 0.0 all-to-all-done
  65.8 0.0 copy-done.9
  65.8 0.0 copy-done.12
  65.8 3.3 %pack.1 = f32[128,48,128]{2,1,0:T(8,128)S(1)} custom-call(s32[128,20]{1,0:T(8,128)} %bitcast.5.asked_ref, f32[3,128,128]{2,1,0:T(8,128)S(1)} %copy-done.9, f32[3,16,128]{2,1,0:T(8,128)S(1)} %copy-done.12, f32[3,128]{1,0:T(4,128)S(1)} %get-tuple-element.14.lift_ref), custom_call_target="tpu_custom_call" | custom-call | flops 1000000000 | bytes 4000000 | tf_op jit(solution)/shard_map/pack/pallas_call | solution.py:400
  69.2 0.0 copy-start.3
  69.2 1.7 copy-done.3
  70.9 9.8 %all-to-all-start.1 = ((f32[128,48,128]{2,1,0:T(8,128)}), f32[128,48,128]{2,1,0:T(8,128)S(1)}, u32[]{:S(2)}, u32[]{:S(2)}) async-start(f32[128,48,128]{2,1,0:T(8,128)} %copy-done.3), calls=%async_computation.1 | async-start | bytes 6291456 | tf_op jit(solution)/shard_map/all_to_all | solution.py:535
  80.6 0.6 broadcast_maximum_fusion
  81.3 0.7 pad_add_fusion.1.count_ref
  82.0 0.0 collective-permute-done.before_ref
  82.0 0.0 collective-permute-done.1.after_ref
  82.0 0.9 copy-done.5
  82.9 67.2 %near.1.near_ref = f32[128,128]{1,0:T(8,128)S(1)} custom-call(s32[3488]{0:T(1024)S(1)} %concatenate.13.code_ref, s32[130]{0:T(256)S(1)} %pad_add_fusion.1.count_ref, s32[128]{0:T(128)S(1)} %get-tuple-element.15.self_ref, f32[4,128,128]{2,1,0:T(8,128)S(1)} %copy-done.5, f32[4,32,128]{2,1,0:T(8,128)} %collective-permute-done.before_ref, ...), custom_call_target="tpu_custom_call" | custom-call | flops 30000001024 | bytes 1000000 | tf_op jit(solution)/shard_map/near/pallas_call | solution.py:412
  150.2 0.0 all-to-all-done.1.arrived_ref
  150.2 0.0 copy-done.2
  150.2 0.0 copy-start.10
  150.2 0.9 copy-done.10
  151.1 1.0 copy-done.17
  152.1 52.8 %far.1 = f32[128,128]{1,0:T(8,128)} custom-call(s32[1]{0:T(128)} %bitcast.dev_ref, s32[224]{0:T(256)S(1)} %reshape.29.lists_ref, s32[224]{0:T(256)S(1)} %reshape.30.class_ref, bf16[2048,2176]{1,0:T(8,128)(2,1)} %copy-done.15, bf16[256,640]{1,0:T(8,128)(2,1)S(1)} %copy-done.17, f32[3,128,128]{2,1,0:T(8,128)S(1)} %copy-done.10, f32[3,16,128]{2,1,0:T(8,128)S(1)} %copy-done.12, ...), custom_call_target="tpu_custom_call" | custom-call | flops 10000000000 | bytes 20000000 | tf_op jit(solution)/shard_map/far/pallas_call | solution.py:461
  (12 shorter events, 0.0 us)
Async XLA Ops:
  1.0 22.0 %copy-start = (f32[1,3,128,128]{3,2,1,0:T(8,128)}, f32[1,3,128,128]{3,2,1,0:T(8,128)S(1)}, u32[]{:S(2)}) copy-start(f32[1,3,128,128]{3,2,1,0:T(8,128)S(1)} %copy.44) | copy-start | bytes 589828
  2.4 79.5 %collective-permute-start = (f32[4,32,128]{2,1,0:T(8,128)}, f32[4,32,128]{2,1,0:T(8,128)}, u32[]{:S(2)}, u32[]{:S(2)}) collective-permute-start(f32[4,32,128]{2,1,0:T(8,128)} %get-tuple-element.18), channel_id=1, source_target_pairs={{0,1},{1,2},{2,3},{3,4},{4,5},{5,6},{6,7},{7,8},{8,9},{9,10},{10,1... | collective-permute-start | bytes 196616 | tf_op jit(solution)/shard_map/ppermute | solution.py:531
  7.0 75.0 %collective-permute-start.1 = (f32[4,32,128]{2,1,0:T(8,128)}, f32[4,32,128]{2,1,0:T(8,128)}, u32[]{:S(2)}, u32[]{:S(2)}) collective-permute-start(f32[4,32,128]{2,1,0:T(8,128)} %get-tuple-element.17), channel_id=1, source_target_pairs={{1,0},{2,1},{3,2},{4,3},{5,4},{6,5},{7,6},{8,7},{9,8},{10,9},{11,1... | collective-permute-start | bytes 196616 | tf_op jit(solution)/shard_map/ppermute | solution.py:532
  10.4 55.4 %all-to-all-start = ((s32[128,1,20]{2,1,0:T(1,128)}), s32[128,1,20]{2,1,0:T(1,128)}, u32[]{:S(2)}, u32[]{:S(2)}) async-start(s32[128,1,20]{2,1,0:T(1,128)} %bitcast.4), calls=%async_computation | async-start | bytes 131072 | tf_op jit(solution)/shard_map/all_to_all | solution.py:524
  30.3 0.9 copy-start.6
  31.2 0.9 copy-start.7
  32.1 0.7 copy-start.13
  32.9 0.7 copy-start.14
  33.6 10.7 %copy-start.1 = (f32[1,3,128,128]{3,2,1,0:T(8,128)S(1)}, f32[1,3,128,128]{3,2,1,0:T(8,128)}, u32[]{:S(2)}) copy-start(f32[1,3,128,128]{3,2,1,0:T(8,128)} %copy-done) | copy-start | bytes 589828
  33.6 10.7 %copy-start.4 = (f32[16384]{0:T(1024)S(1)}, f32[16384]{0:T(1024)}, u32[]{:S(2)}) copy-start(f32[16384]{0:T(1024)} %param.16) | copy-start | bytes 196612
  40.8 3.5 %copy-start.15 = (bf16[2048,2176]{1,0:T(8,128)(2,1)}, bf16[2048,2176]{1,0:T(8,128)(2,1)S(1)}, u32[]{:S(2)}) copy-start(bf16[2048,2176]{1,0:T(8,128)(2,1)S(1)} %get-tuple-element.10.s_ref) | copy-start | bytes 26738692
  44.3 8.0 %copy-start.16 = (bf16[256,640]{1,0:T(8,128)(2,1)}, bf16[256,640]{1,0:T(8,128)(2,1)S(1)}, u32[]{:S(2)}) copy-start(bf16[256,640]{1,0:T(8,128)(2,1)S(1)} %get-tuple-element.11.sp_ref) | copy-start | bytes 983044
  52.3 0.7 copy-start.8
  53.0 0.6 copy-start.11
  54.6 8.3 %copy-start.18 = (f32[8,286,286]{2,0,1:T(8,128)S(1)}, f32[8,286,286]{2,0,1:T(8,128)}, u32[]{:S(2)}) copy-start(f32[8,286,286]{2,0,1:T(8,128)} %param.28) | copy-start | bytes 7852420
  62.9 2.4 %copy-start.19 = (s32[32,7]{0,1:T(8,128)S(1)}, s32[32,7]{0,1:T(8,128)}, u32[]{:S(2)}) copy-start(s32[32,7]{0,1:T(8,128)} %param.25) | copy-start | bytes 2692
  62.9 2.6 %copy-start.20 = (s32[32,7]{0,1:T(8,128)S(1)}, s32[32,7]{0,1:T(8,128)}, u32[]{:S(2)}) copy-start(s32[32,7]{0,1:T(8,128)} %param.26) | copy-start | bytes 2692
  62.9 2.9 %copy-start.9 = (f32[3,128,128]{2,1,0:T(8,128)S(1)}, f32[3,128,128]{2,1,0:T(8,128)}, u32[]{:S(2)}) copy-start(f32[3,128,128]{2,1,0:T(8,128)} %copy-done.8) | copy-start | bytes 589828
  62.9 2.9 %copy-start.12 = (f32[3,16,128]{2,1,0:T(8,128)S(1)}, f32[3,16,128]{2,1,0:T(8,128)}, u32[]{:S(2)}) copy-start(f32[3,16,128]{2,1,0:T(8,128)} %copy-done.11) | copy-start | bytes 73732
  69.2 1.7 copy-start.3
  70.9 79.3 %all-to-all-start.1 = ((f32[128,48,128]{2,1,0:T(8,128)}), f32[128,48,128]{2,1,0:T(8,128)S(1)}, u32[]{:S(2)}, u32[]{:S(2)}) async-start(f32[128,48,128]{2,1,0:T(8,128)} %copy-done.3), calls=%async_computation.1 | async-start | bytes 6291456 | tf_op jit(solution)/shard_map/all_to_all | solution.py:535
  82.0 1.0 copy-start.5
  82.9 67.2 %copy-start.2 = (f32[1,3,128,128]{3,2,1,0:T(8,128)S(1)}, f32[1,3,128,128]{3,2,1,0:T(8,128)}, u32[]{:S(2)}) copy-start(f32[1,3,128,128]{3,2,1,0:T(8,128)} %copy-done) | copy-start | bytes 589828
  150.2 0.9 copy-start.10
  151.1 1.0 copy-start.17

commit v2 on v1

v2 whole, which is shorter than its diff:
```python
import jax
import jax.numpy as jnp
import numpy as np
from jax import lax
from jax.experimental import pallas as pl
from jax.experimental.pallas import tpu as pltpu
from jax.sharding import PartitionSpec as P

ORDER = 10
COEF = 286
RIM = 32
LEAF = 128
K_NEAR = 27
CAP_L = 16
CAP_P = 4
ROWS = 48
TARGETS = 160
GROUP = 64
NOBODY = LEAF + 2 * RIM
SOFT = 0.05 * 0.05
AXES = ("gx", "gy")
F32 = jnp.float32
BF16 = jnp.bfloat16
VMEM = pl.BlockSpec(memory_space=pltpu.VMEM)
SMEM = pl.BlockSpec(memory_space=pltpu.SMEM)


def exponents(order):
    entries = []
    for degree in range(order + 1):
        for first_power in range(degree, -1, -1):
            for second_power in range(degree - first_power, -1, -1):
                entries.append((first_power, second_power, degree - first_power - second_power))
    return entries


INDEX = {powers: number for number, powers in enumerate(exponents(ORDER))}


def split(x):
    high = x.astype(BF16)
    return high, (x - high.astype(F32)).astype(BF16)


def nt(a, b):
    return lax.dot_general(a, b, (((1,), (1,)), ((), ())), preferred_element_type=F32)


def nn(a, b):
    return jnp.dot(a, b, preferred_element_type=F32)


def apply_operator(rows, operator):
    row_high, row_low = split(rows)
    high, low = split(operator)
    return nt(row_high, high) + (nt(row_low, high) + nt(row_high, low))


def fetches(source, chunks, tail, sems, first):
    return [
        pltpu.make_async_copy(source.at[:, 0:128], chunks.at[0], sems.at[first]),
        pltpu.make_async_copy(source.at[:, 128:256], chunks.at[1], sems.at[first + 1]),
        pltpu.make_async_copy(source.at[:, 256:COEF], tail, sems.at[first + 2]),
    ]


def arrive(copies, chunks, tail):
    for copy in copies:
        copy.wait()
    chunks[2, :, 0 : COEF - 256] = tail[...]


def operator_at(chunks, number, count):
    rows = pl.ds(number, COEF, stride=count)
    return jnp.concatenate([chunks[h, rows, :] for h in range(3)], axis=1)[:, :COEF]


def joined(ref, rows):
    return jnp.concatenate([ref[h, rows, :] for h in range(3)], axis=1)[:, :COEF]


def upward_kernel(dev_ref, pos_ref, chg_ref, up_hbm, lt_ref, pt_ref, lift_ref, moments, wide, up_ref,
                  up_tail, sems):
    copies = fetches(up_hbm, up_ref, up_tail, sems, 0)
    for copy in copies:
        copy.start()
    x, y, z = [2.0 * pos_ref[d].T for d in range(3)]
    with_x = chg_ref[...].T
    z_powers = [None, z]
    for k in range(ORDER - 1):
        z_powers.append(z_powers[-1] * z)
    moments[COEF - 6 : 384, :] = jnp.zeros((384 - COEF + 6, LEAF), F32)
    for i in range(ORDER + 1):
        if i:
            with_x = with_x * x
        with_xy = with_x
        for j in range(ORDER + 1 - i):
            if j:
                with_xy = with_xy * y
            for k in range(ORDER + 1 - i - j):
                term = with_xy * z_powers[k] if k else with_xy
                a = INDEX[(i, j, k)]
                moments[a : a + 1, :] = jnp.sum(term, axis=0, keepdims=True)
    for h in range(3):
        lt_ref[h] = moments[128 * h : 128 * h + 128, :].T
    wide[...] = jnp.zeros_like(wide)
    arrive(copies, up_ref, up_tail)
    total = jnp.zeros((16, COEF), F32)
    for c in range(8):
        total = total + apply_operator(joined(lt_ref, pl.ds(c, 16, stride=8)), operator_at(up_ref, c, 8))
    wide[:, :COEF] = total
    for h in range(3):
        pt_ref[h] = wide[:, 128 * h : 128 * h + 128]
    grand = jnp.zeros((2, COEF), F32)
    for c in range(8):
        rows = jnp.concatenate([wide[c : c + 1, :COEF], wide[8 + c : 9 + c, :COEF]], axis=0)
        grand = grand + apply_operator(rows, operator_at(up_ref, c, 8))
    first = lax.rem(2 * dev_ref[0], 8)
    lifted = apply_operator(grand[0:1], operator_at(up_ref, first, 8)) + apply_operator(grand[1:2], operator_at(up_ref, first + 1, 8))
    wide[0:1, :COEF] = lifted
    for h in range(3):
        lift_ref[h : h + 1, :] = wide[0:1, 128 * h : 128 * h + 128]


def pack_kernel(asked_ref, lt_ref, pt_ref, lift_ref, out_ref):
    lane = lax.broadcasted_iota(jnp.int32, (128, 128), 1)
    leaf_rows = jnp.concatenate([lt_ref[h] for h in range(3)], axis=1)
    parent_rows = jnp.concatenate([pt_ref[h] for h in range(3)], axis=1)
    parent_rows = jnp.concatenate([parent_rows, jnp.zeros((112, 384), F32)], axis=0)
    leaf_rows = jnp.concatenate(split(leaf_rows), axis=0)
    parent_rows = jnp.concatenate(split(parent_rows), axis=0)
    for q in range(5):
        tail = jnp.zeros((128, 128), F32)
        for p in range(4):
            j = 4 * q + p
            chosen = jnp.where(asked_ref[:, j : j + 1] == lane, 1.0, 0.0).astype(BF16)
            chosen = jnp.concatenate([chosen, chosen], axis=1)
            rows = nn(chosen, leaf_rows if q < 4 else parent_rows)
            out_ref[pl.ds(2 * j, 128, stride=ROWS), :] = rows[:, 0:128]
            out_ref[pl.ds(2 * j + 1, 128, stride=ROWS), :] = rows[:, 128:256]
            part = rows[:, 256:384]
            tail = tail + (pltpu.roll(part, 32 * p, 1) if p else part)
        out_ref[pl.ds(40 + q, 128, stride=ROWS), :] = tail
    for h in range(3):
        out_ref[pl.ds(45 + h, 128, stride=ROWS), :] = jnp.broadcast_to(lift_ref[h : h + 1, :], (128, 128))


def near_kernel(dev_ref, leaves_ref, offsets_ref, pos_ref, chg_ref, before_ref, after_ref, out_ref,
                eight, charge, offsets, features, spread, sums, ready, lists, plan, sem):
    sub = lax.broadcasted_iota(jnp.int32, (8, 128), 0)
    named = leaves_ref[...]
    first_leaf = dev_ref[0] * LEAF
    present = named >= 0
    own_id = first_leaf + lax.broadcasted_iota(jnp.int32, (K_NEAR, LEAF), 1)
    itself = (named == own_id) & (offsets_ref[...] == 13)
    counted = present & jnp.logical_not(itself)
    code = jnp.where(counted, (named - first_leaf + RIM) * 32 + offsets_ref[...], NOBODY * 32 + 13)
    count = jnp.sum(jnp.where(present, 1.0, 0.0), axis=0, keepdims=True).astype(jnp.int32)
    quads = jnp.maximum((count + 2) // 4, 1)
    selves = jnp.sum(jnp.where(itself, 1.0, 0.0), axis=0, keepdims=True).astype(jnp.int32)
    total = jnp.sum(quads.astype(F32), axis=1, keepdims=True).astype(jnp.int32)
    lists[...] = jnp.full_like(lists, NOBODY * 32 + 13)
    lists[0:K_NEAR, :] = code
    lists[37:38, :] = quads
    lists[38:39, :] = selves
    lists[39:40, :] = jnp.broadcast_to(total, (1, 128))
    copy = pltpu.make_async_copy(lists, plan, sem)
    copy.start()
    eight[:, 3, :] = jnp.full((LEAF + 2 * RIM, 128), 1.0, F32)
    eight[:, 7, :] = jnp.full((LEAF + 2 * RIM, 128), SOFT, F32)
    eight3 = ((0, 4), (1, 5), (2, 6))
    for d in range(3):
        for row in eight3[d]:
            eight[0:RIM, row, :] = before_ref[d]
            eight[RIM : RIM + LEAF, row, :] = pos_ref[d]
            eight[RIM + LEAF : 2 * RIM + LEAF, row, :] = after_ref[d]
    charge[0:RIM, :] = before_ref[3]
    charge[RIM : RIM + LEAF, :] = chg_ref[...]
    charge[RIM + LEAF : 2 * RIM + LEAF, :] = after_ref[3]
    lane = lax.broadcasted_iota(jnp.int32, (128, 128), 1)
    features[NOBODY] = jnp.where(lane == 7, 1.0, 0.0).astype(BF16)
    spread[NOBODY] = jnp.zeros((128, 128), F32)
    for o in range(27):
        shift = (o // 9 - 1, o // 3 % 3 - 1, o % 3 - 1)
        table = jnp.zeros((8, 128), F32)
        for d in range(3):
            table = jnp.where((sub == d) | (sub == d + 4), -float(shift[d]), table)
        offsets[o] = table
    squares = (sub >= 4) & (sub < 7)

    def thirds(v):
        high = v.astype(BF16).astype(F32)
        rest = v - high
        middle = rest.astype(BF16).astype(F32)
        return high, middle, rest - middle

    def target(leaf, offset):
        v = eight[RIM + leaf] + offsets[offset]
        v = jnp.where(squares, v * v, v)
        high, middle, low = thirds(v)
        return jnp.concatenate([high, high, high, middle, middle, low], axis=0).astype(BF16)

    def separations(leaf, rows):
        padded = jnp.concatenate([rows, jnp.zeros((80, 128), BF16)], axis=0)
        return nn(features[leaf], padded)

    row = lax.broadcasted_iota(jnp.int32, (128, 128), 0)
    three = jnp.where((row >= 48) & (row < 51), 1.0, 0.0).astype(BF16)
    diagonal = row == lane
    identity = jnp.where(diagonal, 1.0, 0.0).astype(BF16)

    def source(leaf):
        v = eight[leaf]
        norm = jnp.sum(jnp.where(sub < 3, v * v, 0.0), axis=0, keepdims=True)
        v = jnp.where(sub < 3, -2.0 * v, jnp.where(sub == 3, norm, 1.0))
        high, middle, low = thirds(v)
        first, second, third = thirds(charge[pl.ds(leaf, 1), :])
        parts = jnp.where(sub == 0, first, jnp.where(sub == 1, second, jnp.where(sub == 2, third, 0.0)))
        rows = jnp.concatenate([high, middle, low, high, middle, high, parts], axis=0)
        rows = jnp.concatenate([rows, jnp.zeros((72, 128), F32)], axis=0)
        rows = rows.T.astype(BF16)
        features[leaf] = rows
        spread[leaf] = nn(rows, three)

    def prepare(step, carry):
        for u in range(16):
            source(16 * step + u)
        return carry

    lax.fori_loop(0, (LEAF + 2 * RIM) // 16, prepare, 0)
    copy.wait()

    def own_leaf(step, carry):
        for u in range(16):
            leaf = 16 * step + u
            squared = separations(RIM + leaf, target(leaf, 13))
            terms = jnp.where(diagonal, 0.0, spread[RIM + leaf] * lax.rsqrt(squared))
            sums[leaf] = jnp.sum(terms.reshape(16, 8, 128), axis=0) * plan[38, leaf].astype(F32)
        return carry

    lax.fori_loop(0, LEAF // 16, own_leaf, 0)

    def advance(state):
        leaf, quad = state
        last = quad + 1 >= plan[37, leaf]
        return (
            jnp.where(last, jnp.minimum(leaf + 1, LEAF - 1), leaf),
            jnp.where(last, jnp.where(leaf == LEAF - 1, 7, 0), quad + 1),
        )

    def produce(states):
        for g, (leaf, quad) in enumerate(states):
            for u in range(4):
                code = plan[4 * quad + u + 1, leaf]
                ready[4 * g + u] = target(leaf, code & 31)

    def consume(states):
        for g, (leaf, quad) in enumerate(states):
            part = sums[leaf]
            for u in range(4):
                code = plan[4 * quad + u + 1, leaf]
                squared = separations(code >> 5, ready[4 * g + u])
                terms = spread[code >> 5] * lax.rsqrt(squared)
                part = part + jnp.sum(terms.reshape(16, 8, 128), axis=0)
            sums[leaf] = part

    def following(state, number):
        made = []
        for _ in range(number):
            state = advance(state)
            made.append(state)
        return tuple(made)

    first = (jnp.int32(0), jnp.int32(0))
    states = (first,) + following(first, GROUP // 4 - 1)
    produce(states)

    def one_group(step, states):
        after = following(states[-1], GROUP // 4)
        consume(states)
        produce(after)
        return after

    quads = GROUP // 4
    lax.fori_loop(0, (plan[39, 0] + quads - 1) // quads, one_group, states)
    out_ref[...] = jnp.sum(sums[...], axis=1)


def count_rows(code, low, rows):
    wide = lax.broadcasted_iota(jnp.int32, (rows, 256), 0) == code
    narrow = lax.broadcasted_iota(jnp.int32, (128, 256), 0) == low
    return nt(
        jnp.where(wide, 1.0, 0.0).astype(BF16), jnp.where(narrow, 1.0, 0.0).astype(BF16)
    ).astype(BF16)


def counts_kernel(leaf_ref, leaf_class_ref, parent_ref, parent_class_ref, s_ref, sp_ref,
                  code_scr, low_scr, turned):
    step = pl.program_id(0)

    def encode(slots, classes, cells, capacity):
        ghost = jnp.maximum(slots - cells, 0)
        own = slots < cells
        code = jnp.where(own, 0, 1 + lax.rem(ghost, capacity)) * 16 + classes
        return jnp.where(slots < 0, -1, code), jnp.where(own, slots, lax.div(ghost, capacity))

    def tables(first, capacity, out_ref):
        blocks = capacity + 1
        for t in range(16):
            rows = pl.ds(first + t, 1)
            table = count_rows(code_scr[rows, :], low_scr[rows, :], 16 * blocks)
            for b in range(blocks):
                out_ref[16 * t : 16 * t + 16, 128 * b : 128 * b + 128] = table[16 * b : 16 * b + 16]

    @pl.when(step == 0)
    def _():
        width = leaf_ref.shape[0]
        code_scr[...] = jnp.full_like(code_scr, -1)
        low_scr[...] = jnp.full_like(low_scr, -1)
        for part, scratch in zip(
            encode(leaf_ref[...], leaf_class_ref[...], LEAF, CAP_L), (code_scr, low_scr)
        ):
            turned[...] = jnp.full_like(turned, -1.0)
            turned[:width, :] = part.astype(F32)
            scratch[0:128, 0:128] = turned[0:128, :].T.astype(jnp.int32)
            scratch[0:128, 128:256] = turned[128:256, :].T.astype(jnp.int32)
        for part, scratch in zip(
            encode(parent_ref[...], parent_class_ref[...], 16, CAP_P), (code_scr, low_scr)
        ):
            scratch[128:144, :width] = part
        tables(128, CAP_P, sp_ref)

    tables(pl.multiple_of(16 * step, 16), CAP_L, s_ref)


def far_kernel(dev_ref, lists_ref, class_ref, s_ref, sp_ref, lt_ref, pt_ref, arrived_ref, pos_ref,
               near_ref, down_hbm, far_hbm, out_ref,
               src, src_parent, grouped, locals_rows, wide, loc, result, down_ref, down_tail, far_ref, far_tail, sems):
    step = pl.program_id(0)
    far_copies = fetches(far_hbm, far_ref, far_tail, sems, 0)
    down_copies = fetches(down_hbm, down_ref, down_tail, sems, 3)
    lane = lax.broadcasted_iota(jnp.int32, (128, 128), 1)

    def place(ref, row, parts):
        count = parts[0].shape[0]
        (h0, l0), (h1, l1) = split(parts[0]), split(parts[1])
        tail = parts[2]
        high = tail.astype(BF16).astype(F32)
        low = pltpu.roll(tail - high, 32, 1)
        ref[row : row + count, 0:128] = h0
        ref[row : row + count, 128:256] = h1
        ref[row : row + count, 256:384] = l0
        ref[row : row + count, 384:512] = l1
        ref[row : row + count, 512:640] = (high + low).astype(BF16)

    def collect(product, row, count):
        grouped[0, pl.ds(row, count), :] = product[:, 0:128] + product[:, 256:384]
        grouped[1, pl.ds(row, count), :] = product[:, 128:256] + product[:, 384:512]
        tail = product[:, 512:640]
        grouped[2, pl.ds(row, count), :] = tail + pltpu.roll(tail, 96, 1)

    def arrived_tail(row, p):
        part = arrived_ref[pl.ds(row, 128, stride=ROWS), :]
        part = pltpu.roll(part, 128 - 32 * p, 1) if p else part
        return jnp.where(lane < 32, part, 0.0)

    @pl.when(step == 0)
    def _():
        for copy in far_copies + down_copies:
            copy.start()
        place(src, 0, [lt_ref[h] for h in range(3)])
        for c in range(CAP_L):
            place(
                src,
                128 * (c + 1),
                [arrived_ref[pl.ds(2 * c, 128, stride=ROWS), :], arrived_ref[pl.ds(2 * c + 1, 128, stride=ROWS), :], arrived_tail(40 + c // 4, c % 4)],
            )
        own = [jnp.concatenate([pt_ref[h], jnp.zeros((112, 128), F32)], axis=0) for h in range(3)]
        place(src_parent, 0, own)
        for c in range(CAP_P):
            place(
                src_parent,
                128 * (c + 1),
                [arrived_ref[pl.ds(32 + 2 * c, 128, stride=ROWS), :], arrived_ref[pl.ds(33 + 2 * c, 128, stride=ROWS), :], arrived_tail(44, c)],
            )
        collect(nn(sp_ref[...], src_parent[...]), 2048, 256)
        mine = dev_ref[0] // 4
        operator = lax.broadcasted_iota(jnp.int32, (16, 128), 0)
        cell = lax.broadcasted_iota(jnp.int32, (16, 128), 1) // 4
        chosen = jnp.zeros((16, 128), F32)
        for k in range(7):
            hit = (operator == class_ref[mine * 7 + k]) & (cell == lists_ref[mine * 7 + k])
            chosen = chosen + jnp.where(hit, 1.0, 0.0)
        chosen = chosen.astype(BF16)
        for h in range(3):
            high, low = split(arrived_ref[pl.ds(45 + h, 128, stride=ROWS), :])
            grouped[h, 2304:2320, :] = nn(chosen, high) + nn(chosen, low)
            grouped[h, 2320:2560, :] = jnp.zeros((240, 128), F32)

    collect(nn(s_ref[...], src[...]), pl.multiple_of(step * 256, 256), 256)

    @pl.when(step == 7)
    def _():
        arrive(far_copies, far_ref, far_tail)
        total = jnp.zeros((TARGETS, COEF), F32)
        for o in range(16):
            total = total + apply_operator(
                joined(grouped, pl.ds(o, TARGETS, stride=16)), operator_at(far_ref, o, 16)
            )
        wide[...] = jnp.zeros_like(wide)
        wide[:, :COEF] = total
        for h in range(3):
            locals_rows[h] = wide[0:128, 128 * h : 128 * h + 128]
        arrive(down_copies, down_ref, down_tail)
        first = lax.rem(2 * dev_ref[0], 8)
        coarse = wide[144:145, :COEF]
        grand = jnp.concatenate(
            [apply_operator(coarse, operator_at(down_ref, first, 8)), apply_operator(coarse, operator_at(down_ref, first + 1, 8))],
            axis=0,
        )
        for c in range(8):
            rows = apply_operator(grand, operator_at(down_ref, c, 8))
            wide[128 + c : 129 + c, :COEF] = wide[128 + c : 129 + c, :COEF] + rows[0:1]
            wide[136 + c : 137 + c, :COEF] = wide[136 + c : 137 + c, :COEF] + rows[1:2]
        parents = wide[128:144, :COEF]
        for c in range(8):
            wide[0:16, :COEF] = apply_operator(parents, operator_at(down_ref, c, 8))
            for h in range(3):
                rows = pl.ds(c, 16, stride=8)
                locals_rows[h, rows, :] = (
                    locals_rows[h, rows, :] + wide[0:16, 128 * h : 128 * h + 128]
                )
        for h in range(3):
            loc[128 * h : 128 * h + 128, :] = locals_rows[h].T
        x_all, y_all, z_all = [2.0 * pos_ref[d].T for d in range(3)]
        for part in range(2):
            piece = slice(64 * part, 64 * part + 64)
            x, y, z = x_all[piece], y_all[piece], z_all[piece]
            over_i = None
            for i in range(ORDER, -1, -1):
                over_j = None
                for j in range(ORDER - i, -1, -1):
                    over_k = None
                    for k in range(ORDER - i - j, -1, -1):
                        a = INDEX[(i, j, k)]
                        value = loc[a : a + 1, :]
                        over_k = value if over_k is None else over_k * z + value
                    over_j = over_k if over_j is None else over_j * y + over_k
                over_i = over_j if over_i is None else over_i * x + over_j
            result[piece, :] = over_i
        out_ref[...] = near_ref[...] + result[...].T


def cost(flops, moved):
    return pl.CostEstimate(flops=flops, bytes_accessed=moved, transcendentals=0)


def shape(*dims, dtype=F32):
    return jax.ShapeDtypeStruct(dims, dtype)


def limits(mib):
    return pltpu.CompilerParams(vmem_limit_bytes=mib * 1024 * 1024)


def upward_call(dev, pos, chg, up_shift):
    return pl.pallas_call(
        upward_kernel,
        out_shape=(shape(3, 128, 128), shape(3, 16, 128), shape(3, 128)),
        in_specs=[SMEM, VMEM, VMEM, pl.BlockSpec(memory_space=pl.ANY)],
        out_specs=(VMEM, VMEM, VMEM),
        scratch_shapes=[
            pltpu.VMEM((384, 128), F32),
            pltpu.VMEM((16, 384), F32),
            pltpu.VMEM((3, 8 * COEF, 128), F32),
            pltpu.VMEM((8 * COEF, COEF - 256), F32),
            pltpu.SemaphoreType.DMA((3,)),
        ],
        compiler_params=limits(40),
        cost_estimate=cost(10**9, 3 * 10**6),
        name="upward",
    )(dev, pos, chg, up_shift)


def pack_call(asked, lt, pt, lift):
    return pl.pallas_call(
        pack_kernel,
        out_shape=shape(128 * ROWS, 128),
        in_specs=[VMEM] * 4,
        out_specs=VMEM,
        compiler_params=limits(40),
        cost_estimate=cost(10**9, 4 * 10**6),
        name="pack",
    )(asked, lt, pt, lift)


def near_call(dev, near_leaves, near_offsets, pos, chg, before, after):
    return pl.pallas_call(
        near_kernel,
        out_shape=shape(128, 128),
        in_specs=[SMEM] + [VMEM] * 6,
        out_specs=VMEM,
        scratch_shapes=[
            pltpu.VMEM((LEAF + 2 * RIM, 8, 128), F32),
            pltpu.VMEM((LEAF + 2 * RIM, 128), F32),
            pltpu.VMEM((27, 8, 128), F32),
            pltpu.VMEM((NOBODY + 1, 128, 128), BF16),
            pltpu.VMEM((NOBODY + 1, 128, 128), F32),
            pltpu.VMEM((LEAF, 8, 128), F32),
            pltpu.VMEM((GROUP, 48, 128), BF16),
            pltpu.VMEM((40, 128), jnp.int32),
            pltpu.SMEM((40, 128), jnp.int32),
            pltpu.SemaphoreType.DMA(()),
        ],
        compiler_params=limits(40),
        cost_estimate=cost(30 * 10**9, 10**6),
        name="near",
    )(dev, near_leaves, near_offsets, pos, chg, before, after)


def counts_call(far_leaves, far_leaf_class, far_parents, far_parent_class):
    width = far_leaves.shape[0]
    blocks = lambda i: (i, 0)
    whole = lambda i: (0, 0)
    return pl.pallas_call(
        counts_kernel,
        grid=(8,),
        out_shape=(shape(2048, 2176, dtype=BF16), shape(256, 640, dtype=BF16)),
        in_specs=[
            pl.BlockSpec((width, 128), whole),
            pl.BlockSpec((width, 128), whole),
            pl.BlockSpec((16, width), whole),
            pl.BlockSpec((16, width), whole),
        ],
        out_specs=(pl.BlockSpec((256, 2176), blocks), pl.BlockSpec((256, 640), whole)),
        scratch_shapes=[
            pltpu.VMEM((144, 256), jnp.int32),
            pltpu.VMEM((144, 256), jnp.int32),
            pltpu.VMEM((256, 128), F32),
        ],
        compiler_params=limits(40),
        cost_estimate=cost(10 * 10**9, 9 * 10**6),
        name="counts",
    )(far_leaves, far_leaf_class, far_parents, far_parent_class)


def far_call(dev, lists, classes, s, sp, lt, pt, arrived, pos, near, down_shift, far_shift):
    def whole(*dims):
        return pl.BlockSpec(dims, lambda i: (0,) * len(dims))

    hbm = pl.BlockSpec(memory_space=pl.ANY)
    return pl.pallas_call(
        far_kernel,
        grid=(8,),
        out_shape=shape(128, 128),
        in_specs=[
            SMEM, SMEM, SMEM,
            pl.BlockSpec((256, 2176), lambda i: (i, 0)),
            whole(256, 640), whole(3, 128, 128), whole(3, 16, 128), whole(128 * ROWS, 128),
            whole(3, 128, 128), whole(128, 128), hbm, hbm,
        ],
        out_specs=whole(128, 128),
        scratch_shapes=[
            pltpu.VMEM((2176, 640), BF16),
            pltpu.VMEM((640, 640), BF16),
            pltpu.VMEM((3, 16 * TARGETS, 128), F32),
            pltpu.VMEM((3, 128, 128), F32),
            pltpu.VMEM((TARGETS, 384), F32),
            pltpu.VMEM((384, 128), F32),
            pltpu.VMEM((128, 128), F32),
            pltpu.VMEM((3, 8 * COEF, 128), F32),
            pltpu.VMEM((8 * COEF, COEF - 256), F32),
            pltpu.VMEM((3, 16 * COEF, 128), F32),
            pltpu.VMEM((16 * COEF, COEF - 256), F32),
            pltpu.SemaphoreType.DMA((6,)),
        ],
        compiler_params=limits(48),
        cost_estimate=cost(10 * 10**9, 20 * 10**6),
        name="far",
    )(dev, lists, classes, s, sp, lt, pt, arrived, pos, near, down_shift, far_shift)


def by_rows(operators):
    return jnp.swapaxes(operators, 0, 1).reshape(-1, operators.shape[2])


def per_device(
    positions,
    charges,
    near_leaves,
    near_offsets,
    far_leaves,
    far_leaf_class,
    leaf_plan,
    far_parents,
    far_parent_class,
    parent_plan,
    coarse_lists,
    coarse_class,
    up_shift,
    down_shift,
    far_shift,
):
    device = lax.axis_index(AXES)
    dev = device.reshape(1).astype(jnp.int32)
    plans = jnp.concatenate([leaf_plan[0], parent_plan[0]], 1)
    asked = lax.all_to_all(plans, AXES, split_axis=0, concat_axis=0, tiled=True)
    pos = positions.reshape(3, LEAF, 128)
    chg = charges.reshape(LEAF, 128)
    own = jnp.concatenate([pos, chg[None]], 0)
    size = lax.axis_size(AXES)
    up = [(i, i + 1) for i in range(size - 1)]
    down = [(j, i) for i, j in up]
    before = lax.ppermute(own[:, LEAF - RIM :], AXES, up)
    after = lax.ppermute(own[:, :RIM], AXES, down)
    lt, pt, lift = upward_call(dev, pos, chg, by_rows(up_shift))
    outgoing = pack_call(asked, lt, pt, lift).reshape(LEAF, ROWS, 128)
    arrived = lax.all_to_all(outgoing, AXES, split_axis=0, concat_axis=0, tiled=True)
    arrived = arrived.reshape(LEAF * ROWS, 128)
    near = near_call(dev, near_leaves.T, near_offsets.T, pos, chg, before, after)
    s, sp = counts_call(far_leaves.T, far_leaf_class.T, far_parents, far_parent_class)
    potential = far_call(
        dev, coarse_lists.reshape(-1), coarse_class.reshape(-1), s, sp, lt, pt, arrived, pos, near,
        by_rows(down_shift), by_rows(far_shift),
    )
    return potential.reshape(-1)


def solution(mesh):
    row = P(AXES, None)
    placed = (
        P(None, AXES), P(AXES), row, row, row, row, P(AXES, None, None), row, row,
        P(AXES, None, None), P(), P(), P(), P(), P(),
    )
    return jax.shard_map(
        per_device, mesh=mesh, in_specs=placed, out_specs=P(AXES), check_vma=False
    )
```

time: 204 us -> 135 us (0.66); the launches traced: 205 us -> 133 us
  Pallas kernels: 139 us -> 84.3 us
  local copies, waits for them, and re-layouts: 32.3 us -> 15.7 us
  other arithmetic: 6.45 us -> 2.12 us
  starting transfers between devices: 27.3 us -> 30.3 us
    pallas_call x2, Pallas kernels: 70.6 us -> 38.1 us  [the longest x1 36.6 us: near_call(): pl.pallas_call(near_kernel, out_shape=shape(128, 128), in_specs=[SMEM] +...]
    pallas_call x1, Pallas kernels: 52.8 us -> 31.1 us  [far_call(): pl.pallas_call(far_kernel, grid=(8,), out_shape=shape(128, 128), in_specs...]
    unnamed x50 -> x37, local copies, waits for them, and re-layouts: 30.4 us -> 14.7 us
    all_to_all x1, starting transfers between devices: 9.75 us -> 13.2 us  [per_device(): lax.all_to_all(outgoing, AXES, split_axis=0, concat_axis=0, tiled=True)]
  transfers between devices with their start and end apart: 4 -> 4, of which waited for: 0 -> 0; matrix products, arithmetic and copies ran while one was open for 12% -> 2% of each run, Pallas kernels for 42% -> 40%
where the time goes in v2:
time: 135 us; the launch traced here: 133 us
  Pallas kernels  84.3 us (62%)
  starting transfers between devices  30.3 us (22%)
  local copies, waits for them, and re-layouts  15.7 us (12%)
  other arithmetic  2.12 us (2%)
    pallas_call x1, Pallas kernels, near_call(): pl.pallas_call(near_kernel, out_shape=shape(128, 128), in_specs=[SMEM] +...  36.6 us
    pallas_call x1, Pallas kernels, far_call(): pl.pallas_call(far_kernel, grid=(8,), out_shape=shape(128, 128), in_specs...  31.1 us
    unnamed x37, local copies, waits for them, and re-layouts  14.7 us
    all_to_all x1, starting transfers between devices, per_device(): lax.all_to_all(outgoing, AXES, split_axis=0, concat_axis=0, tiled=True)  13.2 us
    all_to_all x1, starting transfers between devices, per_device(): asked = lax.all_to_all(plans, AXES, split_axis=0, concat_axis=0, tiled=True)  11.5 us
    pallas_call x1, Pallas kernels, upward_call(): pl.pallas_call(upward_kernel, out_shape=(shape(3, 128, 128), shape(3, 16,...  8.42 us
    pallas_call x1, Pallas kernels, counts_call(): pl.pallas_call(counts_kernel, grid=(8,), out_shape=(shape(2048, 2176, dty...  6.79 us
    ppermute x1, starting transfers between devices, per_device(): after = lax.ppermute(own[:, :RIM], AXES, down)  2.96 us
  transfers between devices with their start and end apart: 4, of which 0 were waited for; matrix products, arithmetic and copies ran while one was open for 2% of the time, Pallas kernels for 40%

profile of v2, /device:TPU:1, one launch (start us, length us, event | category | flops | bytes accessed | tf_op | source)
XLA Modules:
  0.0 132.8 jit_solution(4655132990534122018)
XLA Ops:
  0.0 0.7 pad_add_fusion
  0.7 0.7 copy.24
  1.5 11.5 %all-to-all-start = ((s32[128,1,20]{2,1,0:T(1,128)}), s32[128,1,20]{2,1,0:T(1,128)S(1)}, u32[]{:S(2)}, u32[]{:S(2)}) async-start(s32[128,1,20]{2,1,0:T(1,128)} %bitcast.8), calls=%async_computation | async-start | bytes 131072 | tf_op jit(solution)/shard_map/all_to_all | solution.py:607
  13.0 1.0 copy.27
  13.9 1.4 %pad_maximum_fusion = (f32[4,32,128]{2,1,0:T(8,128)}, f32[4,32,128]{2,1,0:T(8,128)}) fusion(f32[1,128,128]{2,1,0:T(8,128)} %bitcast.34, f32[3,128,128]{2,1,0:T(8,128)S(1)} %bitcast.30), kind=kLoop, calls=%fused_computation.1 | loop fusion | flops 32768 | bytes 393216 | tf_op jit(solution)/shard_map/concatenate | solution.py:610
  15.3 3.0 %collective-permute-start.1 = (f32[4,32,128]{2,1,0:T(8,128)}, f32[4,32,128]{2,1,0:T(8,128)}, u32[]{:S(2)}, u32[]{:S(2)}) collective-permute-start(f32[4,32,128]{2,1,0:T(8,128)} %get-tuple-element.15), channel_id=1, source_target_pairs={{1,0},{2,1},{3,2},{4,3},{5,4},{6,5},{7,6},{8,7},{9,8},{10,9},{11,1... | collective-permute-start | bytes 196616 | tf_op jit(solution)/shard_map/ppermute | solution.py:615
  18.3 2.6 %collective-permute-start = (f32[4,32,128]{2,1,0:T(8,128)}, f32[4,32,128]{2,1,0:T(8,128)}, u32[]{:S(2)}, u32[]{:S(2)}) collective-permute-start(f32[4,32,128]{2,1,0:T(8,128)} %get-tuple-element.16), channel_id=1, source_target_pairs={{0,1},{1,2},{2,3},{3,4},{4,5},{5,6},{6,7},{7,8},{8,9},{9,10},{10,1... | collective-permute-start | bytes 196616 | tf_op jit(solution)/shard_map/ppermute | solution.py:614
  20.9 0.0 copy-start
  20.9 2.0 %copy-done = f32[8,286,286]{2,0,1:T(8,128)S(1)} copy-done((f32[8,286,286]{2,0,1:T(8,128)S(1)}, f32[8,286,286]{2,0,1:T(8,128)}, u32[]{:S(2)}) %copy-start) | copy-done | bytes 2617496
  22.9 0.0 copy-start.2
  22.9 0.8 copy-done.2
  23.7 8.4 %upward.1 = (f32[3,128,128]{2,1,0:T(8,128)S(1)}, f32[3,16,128]{2,1,0:T(8,128)S(1)}, f32[3,128]{1,0:T(4,128)S(1)}) custom-call(s32[1]{0:T(128)} %bitcast.dev_ref, f32[3,128,128]{2,1,0:T(8,128)S(1)} %bitcast.31, f32[128,128]{1,0:T(8,128)S(1)} %bitcast.35, f32[2288,286]{1,0:T(8,128)S(1)} %bitcast.27), custom_call_target="tpu_custom_call" | custom-call | flops 1000000000 | bytes 3000000 | tf_op jit(solution)/shard_map/upward/pallas_call | solution.py:467
  32.2 0.0 copy-start.4
  32.2 0.0 all-to-all-done
  32.2 1.5 %pack.1 = f32[6144,128]{1,0:T(8,128)S(1)} custom-call(s32[128,20]{1,0:T(8,128)S(1)} %bitcast.37, f32[3,128,128]{2,1,0:T(8,128)S(1)} %get-tuple-element.12.lt_ref, f32[3,16,128]{2,1,0:T(8,128)S(1)} %get-tuple-element.13.pt_ref, f32[3,128]{1,0:T(4,128)S(1)} %get-tuple-element.14.lift_ref), custom_call_target="tpu_custom_call" | custom-call | flops 1000000000 | bytes 4000000 | tf_op jit(solution)/shard_map/pack/pallas_call | solution.py:486
  33.7 0.0 copy-start.1
  33.7 1.6 %copy-done.1 = f32[6144,128]{1,0:T(8,128)} copy-done((f32[6144,128]{1,0:T(8,128)}, f32[6144,128]{1,0:T(8,128)S(1)}, u32[]{:S(2)}) %copy-start.1) | copy-done | bytes 3145752
  35.3 0.0 copy-start.6
  35.3 0.0 copy-start.8
  35.3 0.0 copy-done.4
  35.3 13.2 %all-to-all-start.1 = ((f32[128,48,128]{2,1,0:T(8,128)}), f32[128,48,128]{2,1,0:T(8,128)S(1)}, u32[]{:S(2)}, u32[]{:S(2)}) async-start(f32[128,48,128]{2,1,0:T(8,128)} %bitcast.29), calls=%async_computation.1 | async-start | bytes 6291456 | tf_op jit(solution)/shard_map/all_to_all | solution.py:618
  48.6 0.0 copy-done.6
  48.6 0.0 copy-done.8
  48.6 0.0 copy-start.7
  48.6 0.9 copy-done.7
  49.5 0.0 copy-start.9
  49.5 0.7 copy-done.9
  50.2 0.0 copy-start.15
  50.2 0.0 copy-start.16
  50.2 0.0 copy-start.3
  50.2 6.8 %counts.1 = (bf16[2048,2176]{1,0:T(8,128)(2,1)S(1)}, bf16[256,640]{1,0:T(8,128)(2,1)S(1)}) custom-call(s32[189,128]{1,0:T(8,128)S(1)} %bitcast.38, s32[189,128]{1,0:T(8,128)S(1)} %bitcast.39, s32[16,189]{1,0:T(8,128)S(1)} %copy-done.8, s32[16,189]{1,0:T(8,128)S(1)} %copy-done.9), custom_call_target="tpu_custom_call" | custom-call | flops 10000000000 | bytes 9000000 | tf_op jit(solution)/shard_map/counts/pallas_call | solution.py:525
  57.0 0.0 copy-start.12
  57.0 3.5 %copy-done.12 = bf16[2048,2176]{1,0:T(8,128)(2,1)} copy-done((bf16[2048,2176]{1,0:T(8,128)(2,1)}, bf16[2048,2176]{1,0:T(8,128)(2,1)S(1)}, u32[]{:S(2)}) %copy-start.12) | copy-done | bytes 8912920
  60.5 0.0 copy-start.13
  60.5 0.7 copy-done.13
  61.2 0.0 copy-done.15
  61.2 0.1 copy.22
  61.3 0.1 reshape.36.lists_ref
  61.4 0.0 copy-done.16
  61.4 0.1 copy.23
  61.5 0.1 reshape.37.class_ref
  61.6 0.0 collective-permute-done.1.after_ref
  61.6 0.0 collective-permute-done.before_ref
  61.6 0.0 copy-done.3
  61.6 0.0 copy-start.10
  61.6 0.7 copy-done.10
  62.3 0.0 copy-start.11
  62.3 0.7 copy-done.11
  63.1 36.6 %near.1.near_ref = f32[128,128]{1,0:T(8,128)S(1)} custom-call(s32[1]{0:T(128)} %bitcast.dev_ref, s32[27,128]{1,0:T(8,128)S(1)} %bitcast.40, s32[27,128]{1,0:T(8,128)S(1)} %bitcast.41, f32[3,128,128]{2,1,0:T(8,128)S(1)} %bitcast.32, f32[128,128]{1,0:T(8,128)S(1)} %bitcast.36, f32[4,32,128]{2,1,0:T(8,128)} %collective-permute-done.before_ref, ...), custom_call_target="tpu_custom_call" | custom-call | flops 30000001024 | bytes 1000000 | tf_op jit(solution)/shard_map/near/pallas_call | solution.py:498
  99.6 0.0 all-to-all-done.1
  99.6 0.0 copy-start.5
  99.7 0.9 copy-done.5
  100.6 0.0 copy-start.14
  100.6 1.0 copy-done.14
  101.6 31.1 %far.1 = f32[128,128]{1,0:T(8,128)} custom-call(s32[1]{0:T(128)} %bitcast.dev_ref, s32[224]{0:T(256)S(1)} %reshape.36.lists_ref, s32[224]{0:T(256)S(1)} %reshape.37.class_ref, bf16[2048,2176]{1,0:T(8,128)(2,1)} %copy-done.12, bf16[256,640]{1,0:T(8,128)(2,1)S(1)} %copy-done.14, f32[3,128,128]{2,1,0:T(8,128)S(1)} %copy-done.5, ...), custom_call_target="tpu_custom_call" | custom-call | flops 10000000000 | bytes 20000000 | tf_op jit(solution)/shard_map/far/pallas_call | solution.py:552
Async XLA Ops:
  1.5 30.7 %all-to-all-start = ((s32[128,1,20]{2,1,0:T(1,128)}), s32[128,1,20]{2,1,0:T(1,128)S(1)}, u32[]{:S(2)}, u32[]{:S(2)}) async-start(s32[128,1,20]{2,1,0:T(1,128)} %bitcast.8), calls=%async_computation | async-start | bytes 131072 | tf_op jit(solution)/shard_map/all_to_all | solution.py:607
  15.3 46.3 %collective-permute-start.1 = (f32[4,32,128]{2,1,0:T(8,128)}, f32[4,32,128]{2,1,0:T(8,128)}, u32[]{:S(2)}, u32[]{:S(2)}) collective-permute-start(f32[4,32,128]{2,1,0:T(8,128)} %get-tuple-element.15), channel_id=1, source_target_pairs={{1,0},{2,1},{3,2},{4,3},{5,4},{6,5},{7,6},{8,7},{9,8},{10,9},{11,1... | collective-permute-start | bytes 196616 | tf_op jit(solution)/shard_map/ppermute | solution.py:615
  18.3 43.3 %collective-permute-start = (f32[4,32,128]{2,1,0:T(8,128)}, f32[4,32,128]{2,1,0:T(8,128)}, u32[]{:S(2)}, u32[]{:S(2)}) collective-permute-start(f32[4,32,128]{2,1,0:T(8,128)} %get-tuple-element.16), channel_id=1, source_target_pairs={{0,1},{1,2},{2,3},{3,4},{4,5},{5,6},{6,7},{7,8},{8,9},{9,10},{10,1... | collective-permute-start | bytes 196616 | tf_op jit(solution)/shard_map/ppermute | solution.py:614
  20.9 2.0 %copy-start = (f32[8,286,286]{2,0,1:T(8,128)S(1)}, f32[8,286,286]{2,0,1:T(8,128)}, u32[]{:S(2)}) copy-start(f32[8,286,286]{2,0,1:T(8,128)} %param.27) | copy-start | bytes 7852420
  22.9 0.8 copy-start.2
  32.2 3.2 %copy-start.4 = (f32[3,128,128]{2,1,0:T(8,128)}, f32[3,128,128]{2,1,0:T(8,128)S(1)}, u32[]{:S(2)}) copy-start(f32[3,128,128]{2,1,0:T(8,128)S(1)} %get-tuple-element.12.lt_ref) | copy-start | bytes 589828
  33.7 1.6 %copy-start.1 = (f32[6144,128]{1,0:T(8,128)}, f32[6144,128]{1,0:T(8,128)S(1)}, u32[]{:S(2)}) copy-start(f32[6144,128]{1,0:T(8,128)S(1)} %pack.1) | copy-start | bytes 9437188
  35.3 13.2 %copy-start.6 = (s32[128,189]{0,1:T(8,128)S(1)}, s32[128,189]{0,1:T(8,128)}, u32[]{:S(2)}) copy-start(s32[128,189]{0,1:T(8,128)} %param.19) | copy-start | bytes 290308
  35.3 13.3 %copy-start.8 = (s32[16,189]{1,0:T(8,128)S(1)}, s32[16,189]{1,0:T(8,128)}, u32[]{:S(2)}) copy-start(s32[16,189]{1,0:T(8,128)} %parent_ref.1) | copy-start | bytes 36292
  35.3 64.3 %all-to-all-start.1 = ((f32[128,48,128]{2,1,0:T(8,128)}), f32[128,48,128]{2,1,0:T(8,128)S(1)}, u32[]{:S(2)}, u32[]{:S(2)}) async-start(f32[128,48,128]{2,1,0:T(8,128)} %bitcast.29), calls=%async_computation.1 | async-start | bytes 6291456 | tf_op jit(solution)/shard_map/all_to_all | solution.py:618
  48.6 0.9 copy-start.7
  49.5 0.7 copy-start.9
  50.2 11.0 %copy-start.15 = (s32[32,7]{0,1:T(8,128)S(1)}, s32[32,7]{0,1:T(8,128)}, u32[]{:S(2)}) copy-start(s32[32,7]{0,1:T(8,128)} %param.25) | copy-start | bytes 2692
  50.2 11.2 %copy-start.16 = (s32[32,7]{0,1:T(8,128)S(1)}, s32[32,7]{0,1:T(8,128)}, u32[]{:S(2)}) copy-start(s32[32,7]{0,1:T(8,128)} %param.26) | copy-start | bytes 2692
  50.2 11.4 %copy-start.3 = (f32[16384]{0:T(1024)S(1)}, f32[16384]{0:T(1024)}, u32[]{:S(2)}) copy-start(f32[16384]{0:T(1024)} %param.16) | copy-start | bytes 196612
  57.0 3.5 %copy-start.12 = (bf16[2048,2176]{1,0:T(8,128)(2,1)}, bf16[2048,2176]{1,0:T(8,128)(2,1)S(1)}, u32[]{:S(2)}) copy-start(bf16[2048,2176]{1,0:T(8,128)(2,1)S(1)} %get-tuple-element.10.s_ref) | copy-start | bytes 26738692
  60.5 0.7 copy-start.13
  61.6 0.7 copy-start.10
  62.3 0.7 copy-start.11
  99.6 0.9 copy-start.5
  100.6 1.0 copy-start.14

commit v3 on v2

v3 whole, which is shorter than its diff:
```python
import jax
import jax.numpy as jnp
import numpy as np
from jax import lax
from jax.experimental import pallas as pl
from jax.experimental.pallas import tpu as pltpu
from jax.sharding import PartitionSpec as P

ORDER = 10
COEF = 286
RIM = 32
LEAF = 128
K_NEAR = 27
CAP_L = 16
CAP_P = 4
ROWS = 48
PLAN = 24
TARGETS = 160
GROUP = 64
NOBODY = LEAF + 2 * RIM
SOFT = 0.05 * 0.05
AXES = ("gx", "gy")
F32 = jnp.float32
BF16 = jnp.bfloat16
VMEM = pl.BlockSpec(memory_space=pltpu.VMEM)
SMEM = pl.BlockSpec(memory_space=pltpu.SMEM)


def exponents(order):
    entries = []
    for degree in range(order + 1):
        for first_power in range(degree, -1, -1):
            for second_power in range(degree - first_power, -1, -1):
                entries.append((first_power, second_power, degree - first_power - second_power))
    return entries


INDEX = {powers: number for number, powers in enumerate(exponents(ORDER))}


def split(x):
    high = x.astype(BF16)
    return high, (x - high.astype(F32)).astype(BF16)


def nt(a, b):
    return lax.dot_general(a, b, (((1,), (1,)), ((), ())), preferred_element_type=F32)


def nn(a, b):
    return jnp.dot(a, b, preferred_element_type=F32)


def turn(x, left):
    return pltpu.roll(x, 128 - left, 1)


def apply_parts(operator, high, low):
    operator_high, operator_low = split(operator)
    both = nn(operator_high, jnp.concatenate([high, low], axis=1))
    return both[:, 0:128] + (both[:, 128:256] + nn(operator_low, high))


def apply_operator(operator, columns):
    return apply_parts(operator, *split(columns))


def cut(source, chunks):
    chunks[0] = source[:, 0:128]
    chunks[1] = source[:, 128:256]
    chunks[2] = jnp.zeros(chunks.shape[1:], F32)
    chunks[2, :, 0 : COEF - 256] = source[:, 256:COEF]


def operator_at(chunks, number, count):
    rows = pl.ds(number, COEF, stride=count)
    return jnp.concatenate([chunks[h, rows, :] for h in range(3)], axis=1)


def upward_kernel(dev_ref, pos_ref, chg_ref, stored_up, lt_ref, pt_ref, lift_ref, moments, column,
                  up_ref):
    x, y, z = [2.0 * pos_ref[d].T for d in range(3)]
    with_x = chg_ref[...].T
    z_powers = [None, z]
    for k in range(ORDER - 1):
        z_powers.append(z_powers[-1] * z)
    moments[COEF - 6 : 384, :] = jnp.zeros((384 - COEF + 6, LEAF), F32)
    for i in range(ORDER + 1):
        if i:
            with_x = with_x * x
        with_xy = with_x
        for j in range(ORDER + 1 - i):
            if j:
                with_xy = with_xy * y
            for k in range(ORDER + 1 - i - j):
                term = with_xy * z_powers[k] if k else with_xy
                a = INDEX[(i, j, k)]
                moments[a : a + 1, :] = jnp.sum(term, axis=0, keepdims=True)
    for h in range(3):
        lt_ref[h] = moments[128 * h : 128 * h + 128, :].T
    column[...] = jnp.zeros_like(column)
    cut(stored_up, up_ref)
    lane = lax.broadcasted_iota(jnp.int32, (384, 128), 1)
    leaves = moments[...]
    total = jnp.zeros((COEF, 128), F32)
    for c in range(8):
        total = total + apply_operator(
            operator_at(up_ref, c, 8), jnp.where(lane % 8 == c, leaves, 0.0)
        )
    for left in (4, 2, 1):
        total = total + turn(total, left)
    column[0:COEF, :] = total
    parents = column[...]
    total = jnp.zeros((COEF, 128), F32)
    for c in range(8):
        total = total + apply_operator(
            operator_at(up_ref, c, 8), jnp.where(lane % 64 == 8 * c, parents, 0.0)
        )
    for h in range(3):
        moments[0:128, :] = column[128 * h : 128 * h + 128, :].T
        pt_ref[h] = moments[pl.ds(0, 16, stride=8), :]
    for left in (8, 16, 32):
        total = total + turn(total, left)
    column[0:COEF, :] = total
    grand = column[...]
    first = lax.rem(2 * dev_ref[0], 8)
    total = apply_operator(operator_at(up_ref, first, 8), jnp.where(lane == 0, grand, 0.0))
    total = total + apply_operator(
        operator_at(up_ref, first + 1, 8), jnp.where(lane == 64, grand, 0.0)
    )
    column[0:COEF, :] = total + turn(total, 64)
    for h in range(3):
        lift_ref[h : h + 1, :] = column[128 * h : 128 * h + 128, :].T[0:1, :]


def pack_kernel(dev_ref, asked_ref, lt_ref, pt_ref, lift_ref, out_ref):
    lane = lax.broadcasted_iota(jnp.int32, (128, 128), 1)
    leaf_rows = jnp.concatenate([lt_ref[h] for h in range(3)], axis=1)
    parent_rows = jnp.concatenate([pt_ref[h] for h in range(3)], axis=1)
    parent_rows = jnp.concatenate([parent_rows, jnp.zeros((112, 384), F32)], axis=0)
    leaf_rows = jnp.concatenate(split(leaf_rows), axis=0)
    parent_rows = jnp.concatenate(split(parent_rows), axis=0)
    for q in range(5):
        tail = jnp.zeros((128, 128), F32)
        for p in range(4):
            j = 4 * q + p
            asked = asked_ref[pl.ds(j, 128, stride=PLAN), :]
            asked = jnp.where(lane == dev_ref[0], asked.astype(F32), 0.0)
            asked = jnp.sum(asked, axis=1, keepdims=True)
            chosen = jnp.where(asked == lane.astype(F32), 1.0, 0.0).astype(BF16)
            chosen = jnp.concatenate([chosen, chosen], axis=1)
            rows = nn(chosen, leaf_rows if q < 4 else parent_rows)
            out_ref[pl.ds(2 * j, 128, stride=ROWS), :] = rows[:, 0:128]
            out_ref[pl.ds(2 * j + 1, 128, stride=ROWS), :] = rows[:, 128:256]
            part = rows[:, 256:384]
            tail = tail + (pltpu.roll(part, 32 * p, 1) if p else part)
        out_ref[pl.ds(40 + q, 128, stride=ROWS), :] = tail
    for h in range(3):
        out_ref[pl.ds(45 + h, 128, stride=ROWS), :] = jnp.broadcast_to(lift_ref[h : h + 1, :], (128, 128))


def near_kernel(dev_ref, leaves_ref, offsets_ref, pos_ref, chg_ref, before_ref, after_ref, out_ref,
                eight, charge, offsets, features, spread, sums, ready, lists, plan, sem):
    sub = lax.broadcasted_iota(jnp.int32, (8, 128), 0)
    named = leaves_ref[...]
    first_leaf = dev_ref[0] * LEAF
    present = named >= 0
    own_id = first_leaf + lax.broadcasted_iota(jnp.int32, (K_NEAR, LEAF), 1)
    itself = (named == own_id) & (offsets_ref[...] == 13)
    counted = present & jnp.logical_not(itself)
    code = jnp.where(counted, (named - first_leaf + RIM) * 32 + offsets_ref[...], NOBODY * 32 + 13)
    count = jnp.sum(jnp.where(present, 1.0, 0.0), axis=0, keepdims=True).astype(jnp.int32)
    quads = jnp.maximum((count + 2) // 4, 1)
    selves = jnp.sum(jnp.where(itself, 1.0, 0.0), axis=0, keepdims=True).astype(jnp.int32)
    total = jnp.sum(quads.astype(F32), axis=1, keepdims=True).astype(jnp.int32)
    lists[...] = jnp.full_like(lists, NOBODY * 32 + 13)
    lists[0:K_NEAR, :] = code
    lists[37:38, :] = quads
    lists[38:39, :] = selves
    lists[39:40, :] = jnp.broadcast_to(total, (1, 128))
    copy = pltpu.make_async_copy(lists, plan, sem)
    copy.start()
    eight[:, 3, :] = jnp.full((LEAF + 2 * RIM, 128), 1.0, F32)
    eight[:, 7, :] = jnp.full((LEAF + 2 * RIM, 128), SOFT, F32)
    eight3 = ((0, 4), (1, 5), (2, 6))
    for d in range(3):
        for row in eight3[d]:
            eight[0:RIM, row, :] = before_ref[d]
            eight[RIM : RIM + LEAF, row, :] = pos_ref[d]
            eight[RIM + LEAF : 2 * RIM + LEAF, row, :] = after_ref[d]
    charge[0:RIM, :] = before_ref[3]
    charge[RIM : RIM + LEAF, :] = chg_ref[...]
    charge[RIM + LEAF : 2 * RIM + LEAF, :] = after_ref[3]
    lane = lax.broadcasted_iota(jnp.int32, (128, 128), 1)
    features[NOBODY] = jnp.where(lane == 7, 1.0, 0.0).astype(BF16)
    spread[NOBODY] = jnp.zeros((128, 128), F32)
    for o in range(27):
        shift = (o // 9 - 1, o // 3 % 3 - 1, o % 3 - 1)
        table = jnp.zeros((8, 128), F32)
        for d in range(3):
            table = jnp.where((sub == d) | (sub == d + 4), -float(shift[d]), table)
        offsets[o] = table
    squares = (sub >= 4) & (sub < 7)

    def thirds(v):
        high = v.astype(BF16).astype(F32)
        rest = v - high
        middle = rest.astype(BF16).astype(F32)
        return high, middle, rest - middle

    def target(leaf, offset):
        v = eight[RIM + leaf] + offsets[offset]
        v = jnp.where(squares, v * v, v)
        high, middle, low = thirds(v)
        return jnp.concatenate([high, high, high, middle, middle, low], axis=0).astype(BF16)

    def separations(leaf, rows):
        padded = jnp.concatenate([rows, jnp.zeros((80, 128), BF16)], axis=0)
        return nn(features[leaf], padded)

    row = lax.broadcasted_iota(jnp.int32, (128, 128), 0)
    three = jnp.where((row >= 48) & (row < 51), 1.0, 0.0).astype(BF16)
    diagonal = row == lane
    identity = jnp.where(diagonal, 1.0, 0.0).astype(BF16)

    def source(leaf):
        v = eight[leaf]
        norm = jnp.sum(jnp.where(sub < 3, v * v, 0.0), axis=0, keepdims=True)
        v = jnp.where(sub < 3, -2.0 * v, jnp.where(sub == 3, norm, 1.0))
        high, middle, low = thirds(v)
        first, second, third = thirds(charge[pl.ds(leaf, 1), :])
        parts = jnp.where(sub == 0, first, jnp.where(sub == 1, second, jnp.where(sub == 2, third, 0.0)))
        rows = jnp.concatenate([high, middle, low, high, middle, high, parts], axis=0)
        rows = jnp.concatenate([rows, jnp.zeros((72, 128), F32)], axis=0)
        rows = rows.T.astype(BF16)
        features[leaf] = rows
        spread[leaf] = nn(rows, three)

    def prepare(step, carry):
        for u in range(16):
            source(16 * step + u)
        return carry

    lax.fori_loop(0, (LEAF + 2 * RIM) // 16, prepare, 0)
    copy.wait()

    def own_leaf(step, carry):
        for u in range(16):
            leaf = 16 * step + u
            squared = separations(RIM + leaf, target(leaf, 13))
            terms = jnp.where(diagonal, 0.0, spread[RIM + leaf] * lax.rsqrt(squared))
            sums[leaf] = jnp.sum(terms.reshape(16, 8, 128), axis=0) * plan[38, leaf].astype(F32)
        return carry

    lax.fori_loop(0, LEAF // 16, own_leaf, 0)

    def advance(state):
        leaf, quad = state
        last = quad + 1 >= plan[37, leaf]
        return (
            jnp.where(last, jnp.minimum(leaf + 1, LEAF - 1), leaf),
            jnp.where(last, jnp.where(leaf == LEAF - 1, 7, 0), quad + 1),
        )

    def produce(states):
        for g, (leaf, quad) in enumerate(states):
            for u in range(4):
                code = plan[4 * quad + u + 1, leaf]
                ready[4 * g + u] = target(leaf, code & 31)

    def consume(states):
        for g, (leaf, quad) in enumerate(states):
            part = sums[leaf]
            for u in range(4):
                code = plan[4 * quad + u + 1, leaf]
                squared = separations(code >> 5, ready[4 * g + u])
                terms = spread[code >> 5] * lax.rsqrt(squared)
                part = part + jnp.sum(terms.reshape(16, 8, 128), axis=0)
            sums[leaf] = part

    def following(state, number):
        made = []
        for _ in range(number):
            state = advance(state)
            made.append(state)
        return tuple(made)

    first = (jnp.int32(0), jnp.int32(0))
    states = (first,) + following(first, GROUP // 4 - 1)
    produce(states)

    def one_group(step, states):
        after = following(states[-1], GROUP // 4)
        consume(states)
        produce(after)
        return after

    quads = GROUP // 4
    lax.fori_loop(0, (plan[39, 0] + quads - 1) // quads, one_group, states)
    out_ref[...] = jnp.sum(sums[...], axis=1)


def count_rows(code, low, rows):
    wide = lax.broadcasted_iota(jnp.int32, (rows, 256), 0) == code
    narrow = lax.broadcasted_iota(jnp.int32, (128, 256), 0) == low
    return nt(
        jnp.where(wide, 1.0, 0.0).astype(BF16), jnp.where(narrow, 1.0, 0.0).astype(BF16)
    ).astype(BF16)


def encode(slots, classes, cells, capacity):
    ghost = jnp.maximum(slots - cells, 0)
    own = slots < cells
    code = jnp.where(own, 0, 1 + lax.rem(ghost, capacity)) * 16 + classes
    return jnp.where(slots < 0, -1, code), jnp.where(own, slots, lax.div(ghost, capacity))


def far_kernel(dev_ref, lists_ref, class_ref, leaf_ref, leaf_class_ref, parent_ref, parent_class_ref,
               lt_ref, pt_ref, arrived_ref, pos_ref, near_ref, stored_down, stored_far, out_ref,
               src, src_parent, even, odd, even_parent, grouped, code_scr, low_scr, turned, column, loc,
               result, down_ref, far_ref):
    lane = lax.broadcasted_iota(jnp.int32, (128, 128), 1)

    def count(first, capacity, table_ref):
        blocks = capacity + 1
        for t in range(16):
            rows = pl.ds(first + t, 1)
            table = count_rows(code_scr[rows, :], low_scr[rows, :], 16 * blocks)
            for b in range(blocks):
                table_ref[16 * t : 16 * t + 16, 128 * b : 128 * b + 128] = table[
                    16 * b : 16 * b + 16
                ]

    def place(ref, row, parts):
        count = parts[0].shape[0]
        (h0, l0), (h1, l1) = split(parts[0]), split(parts[1])
        tail = parts[2]
        high = tail.astype(BF16).astype(F32)
        low = pltpu.roll(tail - high, 32, 1)
        ref[row : row + count, 0:128] = h0
        ref[row : row + count, 128:256] = h1
        ref[row : row + count, 256:384] = l0
        ref[row : row + count, 384:512] = l1
        ref[row : row + count, 512:640] = (high + low).astype(BF16)

    def collect(product, row, count):
        grouped[0, pl.ds(row, count), :] = product[:, 0:128] + product[:, 256:384]
        grouped[1, pl.ds(row, count), :] = product[:, 128:256] + product[:, 384:512]
        tail = product[:, 512:640]
        grouped[2, pl.ds(row, count), :] = tail + pltpu.roll(tail, 96, 1)

    def arrived_tail(row, p):
        part = arrived_ref[pl.ds(row, 128, stride=ROWS), :]
        part = pltpu.roll(part, 128 - 32 * p, 1) if p else part
        return jnp.where(lane < 32, part, 0.0)

    width = leaf_ref.shape[0]
    code_scr[...] = jnp.full_like(code_scr, -1)
    low_scr[...] = jnp.full_like(low_scr, -1)
    for part, scratch in zip(
        encode(leaf_ref[...], leaf_class_ref[...], LEAF, CAP_L), (code_scr, low_scr)
    ):
        turned[...] = jnp.full_like(turned, -1.0)
        turned[:width, :] = part.astype(F32)
        scratch[0:128, 0:128] = turned[0:128, :].T.astype(jnp.int32)
        scratch[0:128, 128:256] = turned[128:256, :].T.astype(jnp.int32)
    for part, scratch in zip(
        encode(parent_ref[...], parent_class_ref[...], 16, CAP_P), (code_scr, low_scr)
    ):
        scratch[128:144, :width] = part
    count(128, CAP_P, even_parent)
    count(0, CAP_L, even)
    place(src, 0, [lt_ref[h] for h in range(3)])
    for c in range(CAP_L):
        place(
            src,
            128 * (c + 1),
            [arrived_ref[pl.ds(2 * c, 128, stride=ROWS), :], arrived_ref[pl.ds(2 * c + 1, 128, stride=ROWS), :], arrived_tail(40 + c // 4, c % 4)],
        )
    own = [jnp.concatenate([pt_ref[h], jnp.zeros((112, 128), F32)], axis=0) for h in range(3)]
    place(src_parent, 0, own)
    for c in range(CAP_P):
        place(
            src_parent,
            128 * (c + 1),
            [arrived_ref[pl.ds(32 + 2 * c, 128, stride=ROWS), :], arrived_ref[pl.ds(33 + 2 * c, 128, stride=ROWS), :], arrived_tail(44, c)],
        )
    collect(nn(even_parent[...], src_parent[...]), 2048, 256)
    mine = dev_ref[0] // 4
    operator = lax.broadcasted_iota(jnp.int32, (16, 128), 0)
    cell = lax.broadcasted_iota(jnp.int32, (16, 128), 1) // 4
    chosen = jnp.zeros((16, 128), F32)
    for k in range(7):
        hit = (operator == class_ref[mine * 7 + k]) & (cell == lists_ref[mine * 7 + k])
        chosen = chosen + jnp.where(hit, 1.0, 0.0)
    chosen = chosen.astype(BF16)
    for h in range(3):
        high, low = split(arrived_ref[pl.ds(45 + h, 128, stride=ROWS), :])
        grouped[h, 2304:2320, :] = nn(chosen, high) + nn(chosen, low)
        grouped[h, 2320:2560, :] = jnp.zeros((240, 128), F32)

    def two_blocks(step, carry):
        row = pl.multiple_of(step * 512, 512)
        count(32 * step + 16, CAP_L, odd)
        collect(nn(even[...], src[...]), row, 256)
        count(jnp.minimum(32 * step + 32, 112), CAP_L, even)
        collect(nn(odd[...], src[...]), row + 256, 256)
        return carry

    lax.fori_loop(0, 4, two_blocks, 0)

    cut(stored_far, far_ref)
    column[...] = jnp.zeros_like(column)
    loc[...] = jnp.zeros_like(loc)
    tall = lax.broadcasted_iota(jnp.int32, (384, 128), 1)
    leaf_total = jnp.zeros((COEF, 128), F32)
    upper_total = jnp.zeros((COEF, 128), F32)
    for q in range(4):
        upper = jnp.concatenate(
            [
                jnp.concatenate(
                    [grouped[h, pl.ds(2048 + 4 * q + p, 32, stride=16), :] for p in range(4)],
                    axis=0,
                ).T
                for h in range(3)
            ],
            axis=0,
        )
        for p in range(4):
            o = 4 * q + p
            leaf = jnp.concatenate(
                [grouped[h, pl.ds(o, 128, stride=16), :].T for h in range(3)], axis=0
            )
            operator_high, operator_low = split(operator_at(far_ref, o, 16))
            leaf_high, leaf_low = split(leaf)
            upper_high, upper_low = split(jnp.where(tall // 32 == p, upper, 0.0))
            first = nn(operator_high, jnp.concatenate([leaf_high, leaf_low], axis=1))
            second = nn(operator_high, jnp.concatenate([upper_high, upper_low], axis=1))
            third = nn(operator_low, jnp.concatenate([leaf_high, upper_high], axis=1))
            leaf_total = leaf_total + (first[:, 0:128] + (first[:, 128:256] + third[:, 0:128]))
            upper_total = upper_total + (
                second[:, 0:128] + (second[:, 128:256] + third[:, 128:256])
            )
    upper_total = upper_total + turn(upper_total, 32)
    upper_total = upper_total + turn(upper_total, 64)
    cut(stored_down, down_ref)
    column[0:COEF, :] = upper_total
    coarse = jnp.broadcast_to(column[:, 16:17], (384, 128))
    first = lax.rem(2 * dev_ref[0], 8)
    grand = apply_operator(operator_at(down_ref, first, 8), jnp.where(tall < 8, coarse, 0.0))
    grand = grand + apply_operator(
        operator_at(down_ref, first + 1, 8), jnp.where((tall >= 8) & (tall < 16), coarse, 0.0)
    )
    loc[0:COEF, :] = grand
    grand = loc[...]
    for c in range(8):
        upper_total = upper_total + apply_operator(
            operator_at(down_ref, c, 8), jnp.where((tall % 8 == c) & (tall < 16), grand, 0.0)
        )
    column[0:COEF, :] = upper_total
    parents = split(jnp.where(tall < 16, column[...], 0.0))
    repeat = lax.broadcasted_iota(jnp.int32, (128, 128), 0) == lane // 8
    repeat = jnp.where(repeat, 1.0, 0.0).astype(BF16)
    parents = [nn(part, repeat) for part in parents]
    for c in range(8):
        high, low = [jnp.where(tall % 8 == c, part, 0.0).astype(BF16) for part in parents]
        leaf_total = leaf_total + apply_parts(operator_at(down_ref, c, 8), high, low)
    loc[0:COEF, :] = leaf_total
    x_all, y_all, z_all = [2.0 * pos_ref[d].T for d in range(3)]
    for part in range(2):
        piece = slice(64 * part, 64 * part + 64)
        x, y, z = x_all[piece], y_all[piece], z_all[piece]
        over_i = None
        for i in range(ORDER, -1, -1):
            over_j = None
            for j in range(ORDER - i, -1, -1):
                over_k = None
                for k in range(ORDER - i - j, -1, -1):
                    a = INDEX[(i, j, k)]
                    value = loc[a : a + 1, :]
                    over_k = value if over_k is None else over_k * z + value
                over_j = over_k if over_j is None else over_j * y + over_k
            over_i = over_j if over_i is None else over_i * x + over_j
        result[piece, :] = over_i
    out_ref[...] = near_ref[...] + result[...].T


def cost(flops, moved):
    return pl.CostEstimate(flops=flops, bytes_accessed=moved, transcendentals=0)


def shape(*dims, dtype=F32):
    return jax.ShapeDtypeStruct(dims, dtype)


def limits(mib):
    return pltpu.CompilerParams(vmem_limit_bytes=mib * 1024 * 1024)


def upward_call(dev, pos, chg, up_shift):
    return pl.pallas_call(
        upward_kernel,
        out_shape=(shape(3, 128, 128), shape(3, 16, 128), shape(3, 128)),
        in_specs=[SMEM] + [VMEM] * 3,
        out_specs=(VMEM, VMEM, VMEM),
        scratch_shapes=[
            pltpu.VMEM((384, 128), F32),
            pltpu.VMEM((384, 128), F32),
            pltpu.VMEM((3, 8 * COEF, 128), F32),
        ],
        compiler_params=limits(16),
        cost_estimate=cost(8 * 10**9, 3 * 10**6),
        name="upward",
    )(dev, pos, chg, up_shift)


def pack_call(dev, asked, lt, pt, lift):
    return pl.pallas_call(
        pack_kernel,
        out_shape=shape(128 * ROWS, 128),
        in_specs=[SMEM] + [VMEM] * 4,
        out_specs=VMEM,
        compiler_params=limits(24),
        cost_estimate=cost(10**9, 4 * 10**6),
        name="pack",
    )(dev, asked, lt, pt, lift)


def near_call(dev, near_leaves, near_offsets, pos, chg, before, after):
    return pl.pallas_call(
        near_kernel,
        out_shape=shape(128, 128),
        in_specs=[SMEM] + [VMEM] * 6,
        out_specs=VMEM,
        scratch_shapes=[
            pltpu.VMEM((LEAF + 2 * RIM, 8, 128), F32),
            pltpu.VMEM((LEAF + 2 * RIM, 128), F32),
            pltpu.VMEM((27, 8, 128), F32),
            pltpu.VMEM((NOBODY + 1, 128, 128), BF16),
            pltpu.VMEM((NOBODY + 1, 128, 128), F32),
            pltpu.VMEM((LEAF, 8, 128), F32),
            pltpu.VMEM((GROUP, 48, 128), BF16),
            pltpu.VMEM((40, 128), jnp.int32),
            pltpu.SMEM((40, 128), jnp.int32),
            pltpu.SemaphoreType.DMA(()),
        ],
        compiler_params=limits(24),
        cost_estimate=cost(30 * 10**9, 10**6),
        name="near",
    )(dev, near_leaves, near_offsets, pos, chg, before, after)


def far_call(dev, lists, classes, leaves, leaf_class, parents, parent_class, lt, pt, arrived, pos, near,
             down_shift, far_shift):
    return pl.pallas_call(
        far_kernel,
        out_shape=shape(128, 128),
        in_specs=[SMEM] * 3 + [VMEM] * 11,
        out_specs=VMEM,
        scratch_shapes=[
            pltpu.VMEM((2176, 640), BF16),
            pltpu.VMEM((640, 640), BF16),
            pltpu.VMEM((256, 2176), BF16),
            pltpu.VMEM((256, 2176), BF16),
            pltpu.VMEM((256, 640), BF16),
            pltpu.VMEM((3, 16 * TARGETS, 128), F32),
            pltpu.VMEM((144, 256), jnp.int32),
            pltpu.VMEM((144, 256), jnp.int32),
            pltpu.VMEM((256, 128), F32),
            pltpu.VMEM((384, 128), F32),
            pltpu.VMEM((384, 128), F32),
            pltpu.VMEM((128, 128), F32),
            pltpu.VMEM((3, 8 * COEF, 128), F32),
            pltpu.VMEM((3, 16 * COEF, 128), F32),
        ],
        compiler_params=limits(40),
        cost_estimate=cost(20 * 10**9, 20 * 10**6),
        name="far",
    )(dev, lists, classes, leaves, leaf_class, parents, parent_class, lt, pt, arrived, pos, near,
      down_shift, far_shift)


def by_rows(operators):
    return jnp.swapaxes(operators, 0, 1).reshape(-1, operators.shape[2])


def per_device(
    positions,
    charges,
    near_leaves,
    near_offsets,
    far_leaves,
    far_leaf_class,
    leaf_plan,
    far_parents,
    far_parent_class,
    parent_plan,
    coarse_lists,
    coarse_class,
    up_shift,
    down_shift,
    far_shift,
):
    device = lax.axis_index(AXES)
    dev = device.reshape(1).astype(jnp.int32)
    filler = jnp.full((PLAN - CAP_L - CAP_P, 128), -1, jnp.int32)
    plans = jnp.concatenate([leaf_plan[0].T, parent_plan[0].T, filler], 0)
    asked = lax.all_gather(plans, AXES, axis=0, tiled=True)
    pos = positions.reshape(3, LEAF, 128)
    chg = charges.reshape(LEAF, 128)
    own = jnp.concatenate([pos, chg[None]], 0)
    size = lax.axis_size(AXES)
    up = [(i, i + 1) for i in range(size - 1)]
    down = [(j, i) for i, j in up]
    before = lax.ppermute(own[:, LEAF - RIM :], AXES, up)
    after = lax.ppermute(own[:, :RIM], AXES, down)
    lt, pt, lift = upward_call(dev, pos, chg, by_rows(up_shift))
    outgoing = pack_call(dev, asked, lt, pt, lift).reshape(LEAF, ROWS, 128)
    near_leaves, outgoing = lax.optimization_barrier((near_leaves, outgoing))
    arrived = lax.all_to_all(outgoing, AXES, split_axis=0, concat_axis=0, tiled=True)
    arrived = arrived.reshape(LEAF * ROWS, 128)
    near = near_call(dev, near_leaves.T, near_offsets.T, pos, chg, before, after)
    potential = far_call(
        dev, coarse_lists.reshape(-1), coarse_class.reshape(-1), far_leaves.T, far_leaf_class.T,
        far_parents, far_parent_class, lt, pt, arrived, pos, near,
        by_rows(down_shift), by_rows(far_shift),
    )
    return potential.reshape(-1)


def solution(mesh):
    row = P(AXES, None)
    placed = (
        P(None, AXES), P(AXES), row, row, row, row, P(AXES, None, None), row, row,
        P(AXES, None, None), P(), P(), P(), P(), P(),
    )
    return jax.shard_map(
        per_device, mesh=mesh, in_specs=placed, out_specs=P(AXES), check_vma=False
    )
```

time: 135 us -> 215 us (1.59)
  the two profiles are of different devices: /device:TPU:1 before, /device:TPU:96 now
where the time goes in v3:
time: 215 us; the launch traced here: 212 us
  waiting for transfers between devices  81.5 us (38%)
  Pallas kernels  75.7 us (35%)
  local copies, waits for them, and re-layouts  21 us (10%)
  starting transfers between devices  17.8 us (8%)
  between operations  13.5 us (6%)
  other arithmetic  2.77 us (1%)
    all_gather x1, waiting for transfers between devices, per_device(): asked = lax.all_gather(plans, AXES, axis=0, tiled=True)  55.6 us
    pallas_call x1, Pallas kernels, near_call(): pl.pallas_call(near_kernel, out_shape=shape(128, 128), in_specs=[SMEM] +...  36.7 us
    pallas_call x1, Pallas kernels, far_call(): pl.pallas_call(far_kernel, out_shape=shape(128, 128), in_specs=[SMEM] * 3...  29.7 us
    ppermute x1, waiting for transfers between devices, per_device(): before = lax.ppermute(own[:, LEAF - RIM:], AXES, up)  25.9 us
    unnamed x39, local copies, waits for them, and re-layouts  19.3 us
    all_to_all x1, starting transfers between devices, per_device(): lax.all_to_all(outgoing, AXES, split_axis=0, concat_axis=0, tiled=True)  8.06 us
    ppermute x1, starting transfers between devices, per_device(): after = lax.ppermute(own[:, :RIM], AXES, down)  7.73 us
    pallas_call x1, Pallas kernels, upward_call(): pl.pallas_call(upward_kernel, out_shape=(shape(3, 128, 128), shape(3, 16,...  6.1 us
  transfers between devices with their start and end apart: 4, of which 2 were waited for; matrix products, arithmetic and copies ran while one was open for 3% of the time, Pallas kernels for 20%

profile of v3, /device:TPU:96, one launch (start us, length us, event | category | flops | bytes accessed | tf_op | source)
XLA Modules:
  0.0 212.3 jit_solution(10636468896117374539)
XLA Ops:
  6.5 0.0 all-gather.2.cloned.1.call-start
  6.5 0.1 pad.4.clone
  6.6 1.4 add_add_fusion
  8.0 0.0 all-gather.2.cloned.1.call-update
  8.0 1.0 copy.20
  9.0 0.0 copy-start.1
  9.0 0.8 copy-done.1
  9.9 0.0 copy-start.6
  9.9 2.0 copy-done.6
  11.9 6.1 %upward.1 = (f32[3,128,128]{2,1,0:T(8,128)S(1)}, f32[3,16,128]{2,1,0:T(8,128)S(1)}, f32[3,128]{1,0:T(4,128)S(1)}) custom-call(s32[1]{0:T(128)} %bitcast.dev_ref, f32[3,128,128]{2,1,0:T(8,128)S(1)} %bitcast.30, f32[128,128]{1,0:T(8,128)S(1)} %bitcast.35, f32[2288,286]{1,0:T(8,128)S(1)} %bitcast.38), custom_call_target="tpu_custom_call" | custom-call | flops 8000000000 | bytes 3000000 | tf_op jit(solution)/shard_map/upward/pallas_call | solution.py:501
  18.0 0.0 copy-start.3
  18.0 55.6 %all-gather.2.cloned.1.call-done.asked_ref = s32[3072,128]{1,0:T(8,128)} async-done(((s32[24,128]{1,0:T(8,128)}), s32[3072,128]{1,0:T(8,128)}) %all-gather.2.cloned.1.call-update) | async-done | bytes 1572880 | tf_op jit(solution)/shard_map/all_gather | solution.py:608
  73.6 0.0 copy-start
  73.6 1.4 copy-done
  75.0 3.2 %pack.1 = f32[6144,128]{1,0:T(8,128)} custom-call(s32[1]{0:T(128)} %bitcast.dev_ref, s32[3072,128]{1,0:T(8,128)S(1)} %copy-done, f32[3,128,128]{2,1,0:T(8,128)S(1)} %get-tuple-element.10.lt_ref, f32[3,16,128]{2,1,0:T(8,128)S(1)} %get-tuple-element.11.pt_ref, f32[3,128]{1,0:T(4,128)S(1)} %get-tuple-element.12.lift_ref), custom_call_target="tpu_custom_call" | custom-call | flops 1000000000 | bytes 4000000 | tf_op jit(solution)/shard_map/pack/pallas_call | solution.py:518
  78.2 0.0 copy-start.16
  78.2 0.0 copy-start.17
  78.2 0.0 copy-done.3
  78.2 8.1 %all-to-all-start = ((f32[128,48,128]{2,1,0:T(8,128)}), f32[128,48,128]{2,1,0:T(8,128)S(1)}, u32[]{:S(2)}, u32[]{:S(2)}) async-start(f32[128,48,128]{2,1,0:T(8,128)} %bitcast.10), calls=%async_computation | async-start | bytes 6291456 | tf_op jit(solution)/shard_map/all_to_all | solution.py:620
  86.3 1.4 pad_maximum_fusion
  87.7 2.0 collective-permute-start
  89.7 7.7 %collective-permute-start.1 = (f32[4,32,128]{2,1,0:T(8,128)}, f32[4,32,128]{2,1,0:T(8,128)}, u32[]{:S(2)}, u32[]{:S(2)}) collective-permute-start(f32[4,32,128]{2,1,0:T(8,128)} %get-tuple-element.15), channel_id=1, source_target_pairs={{1,0},{2,1},{3,2},{4,3},{5,4},{6,5},{7,6},{8,7},{9,8},{10,9},{11,1... | collective-permute-start | bytes 196616 | tf_op jit(solution)/shard_map/ppermute | solution.py:616
  97.4 0.0 copy-done.16
  97.5 0.7 copy.16
  98.1 0.8 reshape.34.lists_ref
  99.0 0.0 copy-done.17
  99.0 0.7 copy.17
  99.7 0.8 reshape.35.class_ref
  100.5 25.9 %collective-permute-done.before_ref = f32[4,32,128]{2,1,0:T(8,128)} collective-permute-done((f32[4,32,128]{2,1,0:T(8,128)}, f32[4,32,128]{2,1,0:T(8,128)}, u32[]{:S(2)}, u32[]{:S(2)}) %collective-permute-start) | collective-permute-done | bytes 65568 | tf_op jit(solution)/shard_map/ppermute | solution.py:615
  126.3 0.0 collective-permute-done.1.after_ref
  126.3 0.0 copy-start.2
  126.3 0.8 copy-done.2
  127.2 0.0 copy-start.10
  127.2 0.7 copy-done.10
  127.9 0.0 copy-start.11
  127.9 0.7 copy-done.11
  128.6 36.7 %near.1.near_ref = f32[128,128]{1,0:T(8,128)S(1)} custom-call(s32[1]{0:T(128)} %bitcast.dev_ref, s32[27,128]{1,0:T(8,128)S(1)} %bitcast.42, s32[27,128]{1,0:T(8,128)S(1)} %bitcast.43, f32[3,128,128]{2,1,0:T(8,128)S(1)} %bitcast.32, f32[128,128]{1,0:T(8,128)S(1)} %bitcast.36, f32[4,32,128]{2,1,0:T(8,128)} %collective-permute-done.before_ref, ...), custom_call_target="tpu_custom_call" | custom-call | flops 30000001024 | bytes 1000000 | tf_op jit(solution)/shard_map/near/pallas_call | solution.py:530
  165.4 0.0 copy-start.14
  165.4 0.6 copy-done.14
  166.0 0.0 all-to-all-done
  166.0 0.0 copy-start.4
  166.0 0.7 copy-done.4
  166.7 0.0 copy-start.5
  166.7 3.0 %copy-done.5 = f32[16,286,286]{2,0,1:T(8,128)S(1)} copy-done((f32[16,286,286]{2,0,1:T(8,128)S(1)}, f32[16,286,286]{2,0,1:T(8,128)}, u32[]{:S(2)}) %copy-start.5) | copy-done | bytes 5234968
  169.7 0.0 copy-start.7
  169.7 2.0 copy-done.7
  171.7 0.0 copy-start.8
  171.7 0.9 copy-done.8
  172.6 0.0 copy-start.9
  172.6 0.9 copy-done.9
  173.5 0.0 copy-start.12
  173.5 0.7 copy-done.12
  174.2 0.0 copy-start.13
  174.2 0.7 copy-done.13
  175.0 0.0 copy-start.15
  175.0 0.8 copy-done.15
  175.8 29.7 %far.1 = f32[128,128]{1,0:T(8,128)} custom-call(s32[1]{0:T(128)} %bitcast.dev_ref, s32[224]{0:T(256)S(1)} %reshape.34.lists_ref, s32[224]{0:T(256)S(1)} %reshape.35.class_ref, s32[189,128]{1,0:T(8,128)S(1)} %bitcast.40, s32[189,128]{1,0:T(8,128)S(1)} %bitcast.41, s32[16,189]{1,0:T(8,128)S(1)} %copy-done.12, s32[16,189]{1,0:T(8,128)S(1)} %copy-done.13, ...), custom_call_target="tpu_custom_call" | custom-call | flops 20000000000 | bytes 20000000 | tf_op jit(solution)/shard_map/far/pallas_call | solution.py:555
  (1 shorter events, 0.0 us)
Async XLA Ops:
  6.5 67.1 %all-gather.2.cloned.1.call-start = ((), (), s32[]{:S(2)}) async-start(), calls=%async_computation.1 | async-start | bytes 1585152 | tf_op jit(solution)/shard_map/all_gather | solution.py:608
  9.0 0.8 copy-start.1
  9.9 2.0 copy-start.6
  18.0 60.3 %copy-start.3 = (f32[3,16,128]{2,1,0:T(8,128)}, f32[3,16,128]{2,1,0:T(8,128)S(1)}, u32[]{:S(2)}) copy-start(f32[3,16,128]{2,1,0:T(8,128)S(1)} %get-tuple-element.11.pt_ref) | copy-start | bytes 73732
  73.6 1.4 copy-start
  78.2 19.2 %copy-start.16 = (s32[32,7]{0,1:T(8,128)S(1)}, s32[32,7]{0,1:T(8,128)}, u32[]{:S(2)}) copy-start(s32[32,7]{0,1:T(8,128)} %param.25) | copy-start | bytes 2692
  78.2 20.8 %copy-start.17 = (s32[32,7]{0,1:T(8,128)S(1)}, s32[32,7]{0,1:T(8,128)}, u32[]{:S(2)}) copy-start(s32[32,7]{0,1:T(8,128)} %param.26) | copy-start | bytes 2692
  78.2 87.8 %all-to-all-start = ((f32[128,48,128]{2,1,0:T(8,128)}), f32[128,48,128]{2,1,0:T(8,128)S(1)}, u32[]{:S(2)}, u32[]{:S(2)}) async-start(f32[128,48,128]{2,1,0:T(8,128)} %bitcast.10), calls=%async_computation | async-start | bytes 6291456 | tf_op jit(solution)/shard_map/all_to_all | solution.py:620
  87.7 38.7 %collective-permute-start = (f32[4,32,128]{2,1,0:T(8,128)}, f32[4,32,128]{2,1,0:T(8,128)}, u32[]{:S(2)}, u32[]{:S(2)}) collective-permute-start(f32[4,32,128]{2,1,0:T(8,128)} %get-tuple-element.16), channel_id=1, source_target_pairs={{0,1},{1,2},{2,3},{3,4},{4,5},{5,6},{6,7},{7,8},{8,9},{9,10},{10,1... | collective-permute-start | bytes 196616 | tf_op jit(solution)/shard_map/ppermute | solution.py:615
  89.7 36.6 %collective-permute-start.1 = (f32[4,32,128]{2,1,0:T(8,128)}, f32[4,32,128]{2,1,0:T(8,128)}, u32[]{:S(2)}, u32[]{:S(2)}) collective-permute-start(f32[4,32,128]{2,1,0:T(8,128)} %get-tuple-element.15), channel_id=1, source_target_pairs={{1,0},{2,1},{3,2},{4,3},{5,4},{6,5},{7,6},{8,7},{9,8},{10,9},{11,1... | collective-permute-start | bytes 196616 | tf_op jit(solution)/shard_map/ppermute | solution.py:616
  126.3 0.8 copy-start.2
  127.2 0.7 copy-start.10
  127.9 0.7 copy-start.11
  165.4 0.6 copy-start.14
  166.0 0.7 copy-start.4
  166.7 3.0 %copy-start.5 = (f32[16,286,286]{2,0,1:T(8,128)S(1)}, f32[16,286,286]{2,0,1:T(8,128)}, u32[]{:S(2)}) copy-start(f32[16,286,286]{2,0,1:T(8,128)} %param.29) | copy-start | bytes 15704836
  169.7 2.0 copy-start.7
  171.7 0.9 copy-start.8
  172.6 0.9 copy-start.9
  173.5 0.7 copy-start.12
  174.2 0.7 copy-start.13
  175.0 0.8 copy-start.15
Sparse Core Ops, SparseCore 0:
  10.2 63.3 all-gather.1

commit v4 on v3

--- a/solution.py
+++ b/solution.py
@@ -14,7 +14,6 @@
 CAP_L = 16
 CAP_P = 4
 ROWS = 48
-PLAN = 24
 TARGETS = 160
 GROUP = 64
 NOBODY = LEAF + 2 * RIM
@@ -24,6 +23,7 @@
 BF16 = jnp.bfloat16
 VMEM = pl.BlockSpec(memory_space=pltpu.VMEM)
 SMEM = pl.BlockSpec(memory_space=pltpu.SMEM)
+HBM = pl.BlockSpec(memory_space=pl.ANY)
 
 
 def exponents(order):
@@ -65,11 +65,19 @@
     return apply_parts(operator, *split(columns))
 
 
-def cut(source, chunks):
-    chunks[0] = source[:, 0:128]
-    chunks[1] = source[:, 128:256]
+def fetches(source, chunks, tail, sems, first):
+    return [
+        pltpu.make_async_copy(source.at[:, 0:128], chunks.at[0], sems.at[first]),
+        pltpu.make_async_copy(source.at[:, 128:256], chunks.at[1], sems.at[first + 1]),
+        pltpu.make_async_copy(source.at[:, 256:COEF], tail, sems.at[first + 2]),
+    ]
+
+
+def arrive(copies, chunks, tail):
     chunks[2] = jnp.zeros(chunks.shape[1:], F32)
-    chunks[2, :, 0 : COEF - 256] = source[:, 256:COEF]
+    for copy in copies:
+        copy.wait()
+    chunks[2, :, 0 : COEF - 256] = tail[...]
 
 
 def operator_at(chunks, number, count):
@@ -77,8 +85,11 @@
     return jnp.concatenate([chunks[h, rows, :] for h in range(3)], axis=1)
 
 
-def upward_kernel(dev_ref, pos_ref, chg_ref, stored_up, lt_ref, pt_ref, lift_ref, moments, column,
-                  up_ref):
+def upward_kernel(dev_ref, asked_ref, pos_ref, chg_ref, up_hbm, lt_ref, pt_ref, out_ref, moments,
+                  column, up_ref, up_tail, sems):
+    copies = fetches(up_hbm, up_ref, up_tail, sems, 0)
+    for copy in copies:
+        copy.start()
     x, y, z = [2.0 * pos_ref[d].T for d in range(3)]
     with_x = chg_ref[...].T
     z_powers = [None, z]
@@ -99,7 +110,7 @@
     for h in range(3):
         lt_ref[h] = moments[128 * h : 128 * h + 128, :].T
     column[...] = jnp.zeros_like(column)
-    cut(stored_up, up_ref)
+    arrive(copies, up_ref, up_tail)
     lane = lax.broadcasted_iota(jnp.int32, (384, 128), 1)
     leaves = moments[...]
     total = jnp.zeros((COEF, 128), F32)
@@ -130,10 +141,8 @@
     )
     column[0:COEF, :] = total + turn(total, 64)
     for h in range(3):
-        lift_ref[h : h + 1, :] = column[128 * h : 128 * h + 128, :].T[0:1, :]
-
-
-def pack_kernel(dev_ref, asked_ref, lt_ref, pt_ref, lift_ref, out_ref):
+        lift = column[128 * h : 128 * h + 128, :].T[0:1, :]
+        out_ref[pl.ds(45 + h, 128, stride=ROWS), :] = jnp.broadcast_to(lift, (128, 128))
     lane = lax.broadcasted_iota(jnp.int32, (128, 128), 1)
     leaf_rows = jnp.concatenate([lt_ref[h] for h in range(3)], axis=1)
     parent_rows = jnp.concatenate([pt_ref[h] for h in range(3)], axis=1)
@@ -144,10 +153,7 @@
         tail = jnp.zeros((128, 128), F32)
         for p in range(4):
             j = 4 * q + p
-            asked = asked_ref[pl.ds(j, 128, stride=PLAN), :]
-            asked = jnp.where(lane == dev_ref[0], asked.astype(F32), 0.0)
-            asked = jnp.sum(asked, axis=1, keepdims=True)
-            chosen = jnp.where(asked == lane.astype(F32), 1.0, 0.0).astype(BF16)
+            chosen = jnp.where(asked_ref[:, j : j + 1] == lane, 1.0, 0.0).astype(BF16)
             chosen = jnp.concatenate([chosen, chosen], axis=1)
             rows = nn(chosen, leaf_rows if q < 4 else parent_rows)
             out_ref[pl.ds(2 * j, 128, stride=ROWS), :] = rows[:, 0:128]
@@ -155,8 +161,6 @@
             part = rows[:, 256:384]
             tail = tail + (pltpu.roll(part, 32 * p, 1) if p else part)
         out_ref[pl.ds(40 + q, 128, stride=ROWS), :] = tail
-    for h in range(3):
-        out_ref[pl.ds(45 + h, 128, stride=ROWS), :] = jnp.broadcast_to(lift_ref[h : h + 1, :], (128, 128))
 
 
 def near_kernel(dev_ref, leaves_ref, offsets_ref, pos_ref, chg_ref, before_ref, after_ref, out_ref,
@@ -316,9 +320,15 @@
 
 
 def far_kernel(dev_ref, lists_ref, class_ref, leaf_ref, leaf_class_ref, parent_ref, parent_class_ref,
-               lt_ref, pt_ref, arrived_ref, pos_ref, near_ref, stored_down, stored_far, out_ref,
+               lt_ref, pt_ref, pos_ref, near_ref, arrived_hbm, down_hbm, far_hbm, out_ref,
                src, src_parent, even, odd, even_parent, grouped, code_scr, low_scr, turned, column, loc,
-               result, down_ref, far_ref):
+               result, arrived_ref, down_ref, down_tail, far_ref, far_tail, sems):
+    arrival = pltpu.make_async_copy(arrived_hbm, arrived_ref, sems.at[6])
+    arrival.start()
+    far_copies = fetches(far_hbm, far_ref, far_tail, sems, 0)
+    down_copies = fetches(down_hbm, down_ref, down_tail, sems, 3)
+    for copy in far_copies + down_copies:
+        copy.start()
     lane = lax.broadcasted_iota(jnp.int32, (128, 128), 1)
 
     def count(first, capacity, table_ref):
@@ -371,6 +381,7 @@
     count(128, CAP_P, even_parent)
     count(0, CAP_L, even)
     place(src, 0, [lt_ref[h] for h in range(3)])
+    arrival.wait()
     for c in range(CAP_L):
         place(
             src,
@@ -409,7 +420,7 @@
 
     lax.fori_loop(0, 4, two_blocks, 0)
 
-    cut(stored_far, far_ref)
+    arrive(far_copies, far_ref, far_tail)
     column[...] = jnp.zeros_like(column)
     loc[...] = jnp.zeros_like(loc)
     tall = lax.broadcasted_iota(jnp.int32, (384, 128), 1)
@@ -443,7 +454,7 @@
             )
     upper_total = upper_total + turn(upper_total, 32)
     upper_total = upper_total + turn(upper_total, 64)
-    cut(stored_down, down_ref)
+    arrive(down_copies, down_ref, down_tail)
     column[0:COEF, :] = upper_total
     coarse = jnp.broadcast_to(column[:, 16:17], (384, 128))
     first = lax.rem(2 * dev_ref[0], 8)
@@ -497,33 +508,23 @@
     return pltpu.CompilerParams(vmem_limit_bytes=mib * 1024 * 1024)
 
 
-def upward_call(dev, pos, chg, up_shift):
+def upward_call(dev, asked, pos, chg, up_shift):
     return pl.pallas_call(
         upward_kernel,
-        out_shape=(shape(3, 128, 128), shape(3, 16, 128), shape(3, 128)),
-        in_specs=[SMEM] + [VMEM] * 3,
+        out_shape=(shape(3, 128, 128), shape(3, 16, 128), shape(128 * ROWS, 128)),
+        in_specs=[SMEM] + [VMEM] * 3 + [HBM],
         out_specs=(VMEM, VMEM, VMEM),
         scratch_shapes=[
             pltpu.VMEM((384, 128), F32),
             pltpu.VMEM((384, 128), F32),
             pltpu.VMEM((3, 8 * COEF, 128), F32),
+            pltpu.VMEM((8 * COEF, COEF - 256), F32),
+            pltpu.SemaphoreType.DMA((3,)),
         ],
-        compiler_params=limits(16),
+        compiler_params=limits(60),
         cost_estimate=cost(8 * 10**9, 3 * 10**6),
         name="upward",
-    )(dev, pos, chg, up_shift)
-
-
-def pack_call(dev, asked, lt, pt, lift):
-    return pl.pallas_call(
-        pack_kernel,
-        out_shape=shape(128 * ROWS, 128),
-        in_specs=[SMEM] + [VMEM] * 4,
-        out_specs=VMEM,
-        compiler_params=limits(24),
-        cost_estimate=cost(10**9, 4 * 10**6),
-        name="pack",
-    )(dev, asked, lt, pt, lift)
+    )(dev, asked, pos, chg, up_shift)
 
 
 def near_call(dev, near_leaves, near_offsets, pos, chg, before, after):
@@ -544,18 +545,18 @@
             pltpu.SMEM((40, 128), jnp.int32),
             pltpu.SemaphoreType.DMA(()),
         ],
-        compiler_params=limits(24),
+        compiler_params=limits(60),
         cost_estimate=cost(30 * 10**9, 10**6),
         name="near",
     )(dev, near_leaves, near_offsets, pos, chg, before, after)
 
 
-def far_call(dev, lists, classes, leaves, leaf_class, parents, parent_class, lt, pt, arrived, pos, near,
+def far_call(dev, lists, classes, leaves, leaf_class, parents, parent_class, lt, pt, pos, near, arrived,
              down_shift, far_shift):
     return pl.pallas_call(
         far_kernel,
         out_shape=shape(128, 128),
-        in_specs=[SMEM] * 3 + [VMEM] * 11,
+        in_specs=[SMEM] * 3 + [VMEM] * 8 + [HBM] * 3,
         out_specs=VMEM,
         scratch_shapes=[
             pltpu.VMEM((2176, 640), BF16),
@@ -570,13 +571,17 @@
             pltpu.VMEM((384, 128), F32),
             pltpu.VMEM((384, 128), F32),
             pltpu.VMEM((128, 128), F32),
+            pltpu.VMEM((128 * ROWS, 128), F32),
             pltpu.VMEM((3, 8 * COEF, 128), F32),
+            pltpu.VMEM((8 * COEF, COEF - 256), F32),
             pltpu.VMEM((3, 16 * COEF, 128), F32),
+            pltpu.VMEM((16 * COEF, COEF - 256), F32),
+            pltpu.SemaphoreType.DMA((7,)),
         ],
-        compiler_params=limits(40),
+        compiler_params=limits(60),
         cost_estimate=cost(20 * 10**9, 20 * 10**6),
         name="far",
-    )(dev, lists, classes, leaves, leaf_class, parents, parent_class, lt, pt, arrived, pos, near,
+    )(dev, lists, classes, leaves, leaf_class, parents, parent_class, lt, pt, pos, near, arrived,
       down_shift, far_shift)
 
 
@@ -603,26 +608,29 @@
 ):
     device = lax.axis_index(AXES)
     dev = device.reshape(1).astype(jnp.int32)
-    filler = jnp.full((PLAN - CAP_L - CAP_P, 128), -1, jnp.int32)
-    plans = jnp.concatenate([leaf_plan[0].T, parent_plan[0].T, filler], 0)
-    asked = lax.all_gather(plans, AXES, axis=0, tiled=True)
+    plans = jnp.concatenate([leaf_plan[0], parent_plan[0]], 1)
+    asked = lax.all_to_all(plans, AXES, split_axis=0, concat_axis=0, tiled=True)
     pos = positions.reshape(3, LEAF, 128)
     chg = charges.reshape(LEAF, 128)
-    own = jnp.concatenate([pos, chg[None]], 0)
+    rims = [
+        jnp.concatenate([pos[:, rows], chg[None, rows]], 0)
+        for rows in (slice(LEAF - RIM, LEAF), slice(0, RIM))
+    ]
     size = lax.axis_size(AXES)
     up = [(i, i + 1) for i in range(size - 1)]
     down = [(j, i) for i, j in up]
-    before = lax.ppermute(own[:, LEAF - RIM :], AXES, up)
-    after = lax.ppermute(own[:, :RIM], AXES, down)
-    lt, pt, lift = upward_call(dev, pos, chg, by_rows(up_shift))
-    outgoing = pack_call(dev, asked, lt, pt, lift).reshape(LEAF, ROWS, 128)
+    before = lax.ppermute(rims[0], AXES, up)
+    after = lax.ppermute(rims[1], AXES, down)
+    before, after, asked = lax.optimization_barrier((before, after, asked))
+    lt, pt, outgoing = upward_call(dev, asked, pos, chg, by_rows(up_shift))
+    outgoing = outgoing.reshape(LEAF, ROWS, 128)
     near_leaves, outgoing = lax.optimization_barrier((near_leaves, outgoing))
     arrived = lax.all_to_all(outgoing, AXES, split_axis=0, concat_axis=0, tiled=True)
     arrived = arrived.reshape(LEAF * ROWS, 128)
     near = near_call(dev, near_leaves.T, near_offsets.T, pos, chg, before, after)
     potential = far_call(
         dev, coarse_lists.reshape(-1), coarse_class.reshape(-1), far_leaves.T, far_leaf_class.T,
-        far_parents, far_parent_class, lt, pt, arrived, pos, near,
+        far_parents, far_parent_class, lt, pt, pos, near, arrived,
         by_rows(down_shift), by_rows(far_shift),
     )
     return potential.reshape(-1)

time: 215 us -> 121 us (0.56)
  the two profiles are of different devices: /device:TPU:96 before, /device:TPU:1 now
where the time goes in v4:
time: 121 us; the launch traced here: 120 us
  Pallas kernels  78.1 us (65%)
  starting transfers between devices  21.5 us (18%)
  waiting for transfers between devices  13.1 us (11%)
  local copies, waits for them, and re-layouts  6.32 us (5%)
    pallas_call x1, Pallas kernels, near_call(): pl.pallas_call(near_kernel, out_shape=shape(128, 128), in_specs=[SMEM] +...  36.8 us
    pallas_call x1, Pallas kernels, far_call(): pl.pallas_call(far_kernel, out_shape=shape(128, 128), in_specs=[SMEM] * 3...  31.3 us
    all_to_all x1, starting transfers between devices, per_device(): asked = lax.all_to_all(plans, AXES, split_axis=0, concat_axis=0, tiled=True)  10.5 us
    pallas_call x1, Pallas kernels, upward_call(): pl.pallas_call(upward_kernel, out_shape=(shape(3, 128, 128), shape(3, 16,...  9.99 us
    all_to_all x1, waiting for transfers between devices, per_device(): asked = lax.all_to_all(plans, AXES, split_axis=0, concat_axis=0, tiled=True)  9.53 us
    ppermute x1, starting transfers between devices, per_device(): before = lax.ppermute(rims[0], AXES, up)  4.59 us
    all_to_all x1, starting transfers between devices, per_device(): lax.all_to_all(outgoing, AXES, split_axis=0, concat_axis=0, tiled=True)  4.4 us
    all_to_all x1, waiting for transfers between devices, per_device(): lax.all_to_all(outgoing, AXES, split_axis=0, concat_axis=0, tiled=True)  3.58 us
  transfers between devices with their start and end apart: 4, of which 2 were waited for; matrix products, arithmetic and copies ran while one was open for 3% of the time, Pallas kernels for 31%

profile of v4, /device:TPU:1, one launch (start us, length us, event | category | flops | bytes accessed | tf_op | source)
XLA Modules:
  0.0 120.0 jit_solution(11318982099130129233)
XLA Ops:
  0.0 1.0 copy.27
  1.0 0.0 copy-start.1
  1.0 0.8 slice_bitcast_fusion
  1.8 4.6 %collective-permute-start = (f32[4,32,128]{2,1,0:T(8,128)S(1)}, f32[4,32,128]{2,1,0:T(8,128)S(1)}, u32[]{:S(2)}, u32[]{:S(2)}) collective-permute-start(f32[4,32,128]{2,1,0:T(8,128)S(1)} %pad_maximum_fusion), channel_id=1, source_target_pairs={{0,1},{1,2},{2,3},{3,4},{4,5},{5,6},{6,7},{7,8},{8,9},{9,10},{10,1... | collective-permute-start | bytes 196616 | tf_op jit(solution)/shard_map/ppermute | solution.py:622
  6.4 1.9 %collective-permute-start.1 = (f32[4,32,128]{2,1,0:T(8,128)S(1)}, f32[4,32,128]{2,1,0:T(8,128)S(1)}, u32[]{:S(2)}, u32[]{:S(2)}) collective-permute-start(f32[4,32,128]{2,1,0:T(8,128)S(1)} %pad_maximum_fusion.1), channel_id=1, source_target_pairs={{1,0},{2,1},{3,2},{4,3},{5,4},{6,5},{7,6},{8,7},{9,8},{10,9},{11,1... | collective-permute-start | bytes 196616 | tf_op jit(solution)/shard_map/ppermute | solution.py:623
  8.3 0.7 pad_add_fusion
  9.1 0.7 copy.24
  9.8 10.5 %all-to-all-start = ((s32[128,1,20]{2,1,0:T(1,128)}), s32[128,1,20]{2,1,0:T(1,128)S(1)}, u32[]{:S(2)}, u32[]{:S(2)}) async-start(s32[128,1,20]{2,1,0:T(1,128)} %bitcast.7), calls=%async_computation | async-start | bytes 131072 | tf_op jit(solution)/shard_map/all_to_all | solution.py:612
  20.4 9.5 %all-to-all-done = s32[128,1,20]{2,1,0:T(1,128)S(1)} async-done(((s32[128,1,20]{2,1,0:T(1,128)}), s32[128,1,20]{2,1,0:T(1,128)S(1)}, u32[]{:S(2)}, u32[]{:S(2)}) %all-to-all-start) | async-done | bytes 10272 | tf_op jit(solution)/shard_map/all_to_all | solution.py:612
  29.9 0.0 copy-start.2
  29.9 0.0 collective-permute-done.before_ref
  29.9 0.0 copy-start.5
  29.9 0.0 collective-permute-done.1.after_ref
  29.9 0.0 copy-start.6
  29.9 0.0 copy-done.1
  29.9 0.6 copy-done.2
  30.5 10.0 %upward.1 = (f32[3,128,128]{2,1,0:T(8,128)}, f32[3,16,128]{2,1,0:T(8,128)}, f32[6144,128]{1,0:T(8,128)}) custom-call(s32[1]{0:T(128)} %bitcast.dev_ref, s32[128,20]{1,0:T(8,128)} %bitcast.37, f32[3,128,128]{2,1,0:T(8,128)} %bitcast.33, f32[128,128]{1,0:T(8,128)} %bitcast.38, f32[2288,286]{1,0:T(8,128)} %bitcast.43), custom_call_target="tpu_custom_call" | custom-call | flops 8000000000 | bytes 3000000 | tf_op jit(solution)/shard_map/upward/pallas_call | solution.py:512
  40.5 0.0 copy-done.5
  40.5 0.0 copy-done.6
  40.6 0.0 copy-start.3
  40.6 0.0 copy-start.4
  40.6 4.4 %all-to-all-start.1 = ((f32[128,48,128]{2,1,0:T(8,128)}), f32[128,48,128]{2,1,0:T(8,128)S(1)}, u32[]{:S(2)}, u32[]{:S(2)}) async-start(f32[128,48,128]{2,1,0:T(8,128)} %bitcast.31), calls=%async_computation.1 | async-start | bytes 6291456 | tf_op jit(solution)/shard_map/all_to_all | solution.py:628
  45.0 0.0 copy-done.3
  45.0 0.1 copy.22
  45.1 0.7 reshape.56.lists_ref
  45.8 0.0 copy-done.4
  45.8 0.1 copy.23
  45.9 0.7 reshape.57.class_ref
  46.5 36.8 %near.1.near_ref = f32[128,128]{1,0:T(8,128)} custom-call(s32[1]{0:T(128)} %bitcast.dev_ref, s32[27,128]{1,0:T(8,128)} %bitcast.47, s32[27,128]{1,0:T(8,128)} %bitcast.48, f32[3,128,128]{2,1,0:T(8,128)} %bitcast.34, f32[128,128]{1,0:T(8,128)} %bitcast.39, f32[4,32,128]{2,1,0:T(8,128)} %copy-done.5, f32[4,32,128]{2,1,0:T(8,128)} %copy-done.6), custom_call_target="tpu_custom_call" | custom-call | flops 30000001024 | bytes 1000000 | tf_op jit(solution)/shard_map/near/pallas_call | solution.py:531
  83.3 3.6 %all-to-all-done.1 = f32[128,48,128]{2,1,0:T(8,128)S(1)} async-done(((f32[128,48,128]{2,1,0:T(8,128)}), f32[128,48,128]{2,1,0:T(8,128)S(1)}, u32[]{:S(2)}, u32[]{:S(2)}) %all-to-all-start.1) | async-done | bytes 3145760 | tf_op jit(solution)/shard_map/all_to_all | solution.py:628
  86.9 0.0 copy-start
  86.9 1.6 %copy-done = f32[128,48,128]{2,1,0:T(8,128)} copy-done((f32[128,48,128]{2,1,0:T(8,128)}, f32[128,48,128]{2,1,0:T(8,128)S(1)}, u32[]{:S(2)}) %copy-start) | copy-done | bytes 3145752
  88.5 31.3 %far.1 = f32[128,128]{1,0:T(8,128)} custom-call(s32[1]{0:T(128)} %bitcast.dev_ref, s32[224]{0:T(256)} %reshape.56.lists_ref, s32[224]{0:T(256)} %reshape.57.class_ref, s32[189,128]{1,0:T(8,128)} %bitcast.45, s32[189,128]{1,0:T(8,128)} %bitcast.46, s32[16,189]{1,0:T(8,128)} %parent_ref.1, s32[16,189]{1,0:T(8,128)} %parent_class_ref.1, ...), custom_call_target="tpu_custom_call" | custom-call | flops 20000000000 | bytes 20000000 | tf_op jit(solution)/shard_map/far/pallas_call | solution.py:556
  (3 shorter events, 0.0 us)
Async XLA Ops:
  1.0 29.0 %copy-start.1 = (f32[1,3,128,128]{3,2,1,0:T(8,128)}, f32[1,3,128,128]{3,2,1,0:T(8,128)S(1)}, u32[]{:S(2)}) copy-start(f32[1,3,128,128]{3,2,1,0:T(8,128)S(1)} %copy.27) | copy-start | bytes 589828
  1.8 28.1 %collective-permute-start = (f32[4,32,128]{2,1,0:T(8,128)S(1)}, f32[4,32,128]{2,1,0:T(8,128)S(1)}, u32[]{:S(2)}, u32[]{:S(2)}) collective-permute-start(f32[4,32,128]{2,1,0:T(8,128)S(1)} %pad_maximum_fusion), channel_id=1, source_target_pairs={{0,1},{1,2},{2,3},{3,4},{4,5},{5,6},{6,7},{7,8},{8,9},{9,10},{10,1... | collective-permute-start | bytes 196616 | tf_op jit(solution)/shard_map/ppermute | solution.py:622
  6.4 23.5 %collective-permute-start.1 = (f32[4,32,128]{2,1,0:T(8,128)S(1)}, f32[4,32,128]{2,1,0:T(8,128)S(1)}, u32[]{:S(2)}, u32[]{:S(2)}) collective-permute-start(f32[4,32,128]{2,1,0:T(8,128)S(1)} %pad_maximum_fusion.1), channel_id=1, source_target_pairs={{1,0},{2,1},{3,2},{4,3},{5,4},{6,5},{7,6},{8,7},{9,8},{10,9},{11,1... | collective-permute-start | bytes 196616 | tf_op jit(solution)/shard_map/ppermute | solution.py:623
  9.8 20.1 %all-to-all-start = ((s32[128,1,20]{2,1,0:T(1,128)}), s32[128,1,20]{2,1,0:T(1,128)S(1)}, u32[]{:S(2)}, u32[]{:S(2)}) async-start(s32[128,1,20]{2,1,0:T(1,128)} %bitcast.7), calls=%async_computation | async-start | bytes 131072 | tf_op jit(solution)/shard_map/all_to_all | solution.py:612
  29.9 0.6 copy-start.2
  29.9 10.6 %copy-start.5 = (f32[4,32,128]{2,1,0:T(8,128)}, f32[4,32,128]{2,1,0:T(8,128)S(1)}, u32[]{:S(2)}) copy-start(f32[4,32,128]{2,1,0:T(8,128)S(1)} %collective-permute-done.before_ref) | copy-start | bytes 196612
  29.9 10.6 %copy-start.6 = (f32[4,32,128]{2,1,0:T(8,128)}, f32[4,32,128]{2,1,0:T(8,128)S(1)}, u32[]{:S(2)}) copy-start(f32[4,32,128]{2,1,0:T(8,128)S(1)} %collective-permute-done.1.after_ref) | copy-start | bytes 196612
  40.6 4.4 %copy-start.3 = (s32[32,7]{0,1:T(8,128)S(1)}, s32[32,7]{0,1:T(8,128)}, u32[]{:S(2)}) copy-start(s32[32,7]{0,1:T(8,128)} %param.25) | copy-start | bytes 2692
  40.6 5.2 %copy-start.4 = (s32[32,7]{0,1:T(8,128)S(1)}, s32[32,7]{0,1:T(8,128)}, u32[]{:S(2)}) copy-start(s32[32,7]{0,1:T(8,128)} %param.26) | copy-start | bytes 2692
  40.6 46.3 %all-to-all-start.1 = ((f32[128,48,128]{2,1,0:T(8,128)}), f32[128,48,128]{2,1,0:T(8,128)S(1)}, u32[]{:S(2)}, u32[]{:S(2)}) async-start(f32[128,48,128]{2,1,0:T(8,128)} %bitcast.31), calls=%async_computation.1 | async-start | bytes 6291456 | tf_op jit(solution)/shard_map/all_to_all | solution.py:628
  86.9 1.6 %copy-start = (f32[128,48,128]{2,1,0:T(8,128)}, f32[128,48,128]{2,1,0:T(8,128)S(1)}, u32[]{:S(2)}) copy-start(f32[128,48,128]{2,1,0:T(8,128)S(1)} %all-to-all-done.1) | copy-start | bytes 9437188

commit v5 on v3

--- a/solution.py
+++ b/solution.py
@@ -14,9 +14,9 @@
 CAP_L = 16
 CAP_P = 4
 ROWS = 48
-PLAN = 24
+PACK_MIB = 60
 TARGETS = 160
-GROUP = 64
+GROUP = 128
 NOBODY = LEAF + 2 * RIM
 SOFT = 0.05 * 0.05
 AXES = ("gx", "gy")
@@ -24,6 +24,7 @@
 BF16 = jnp.bfloat16
 VMEM = pl.BlockSpec(memory_space=pltpu.VMEM)
 SMEM = pl.BlockSpec(memory_space=pltpu.SMEM)
+HBM = pl.BlockSpec(memory_space=pl.ANY)
 
 
 def exponents(order):
@@ -72,13 +73,43 @@
     chunks[2, :, 0 : COEF - 256] = source[:, 256:COEF]
 
 
+def chunk_at(chunks, h, number, count):
+    return chunks[h, pl.ds(number, COEF, stride=count), :]
+
+
 def operator_at(chunks, number, count):
-    rows = pl.ds(number, COEF, stride=count)
-    return jnp.concatenate([chunks[h, rows, :] for h in range(3)], axis=1)
-
-
-def upward_kernel(dev_ref, pos_ref, chg_ref, stored_up, lt_ref, pt_ref, lift_ref, moments, column,
-                  up_ref):
+    return jnp.concatenate([chunk_at(chunks, h, number, count) for h in range(3)], axis=1)
+
+
+def eight_operators(chunks, numbers, count):
+    parts = [
+        jnp.concatenate([chunk_at(chunks, h, number, count) for h in range(2)], axis=1)
+        for number in numbers
+    ]
+    halves = []
+    for g in range(2):
+        half = chunk_at(chunks, 2, numbers[4 * g], count)
+        for p in range(1, 4):
+            half = half + pltpu.roll(chunk_at(chunks, 2, numbers[4 * g + p], count), 32 * p, 1)
+        halves.append(half)
+    return parts + [jnp.concatenate(halves, axis=1)]
+
+
+def eight_columns(columns):
+    return [c[0:256] for c in columns] + [jnp.concatenate([c[256:288] for c in columns], axis=0)]
+
+
+def apply_eight(chunks, columns, total):
+    operators = eight_operators(chunks, range(8), 8)
+    for operator, part in zip(operators, eight_columns(columns)):
+        total = total + apply_operator(operator, part)
+    return total
+
+
+def upward_kernel(dev_ref, pos_ref, chg_ref, up_hbm, lt_ref, pt_ref, lift_ref, moments, column, up_ref,
+                  stored_up, sem):
+    copy = pltpu.make_async_copy(up_hbm, stored_up, sem)
+    copy.start()
     x, y, z = [2.0 * pos_ref[d].T for d in range(3)]
     with_x = chg_ref[...].T
     z_powers = [None, z]
@@ -99,23 +130,20 @@
     for h in range(3):
         lt_ref[h] = moments[128 * h : 128 * h + 128, :].T
     column[...] = jnp.zeros_like(column)
+    copy.wait()
     cut(stored_up, up_ref)
     lane = lax.broadcasted_iota(jnp.int32, (384, 128), 1)
     leaves = moments[...]
     total = jnp.zeros((COEF, 128), F32)
-    for c in range(8):
-        total = total + apply_operator(
-            operator_at(up_ref, c, 8), jnp.where(lane % 8 == c, leaves, 0.0)
-        )
+    total = apply_eight(up_ref, [jnp.where(lane % 8 == c, leaves, 0.0) for c in range(8)], total)
     for left in (4, 2, 1):
         total = total + turn(total, left)
     column[0:COEF, :] = total
     parents = column[...]
     total = jnp.zeros((COEF, 128), F32)
-    for c in range(8):
-        total = total + apply_operator(
-            operator_at(up_ref, c, 8), jnp.where(lane % 64 == 8 * c, parents, 0.0)
-        )
+    total = apply_eight(
+        up_ref, [jnp.where(lane % 64 == 8 * c, parents, 0.0) for c in range(8)], total
+    )
     for h in range(3):
         moments[0:128, :] = column[128 * h : 128 * h + 128, :].T
         pt_ref[h] = moments[pl.ds(0, 16, stride=8), :]
@@ -133,7 +161,11 @@
         lift_ref[h : h + 1, :] = column[128 * h : 128 * h + 128, :].T[0:1, :]
 
 
-def pack_kernel(dev_ref, asked_ref, lt_ref, pt_ref, lift_ref, out_ref):
+def pack_kernel(asked_ref, lt_ref, pt_ref, lift_ref, out_ref):
+    for h in range(3):
+        out_ref[pl.ds(45 + h, 128, stride=ROWS), :] = jnp.broadcast_to(
+            lift_ref[h : h + 1, :], (128, 128)
+        )
     lane = lax.broadcasted_iota(jnp.int32, (128, 128), 1)
     leaf_rows = jnp.concatenate([lt_ref[h] for h in range(3)], axis=1)
     parent_rows = jnp.concatenate([pt_ref[h] for h in range(3)], axis=1)
@@ -144,10 +176,7 @@
         tail = jnp.zeros((128, 128), F32)
         for p in range(4):
             j = 4 * q + p
-            asked = asked_ref[pl.ds(j, 128, stride=PLAN), :]
-            asked = jnp.where(lane == dev_ref[0], asked.astype(F32), 0.0)
-            asked = jnp.sum(asked, axis=1, keepdims=True)
-            chosen = jnp.where(asked == lane.astype(F32), 1.0, 0.0).astype(BF16)
+            chosen = jnp.where(asked_ref[:, j : j + 1] == lane, 1.0, 0.0).astype(BF16)
             chosen = jnp.concatenate([chosen, chosen], axis=1)
             rows = nn(chosen, leaf_rows if q < 4 else parent_rows)
             out_ref[pl.ds(2 * j, 128, stride=ROWS), :] = rows[:, 0:128]
@@ -155,8 +184,6 @@
             part = rows[:, 256:384]
             tail = tail + (pltpu.roll(part, 32 * p, 1) if p else part)
         out_ref[pl.ds(40 + q, 128, stride=ROWS), :] = tail
-    for h in range(3):
-        out_ref[pl.ds(45 + h, 128, stride=ROWS), :] = jnp.broadcast_to(lift_ref[h : h + 1, :], (128, 128))
 
 
 def near_kernel(dev_ref, leaves_ref, offsets_ref, pos_ref, chg_ref, before_ref, after_ref, out_ref,
@@ -237,22 +264,22 @@
         spread[leaf] = nn(rows, three)
 
     def prepare(step, carry):
-        for u in range(16):
-            source(16 * step + u)
+        for u in range(48):
+            source(48 * step + u)
         return carry
 
-    lax.fori_loop(0, (LEAF + 2 * RIM) // 16, prepare, 0)
+    lax.fori_loop(0, (LEAF + 2 * RIM) // 48, prepare, 0)
     copy.wait()
 
     def own_leaf(step, carry):
-        for u in range(16):
-            leaf = 16 * step + u
+        for u in range(32):
+            leaf = 32 * step + u
             squared = separations(RIM + leaf, target(leaf, 13))
             terms = jnp.where(diagonal, 0.0, spread[RIM + leaf] * lax.rsqrt(squared))
             sums[leaf] = jnp.sum(terms.reshape(16, 8, 128), axis=0) * plan[38, leaf].astype(F32)
         return carry
 
-    lax.fori_loop(0, LEAF // 16, own_leaf, 0)
+    lax.fori_loop(0, LEAF // 32, own_leaf, 0)
 
     def advance(state):
         leaf, quad = state
@@ -316,9 +343,18 @@
 
 
 def far_kernel(dev_ref, lists_ref, class_ref, leaf_ref, leaf_class_ref, parent_ref, parent_class_ref,
-               lt_ref, pt_ref, arrived_ref, pos_ref, near_ref, stored_down, stored_far, out_ref,
+               lt_ref, pt_ref, pos_ref, near_ref, arrived_hbm, down_hbm, far_hbm, out_ref,
                src, src_parent, even, odd, even_parent, grouped, code_scr, low_scr, turned, column, loc,
-               result, down_ref, far_ref):
+               result, arrived_ref, down_ref, stored_down, far_ref, stored_far, sems):
+    arrival, far_copy, down_copy = [
+        pltpu.make_async_copy(origin, scratch, sems.at[i])
+        for i, (origin, scratch) in enumerate(
+            ((arrived_hbm, arrived_ref), (far_hbm, stored_far), (down_hbm, stored_down))
+        )
+    ]
+    arrival.start()
+    far_copy.start()
+    down_copy.start()
     lane = lax.broadcasted_iota(jnp.int32, (128, 128), 1)
 
     def count(first, capacity, table_ref):
@@ -371,6 +407,7 @@
     count(128, CAP_P, even_parent)
     count(0, CAP_L, even)
     place(src, 0, [lt_ref[h] for h in range(3)])
+    arrival.wait()
     for c in range(CAP_L):
         place(
             src,
@@ -409,31 +446,38 @@
 
     lax.fori_loop(0, 4, two_blocks, 0)
 
+    far_copy.wait()
     cut(stored_far, far_ref)
     column[...] = jnp.zeros_like(column)
     loc[...] = jnp.zeros_like(loc)
     tall = lax.broadcasted_iota(jnp.int32, (384, 128), 1)
     leaf_total = jnp.zeros((COEF, 128), F32)
     upper_total = jnp.zeros((COEF, 128), F32)
-    for q in range(4):
-        upper = jnp.concatenate(
-            [
-                jnp.concatenate(
-                    [grouped[h, pl.ds(2048 + 4 * q + p, 32, stride=16), :] for p in range(4)],
-                    axis=0,
-                ).T
-                for h in range(3)
-            ],
-            axis=0,
-        )
-        for p in range(4):
-            o = 4 * q + p
-            leaf = jnp.concatenate(
-                [grouped[h, pl.ds(o, 128, stride=16), :].T for h in range(3)], axis=0
+    for half in range(2):
+        numbers = range(8 * half, 8 * half + 8)
+        uppers = []
+        for q in (2 * half, 2 * half + 1):
+            upper = jnp.concatenate(
+                [
+                    jnp.concatenate(
+                        [grouped[h, pl.ds(2048 + 4 * q + p, 32, stride=16), :] for p in range(4)],
+                        axis=0,
+                    ).T
+                    for h in range(3)
+                ],
+                axis=0,
             )
-            operator_high, operator_low = split(operator_at(far_ref, o, 16))
+            uppers += [jnp.where(tall // 32 == p, upper, 0.0) for p in range(4)]
+        leaves = [
+            jnp.concatenate([grouped[h, pl.ds(o, 128, stride=16), :].T for h in range(3)], axis=0)
+            for o in numbers
+        ]
+        for operator, leaf, upper in zip(
+            eight_operators(far_ref, numbers, 16), eight_columns(leaves), eight_columns(uppers)
+        ):
+            operator_high, operator_low = split(operator)
             leaf_high, leaf_low = split(leaf)
-            upper_high, upper_low = split(jnp.where(tall // 32 == p, upper, 0.0))
+            upper_high, upper_low = split(upper)
             first = nn(operator_high, jnp.concatenate([leaf_high, leaf_low], axis=1))
             second = nn(operator_high, jnp.concatenate([upper_high, upper_low], axis=1))
             third = nn(operator_low, jnp.concatenate([leaf_high, upper_high], axis=1))
@@ -443,6 +487,7 @@
             )
     upper_total = upper_total + turn(upper_total, 32)
     upper_total = upper_total + turn(upper_total, 64)
+    down_copy.wait()
     cut(stored_down, down_ref)
     column[0:COEF, :] = upper_total
     coarse = jnp.broadcast_to(column[:, 16:17], (384, 128))
@@ -453,18 +498,21 @@
     )
     loc[0:COEF, :] = grand
     grand = loc[...]
-    for c in range(8):
-        upper_total = upper_total + apply_operator(
-            operator_at(down_ref, c, 8), jnp.where((tall % 8 == c) & (tall < 16), grand, 0.0)
-        )
+    upper_total = apply_eight(
+        down_ref,
+        [jnp.where((tall % 8 == c) & (tall < 16), grand, 0.0) for c in range(8)],
+        upper_total,
+    )
     column[0:COEF, :] = upper_total
     parents = split(jnp.where(tall < 16, column[...], 0.0))
     repeat = lax.broadcasted_iota(jnp.int32, (128, 128), 0) == lane // 8
     repeat = jnp.where(repeat, 1.0, 0.0).astype(BF16)
     parents = [nn(part, repeat) for part in parents]
-    for c in range(8):
-        high, low = [jnp.where(tall % 8 == c, part, 0.0).astype(BF16) for part in parents]
-        leaf_total = leaf_total + apply_parts(operator_at(down_ref, c, 8), high, low)
+    high, low = [
+        eight_columns([jnp.where(tall % 8 == c, part, 0.0) for c in range(8)]) for part in parents
+    ]
+    for operator, high_part, low_part in zip(eight_operators(down_ref, range(8), 8), high, low):
+        leaf_total = leaf_total + apply_parts(operator, high_part.astype(BF16), low_part.astype(BF16))
     loc[0:COEF, :] = leaf_total
     x_all, y_all, z_all = [2.0 * pos_ref[d].T for d in range(3)]
     for part in range(2):
@@ -501,29 +549,31 @@
     return pl.pallas_call(
         upward_kernel,
         out_shape=(shape(3, 128, 128), shape(3, 16, 128), shape(3, 128)),
-        in_specs=[SMEM] + [VMEM] * 3,
+        in_specs=[SMEM] + [VMEM] * 2 + [HBM],
         out_specs=(VMEM, VMEM, VMEM),
         scratch_shapes=[
             pltpu.VMEM((384, 128), F32),
             pltpu.VMEM((384, 128), F32),
             pltpu.VMEM((3, 8 * COEF, 128), F32),
+            pltpu.VMEM((8 * COEF, COEF), F32),
+            pltpu.SemaphoreType.DMA(()),
         ],
-        compiler_params=limits(16),
+        compiler_params=limits(60),
         cost_estimate=cost(8 * 10**9, 3 * 10**6),
         name="upward",
     )(dev, pos, chg, up_shift)
 
 
-def pack_call(dev, asked, lt, pt, lift):
+def pack_call(asked, lt, pt, lift):
     return pl.pallas_call(
         pack_kernel,
         out_shape=shape(128 * ROWS, 128),
-        in_specs=[SMEM] + [VMEM] * 4,
+        in_specs=[VMEM] * 4,
         out_specs=VMEM,
-        compiler_params=limits(24),
+        compiler_params=limits(PACK_MIB),
         cost_estimate=cost(10**9, 4 * 10**6),
         name="pack",
-    )(dev, asked, lt, pt, lift)
+    )(asked, lt, pt, lift)
 
 
 def near_call(dev, near_leaves, near_offsets, pos, chg, before, after):
@@ -544,18 +594,18 @@
             pltpu.SMEM((40, 128), jnp.int32),
             pltpu.SemaphoreType.DMA(()),
         ],
-        compiler_params=limits(24),
+        compiler_params=limits(60),
         cost_estimate=cost(30 * 10**9, 10**6),
         name="near",
     )(dev, near_leaves, near_offsets, pos, chg, before, after)
 
 
-def far_call(dev, lists, classes, leaves, leaf_class, parents, parent_class, lt, pt, arrived, pos, near,
+def far_call(dev, lists, classes, leaves, leaf_class, parents, parent_class, lt, pt, pos, near, arrived,
              down_shift, far_shift):
     return pl.pallas_call(
         far_kernel,
         out_shape=shape(128, 128),
-        in_specs=[SMEM] * 3 + [VMEM] * 11,
+        in_specs=[SMEM] * 3 + [VMEM] * 8 + [HBM] * 3,
         out_specs=VMEM,
         scratch_shapes=[
             pltpu.VMEM((2176, 640), BF16),
@@ -570,13 +620,17 @@
             pltpu.VMEM((384, 128), F32),
             pltpu.VMEM((384, 128), F32),
             pltpu.VMEM((128, 128), F32),
+            pltpu.VMEM((128 * ROWS, 128), F32),
             pltpu.VMEM((3, 8 * COEF, 128), F32),
+            pltpu.VMEM((8 * COEF, COEF), F32),
             pltpu.VMEM((3, 16 * COEF, 128), F32),
+            pltpu.VMEM((16 * COEF, COEF), F32),
+            pltpu.SemaphoreType.DMA((3,)),
         ],
-        compiler_params=limits(40),
+        compiler_params=limits(60),
         cost_estimate=cost(20 * 10**9, 20 * 10**6),
         name="far",
-    )(dev, lists, classes, leaves, leaf_class, parents, parent_class, lt, pt, arrived, pos, near,
+    )(dev, lists, classes, leaves, leaf_class, parents, parent_class, lt, pt, pos, near, arrived,
       down_shift, far_shift)
 
 
@@ -603,26 +657,30 @@
 ):
     device = lax.axis_index(AXES)
     dev = device.reshape(1).astype(jnp.int32)
-    filler = jnp.full((PLAN - CAP_L - CAP_P, 128), -1, jnp.int32)
-    plans = jnp.concatenate([leaf_plan[0].T, parent_plan[0].T, filler], 0)
-    asked = lax.all_gather(plans, AXES, axis=0, tiled=True)
+    plans = jnp.concatenate([leaf_plan[0], parent_plan[0]], 1)
+    asked = lax.all_to_all(plans, AXES, split_axis=0, concat_axis=0, tiled=True)
     pos = positions.reshape(3, LEAF, 128)
     chg = charges.reshape(LEAF, 128)
-    own = jnp.concatenate([pos, chg[None]], 0)
+    rims = [
+        jnp.concatenate([pos[:, rows], chg[None, rows]], 0)
+        for rows in (slice(LEAF - RIM, LEAF), slice(0, RIM))
+    ]
     size = lax.axis_size(AXES)
     up = [(i, i + 1) for i in range(size - 1)]
     down = [(j, i) for i, j in up]
-    before = lax.ppermute(own[:, LEAF - RIM :], AXES, up)
-    after = lax.ppermute(own[:, :RIM], AXES, down)
+    before = lax.ppermute(rims[0], AXES, up)
+    after = lax.ppermute(rims[1], AXES, down)
     lt, pt, lift = upward_call(dev, pos, chg, by_rows(up_shift))
-    outgoing = pack_call(dev, asked, lt, pt, lift).reshape(LEAF, ROWS, 128)
+    before, after, asked, lt = lax.optimization_barrier((before, after, asked, lt))
+    outgoing = pack_call(asked, lt, pt, lift)
+    outgoing = outgoing.reshape(LEAF, ROWS, 128)
     near_leaves, outgoing = lax.optimization_barrier((near_leaves, outgoing))
     arrived = lax.all_to_all(outgoing, AXES, split_axis=0, concat_axis=0, tiled=True)
     arrived = arrived.reshape(LEAF * ROWS, 128)
     near = near_call(dev, near_leaves.T, near_offsets.T, pos, chg, before, after)
     potential = far_call(
         dev, coarse_lists.reshape(-1), coarse_class.reshape(-1), far_leaves.T, far_leaf_class.T,
-        far_parents, far_parent_class, lt, pt, arrived, pos, near,
+        far_parents, far_parent_class, lt, pt, pos, near, arrived,
         by_rows(down_shift), by_rows(far_shift),
     )
     return potential.reshape(-1)

time: 215 us -> 116 us (0.54)
  the two profiles are of different devices: /device:TPU:96 before, /device:TPU:1 now
where the time goes in v5:
time: 116 us
  Pallas kernels  74.6 us (64%)
  starting transfers between devices  24.3 us (21%)
  waiting for transfers between devices  9.62 us (8%)
  local copies, waits for them, and re-layouts  6.28 us (5%)
    pallas_call x1, Pallas kernels, near_call(): pl.pallas_call(near_kernel, out_shape=shape(128, 128), in_specs=[SMEM] +...  33.4 us
    pallas_call x1, Pallas kernels, far_call(): pl.pallas_call(far_kernel, out_shape=shape(128, 128), in_specs=[SMEM] * 3...  30.3 us
    all_to_all x1, starting transfers between devices, per_device(): asked = lax.all_to_all(plans, AXES, split_axis=0, concat_axis=0, tiled=True)  10.5 us
    all_to_all x1, starting transfers between devices, per_device(): lax.all_to_all(outgoing, AXES, split_axis=0, concat_axis=0, tiled=True)  7.2 us
    all_to_all x1, waiting for transfers between devices, per_device(): lax.all_to_all(outgoing, AXES, split_axis=0, concat_axis=0, tiled=True)  7.04 us
    pallas_call x1, Pallas kernels, upward_call(): pl.pallas_call(upward_kernel, out_shape=(shape(3, 128, 128), shape(3, 16,...  6.93 us
    ppermute x1, starting transfers between devices, per_device(): before = lax.ppermute(rims[0], AXES, up)  4.59 us
    pallas_call x1, Pallas kernels, pack_call(): pl.pallas_call(pack_kernel, out_shape=shape(128 * ROWS, 128), in_specs=[V...  4.07 us
  transfers between devices with their start and end apart: 4, of which 2 were waited for; matrix products, arithmetic and copies ran while one was open for 3% of the time, Pallas kernels for 35%

profile of v5, /device:TPU:1, one launch (start us, length us, event | category | flops | bytes accessed | tf_op | source)
XLA Modules:
  0.0 115.8 jit_solution(7291177121670964417)
XLA Ops:
  0.0 1.0 copy.27
  1.0 0.0 copy-start.1
  1.0 0.8 slice_bitcast_fusion
  1.8 4.6 %collective-permute-start = (f32[4,32,128]{2,1,0:T(8,128)S(1)}, f32[4,32,128]{2,1,0:T(8,128)S(1)}, u32[]{:S(2)}, u32[]{:S(2)}) collective-permute-start(f32[4,32,128]{2,1,0:T(8,128)S(1)} %pad_maximum_fusion), channel_id=1, source_target_pairs={{0,1},{1,2},{2,3},{3,4},{4,5},{5,6},{6,7},{7,8},{8,9},{9,10},{10,1... | collective-permute-start | bytes 196616 | tf_op jit(solution)/shard_map/ppermute | solution.py:671
  6.4 1.9 %collective-permute-start.1 = (f32[4,32,128]{2,1,0:T(8,128)S(1)}, f32[4,32,128]{2,1,0:T(8,128)S(1)}, u32[]{:S(2)}, u32[]{:S(2)}) collective-permute-start(f32[4,32,128]{2,1,0:T(8,128)S(1)} %pad_maximum_fusion.1), channel_id=1, source_target_pairs={{1,0},{2,1},{3,2},{4,3},{5,4},{6,5},{7,6},{8,7},{9,8},{10,9},{11,1... | collective-permute-start | bytes 196616 | tf_op jit(solution)/shard_map/ppermute | solution.py:672
  8.3 0.7 pad_add_fusion
  9.1 0.7 copy.24
  9.8 10.5 %all-to-all-start = ((s32[128,1,20]{2,1,0:T(1,128)}), s32[128,1,20]{2,1,0:T(1,128)S(1)}, u32[]{:S(2)}, u32[]{:S(2)}) async-start(s32[128,1,20]{2,1,0:T(1,128)} %bitcast.7), calls=%async_computation | async-start | bytes 131072 | tf_op jit(solution)/shard_map/all_to_all | solution.py:661
  20.4 0.0 copy-done.1
  20.4 6.9 %upward.1 = (f32[3,128,128]{2,1,0:T(8,128)}, f32[3,16,128]{2,1,0:T(8,128)}, f32[3,128]{1,0:T(4,128)}) custom-call(s32[1]{0:T(128)} %bitcast.dev_ref, f32[3,128,128]{2,1,0:T(8,128)} %bitcast.33, f32[128,128]{1,0:T(8,128)} %bitcast.38, f32[2288,286]{1,0:T(8,128)} %bitcast.43), custom_call_target="tpu_custom_call" | custom-call | flops 8000000000 | bytes 3000000 | tf_op jit(solution)/shard_map/upward/pallas_call | solution.py:549
  27.3 2.6 %all-to-all-done = s32[128,1,20]{2,1,0:T(1,128)S(1)} async-done(((s32[128,1,20]{2,1,0:T(1,128)}), s32[128,1,20]{2,1,0:T(1,128)S(1)}, u32[]{:S(2)}, u32[]{:S(2)}) %all-to-all-start) | async-done | bytes 10272 | tf_op jit(solution)/shard_map/all_to_all | solution.py:661
  29.9 0.0 copy-start.2
  29.9 0.0 collective-permute-done.before_ref
  29.9 0.0 copy-start.5
  29.9 0.0 collective-permute-done.1.after_ref
  29.9 0.0 copy-start.6
  29.9 0.6 copy-done.2
  30.5 4.1 %pack.1 = f32[6144,128]{1,0:T(8,128)} custom-call(s32[128,20]{1,0:T(8,128)} %bitcast.37, f32[3,128,128]{2,1,0:T(8,128)} %get-tuple-element.15.lt_ref, f32[3,16,128]{2,1,0:T(8,128)} %get-tuple-element.16.pt_ref, f32[3,128]{1,0:T(4,128)} %get-tuple-element.18.lift_ref), custom_call_target="tpu_custom_call" | custom-call | flops 1000000000 | bytes 4000000 | tf_op jit(solution)/shard_map/pack/pallas_call | solution.py:568
  34.6 0.0 copy-start.3
  34.6 0.0 copy-start.4
  34.6 0.0 copy-done.5
  34.6 0.0 copy-done.6
  34.6 7.2 %all-to-all-start.1 = ((f32[128,48,128]{2,1,0:T(8,128)}), f32[128,48,128]{2,1,0:T(8,128)S(1)}, u32[]{:S(2)}, u32[]{:S(2)}) async-start(f32[128,48,128]{2,1,0:T(8,128)} %bitcast.31), calls=%async_computation.1 | async-start | bytes 6291456 | tf_op jit(solution)/shard_map/all_to_all | solution.py:678
  41.8 0.0 copy-done.3
  41.8 0.1 copy.22
  41.9 0.7 reshape.56.lists_ref
  42.6 0.0 copy-done.4
  42.6 0.1 copy.23
  42.7 0.7 reshape.57.class_ref
  43.3 33.4 %near.1.near_ref = f32[128,128]{1,0:T(8,128)} custom-call(s32[1]{0:T(128)} %bitcast.dev_ref, s32[27,128]{1,0:T(8,128)} %bitcast.47, s32[27,128]{1,0:T(8,128)} %bitcast.48, f32[3,128,128]{2,1,0:T(8,128)} %bitcast.34, f32[128,128]{1,0:T(8,128)} %bitcast.39, f32[4,32,128]{2,1,0:T(8,128)} %copy-done.5, f32[4,32,128]{2,1,0:T(8,128)} %copy-done.6), custom_call_target="tpu_custom_call" | custom-call | flops 30000001024 | bytes 1000000 | tf_op jit(solution)/shard_map/near/pallas_call | solution.py:580
  76.7 7.0 %all-to-all-done.1 = f32[128,48,128]{2,1,0:T(8,128)S(1)} async-done(((f32[128,48,128]{2,1,0:T(8,128)}), f32[128,48,128]{2,1,0:T(8,128)S(1)}, u32[]{:S(2)}, u32[]{:S(2)}) %all-to-all-start.1) | async-done | bytes 3145760 | tf_op jit(solution)/shard_map/all_to_all | solution.py:678
  83.7 0.0 copy-start
  83.8 1.6 %copy-done = f32[128,48,128]{2,1,0:T(8,128)} copy-done((f32[128,48,128]{2,1,0:T(8,128)}, f32[128,48,128]{2,1,0:T(8,128)S(1)}, u32[]{:S(2)}) %copy-start) | copy-done | bytes 3145752
  85.4 30.3 %far.1 = f32[128,128]{1,0:T(8,128)} custom-call(s32[1]{0:T(128)} %bitcast.dev_ref, s32[224]{0:T(256)} %reshape.56.lists_ref, s32[224]{0:T(256)} %reshape.57.class_ref, s32[189,128]{1,0:T(8,128)} %bitcast.45, s32[189,128]{1,0:T(8,128)} %bitcast.46, s32[16,189]{1,0:T(8,128)} %parent_ref.1, s32[16,189]{1,0:T(8,128)} %parent_class_ref.1, ...), custom_call_target="tpu_custom_call" | custom-call | flops 20000000000 | bytes 20000000 | tf_op jit(solution)/shard_map/far/pallas_call | solution.py:605
  (3 shorter events, 0.0 us)
Async XLA Ops:
  1.0 19.4 %copy-start.1 = (f32[1,3,128,128]{3,2,1,0:T(8,128)}, f32[1,3,128,128]{3,2,1,0:T(8,128)S(1)}, u32[]{:S(2)}) copy-start(f32[1,3,128,128]{3,2,1,0:T(8,128)S(1)} %copy.27) | copy-start | bytes 589828
  1.8 28.1 %collective-permute-start = (f32[4,32,128]{2,1,0:T(8,128)S(1)}, f32[4,32,128]{2,1,0:T(8,128)S(1)}, u32[]{:S(2)}, u32[]{:S(2)}) collective-permute-start(f32[4,32,128]{2,1,0:T(8,128)S(1)} %pad_maximum_fusion), channel_id=1, source_target_pairs={{0,1},{1,2},{2,3},{3,4},{4,5},{5,6},{6,7},{7,8},{8,9},{9,10},{10,1... | collective-permute-start | bytes 196616 | tf_op jit(solution)/shard_map/ppermute | solution.py:671
  6.4 23.5 %collective-permute-start.1 = (f32[4,32,128]{2,1,0:T(8,128)S(1)}, f32[4,32,128]{2,1,0:T(8,128)S(1)}, u32[]{:S(2)}, u32[]{:S(2)}) collective-permute-start(f32[4,32,128]{2,1,0:T(8,128)S(1)} %pad_maximum_fusion.1), channel_id=1, source_target_pairs={{1,0},{2,1},{3,2},{4,3},{5,4},{6,5},{7,6},{8,7},{9,8},{10,9},{11,1... | collective-permute-start | bytes 196616 | tf_op jit(solution)/shard_map/ppermute | solution.py:672
  9.8 20.1 %all-to-all-start = ((s32[128,1,20]{2,1,0:T(1,128)}), s32[128,1,20]{2,1,0:T(1,128)S(1)}, u32[]{:S(2)}, u32[]{:S(2)}) async-start(s32[128,1,20]{2,1,0:T(1,128)} %bitcast.7), calls=%async_computation | async-start | bytes 131072 | tf_op jit(solution)/shard_map/all_to_all | solution.py:661
  29.9 0.6 copy-start.2
  29.9 4.7 %copy-start.5 = (f32[4,32,128]{2,1,0:T(8,128)}, f32[4,32,128]{2,1,0:T(8,128)S(1)}, u32[]{:S(2)}) copy-start(f32[4,32,128]{2,1,0:T(8,128)S(1)} %collective-permute-done.before_ref) | copy-start | bytes 196612
  29.9 4.7 %copy-start.6 = (f32[4,32,128]{2,1,0:T(8,128)}, f32[4,32,128]{2,1,0:T(8,128)S(1)}, u32[]{:S(2)}) copy-start(f32[4,32,128]{2,1,0:T(8,128)S(1)} %collective-permute-done.1.after_ref) | copy-start | bytes 196612
  34.6 7.2 %copy-start.3 = (s32[32,7]{0,1:T(8,128)S(1)}, s32[32,7]{0,1:T(8,128)}, u32[]{:S(2)}) copy-start(s32[32,7]{0,1:T(8,128)} %param.25) | copy-start | bytes 2692
  34.6 8.0 %copy-start.4 = (s32[32,7]{0,1:T(8,128)S(1)}, s32[32,7]{0,1:T(8,128)}, u32[]{:S(2)}) copy-start(s32[32,7]{0,1:T(8,128)} %param.26) | copy-start | bytes 2692
  34.6 49.1 %all-to-all-start.1 = ((f32[128,48,128]{2,1,0:T(8,128)}), f32[128,48,128]{2,1,0:T(8,128)S(1)}, u32[]{:S(2)}, u32[]{:S(2)}) async-start(f32[128,48,128]{2,1,0:T(8,128)} %bitcast.31), calls=%async_computation.1 | async-start | bytes 6291456 | tf_op jit(solution)/shard_map/all_to_all | solution.py:678
  83.7 1.6 %copy-start = (f32[128,48,128]{2,1,0:T(8,128)}, f32[128,48,128]{2,1,0:T(8,128)S(1)}, u32[]{:S(2)}) copy-start(f32[128,48,128]{2,1,0:T(8,128)S(1)} %all-to-all-done.1) | copy-start | bytes 9437188

commit v6 on v5

--- a/solution.py
+++ b/solution.py
@@ -14,7 +14,7 @@
 CAP_L = 16
 CAP_P = 4
 ROWS = 48
-PACK_MIB = 60
+PACK_MIB = 24
 TARGETS = 160
 GROUP = 128
 NOBODY = LEAF + 2 * RIM
@@ -64,6 +64,29 @@
 
 def apply_operator(operator, columns):
     return apply_parts(operator, *split(columns))
+
+
+def pieces(origin, scratch, sems, first):
+    rows = scratch.shape[0]
+    size = (rows // 4 + 7) // 8 * 8
+    return [
+        pltpu.make_async_copy(
+            origin.at[pl.ds(size * i, min(size, rows - size * i))],
+            scratch.at[pl.ds(size * i, min(size, rows - size * i))],
+            sems.at[first + i],
+        )
+        for i in range(4)
+    ]
+
+
+def start(copies):
+    for copy in copies:
+        copy.start()
+
+
+def wait(copies):
+    for copy in copies:
+        copy.wait()
 
 
 def cut(source, chunks):
@@ -107,9 +130,9 @@
 
 
 def upward_kernel(dev_ref, pos_ref, chg_ref, up_hbm, lt_ref, pt_ref, lift_ref, moments, column, up_ref,
-                  stored_up, sem):
-    copy = pltpu.make_async_copy(up_hbm, stored_up, sem)
-    copy.start()
+                  stored_up, sems):
+    copies = pieces(up_hbm, stored_up, sems, 0)
+    start(copies)
     x, y, z = [2.0 * pos_ref[d].T for d in range(3)]
     with_x = chg_ref[...].T
     z_powers = [None, z]
@@ -130,7 +153,7 @@
     for h in range(3):
         lt_ref[h] = moments[128 * h : 128 * h + 128, :].T
     column[...] = jnp.zeros_like(column)
-    copy.wait()
+    wait(copies)
     cut(stored_up, up_ref)
     lane = lax.broadcasted_iota(jnp.int32, (384, 128), 1)
     leaves = moments[...]
@@ -343,18 +366,13 @@
 
 
 def far_kernel(dev_ref, lists_ref, class_ref, leaf_ref, leaf_class_ref, parent_ref, parent_class_ref,
-               lt_ref, pt_ref, pos_ref, near_ref, arrived_hbm, down_hbm, far_hbm, out_ref,
+               lt_ref, pt_ref, pos_ref, near_ref, arrived_ref, down_hbm, far_hbm, out_ref,
                src, src_parent, even, odd, even_parent, grouped, code_scr, low_scr, turned, column, loc,
-               result, arrived_ref, down_ref, stored_down, far_ref, stored_far, sems):
-    arrival, far_copy, down_copy = [
-        pltpu.make_async_copy(origin, scratch, sems.at[i])
-        for i, (origin, scratch) in enumerate(
-            ((arrived_hbm, arrived_ref), (far_hbm, stored_far), (down_hbm, stored_down))
-        )
-    ]
-    arrival.start()
-    far_copy.start()
-    down_copy.start()
+               result, down_ref, stored_down, far_ref, stored_far, sems):
+    far_copies = pieces(far_hbm, stored_far, sems, 0)
+    down_copies = pieces(down_hbm, stored_down, sems, 4)
+    start(far_copies)
+    start(down_copies)
     lane = lax.broadcasted_iota(jnp.int32, (128, 128), 1)
 
     def count(first, capacity, table_ref):
@@ -407,7 +425,6 @@
     count(128, CAP_P, even_parent)
     count(0, CAP_L, even)
     place(src, 0, [lt_ref[h] for h in range(3)])
-    arrival.wait()
     for c in range(CAP_L):
         place(
             src,
@@ -446,7 +463,7 @@
 
     lax.fori_loop(0, 4, two_blocks, 0)
 
-    far_copy.wait()
+    wait(far_copies)
     cut(stored_far, far_ref)
     column[...] = jnp.zeros_like(column)
     loc[...] = jnp.zeros_like(loc)
@@ -487,7 +504,7 @@
             )
     upper_total = upper_total + turn(upper_total, 32)
     upper_total = upper_total + turn(upper_total, 64)
-    down_copy.wait()
+    wait(down_copies)
     cut(stored_down, down_ref)
     column[0:COEF, :] = upper_total
     coarse = jnp.broadcast_to(column[:, 16:17], (384, 128))
@@ -556,9 +573,9 @@
             pltpu.VMEM((384, 128), F32),
             pltpu.VMEM((3, 8 * COEF, 128), F32),
             pltpu.VMEM((8 * COEF, COEF), F32),
-            pltpu.SemaphoreType.DMA(()),
+            pltpu.SemaphoreType.DMA((4,)),
         ],
-        compiler_params=limits(60),
+        compiler_params=limits(40),
         cost_estimate=cost(8 * 10**9, 3 * 10**6),
         name="upward",
     )(dev, pos, chg, up_shift)
@@ -594,7 +611,7 @@
             pltpu.SMEM((40, 128), jnp.int32),
             pltpu.SemaphoreType.DMA(()),
         ],
-        compiler_params=limits(60),
+        compiler_params=limits(56),
         cost_estimate=cost(30 * 10**9, 10**6),
         name="near",
     )(dev, near_leaves, near_offsets, pos, chg, before, after)
@@ -605,7 +622,7 @@
     return pl.pallas_call(
         far_kernel,
         out_shape=shape(128, 128),
-        in_specs=[SMEM] * 3 + [VMEM] * 8 + [HBM] * 3,
+        in_specs=[SMEM] * 3 + [VMEM] * 9 + [HBM] * 2,
         out_specs=VMEM,
         scratch_shapes=[
             pltpu.VMEM((2176, 640), BF16),
@@ -620,14 +637,13 @@
             pltpu.VMEM((384, 128), F32),
             pltpu.VMEM((384, 128), F32),
             pltpu.VMEM((128, 128), F32),
-            pltpu.VMEM((128 * ROWS, 128), F32),
             pltpu.VMEM((3, 8 * COEF, 128), F32),
             pltpu.VMEM((8 * COEF, COEF), F32),
             pltpu.VMEM((3, 16 * COEF, 128), F32),
             pltpu.VMEM((16 * COEF, COEF), F32),
-            pltpu.SemaphoreType.DMA((3,)),
+            pltpu.SemaphoreType.DMA((8,)),
         ],
-        compiler_params=limits(60),
+        compiler_params=limits(52),
         cost_estimate=cost(20 * 10**9, 20 * 10**6),
         name="far",
     )(dev, lists, classes, leaves, leaf_class, parents, parent_class, lt, pt, pos, near, arrived,

time: 116 us -> 116 us (level)
  waiting for transfers between devices: 9.62 us -> 6.93 us
  starting transfers between devices: 24.3 us -> 26.6 us
    all_to_all x1, starting transfers between devices: 7.2 us -> 9.58 us  [per_device(): lax.all_to_all(outgoing, AXES, split_axis=0, concat_axis=0, tiled=True)]
    all_to_all x1, waiting for transfers between devices: 2.57 us -> 0.62 us  [per_device(): asked = lax.all_to_all(plans, AXES, split_axis=0, concat_axis=0, tiled=True)]
    pallas_call x1, Pallas kernels: 33.4 us -> 34.8 us  [near_call(): pl.pallas_call(near_kernel, out_shape=shape(128, 128), in_specs=[SMEM] +...]
    unnamed x17 -> x29, local copies, waits for them, and re-layouts: 3.41 us -> 4.85 us
  transfers between devices with their start and end apart: 4 -> 4, of which waited for: 2 -> 2; matrix products, arithmetic and copies ran while one was open for 3% -> 2% of each run, Pallas kernels for 35% -> 36%
where the time goes in v6:
time: 116 us; the launch traced here: 115 us
  Pallas kernels  73.7 us (64%)
  starting transfers between devices  26.6 us (23%)
  waiting for transfers between devices  6.93 us (6%)
  local copies, waits for them, and re-layouts  6.6 us (6%)
    pallas_call x1, Pallas kernels, near_call(): pl.pallas_call(near_kernel, out_shape=shape(128, 128), in_specs=[SMEM] +...  34.8 us
    pallas_call x1, Pallas kernels, far_call(): pl.pallas_call(far_kernel, out_shape=shape(128, 128), in_specs=[SMEM] * 3...  29.6 us
    all_to_all x1, starting transfers between devices, per_device(): asked = lax.all_to_all(plans, AXES, split_axis=0, concat_axis=0, tiled=True)  10.5 us
    all_to_all x1, starting transfers between devices, per_device(): lax.all_to_all(outgoing, AXES, split_axis=0, concat_axis=0, tiled=True)  9.58 us
    all_to_all x1, waiting for transfers between devices, per_device(): lax.all_to_all(outgoing, AXES, split_axis=0, concat_axis=0, tiled=True)  6.3 us
    pallas_call x1, Pallas kernels, upward_call(): pl.pallas_call(upward_kernel, out_shape=(shape(3, 128, 128), shape(3, 16,...  6.05 us
    unnamed x29, local copies, waits for them, and re-layouts  4.85 us
    ppermute x1, starting transfers between devices, per_device(): before = lax.ppermute(rims[0], AXES, up)  4.59 us
  transfers between devices with their start and end apart: 4, of which 2 were waited for; matrix products, arithmetic and copies ran while one was open for 2% of the time, Pallas kernels for 36%

profile of v6, /device:TPU:1, one launch (start us, length us, event | category | flops | bytes accessed | tf_op | source)
XLA Modules:
  0.0 114.9 jit_solution(16625120282056644807)
XLA Ops:
  0.0 1.0 copy.27
  1.0 0.0 copy-start
  1.0 0.8 slice_bitcast_fusion
  1.8 4.6 %collective-permute-start = (f32[4,32,128]{2,1,0:T(8,128)S(1)}, f32[4,32,128]{2,1,0:T(8,128)S(1)}, u32[]{:S(2)}, u32[]{:S(2)}) collective-permute-start(f32[4,32,128]{2,1,0:T(8,128)S(1)} %pad_maximum_fusion), channel_id=1, source_target_pairs={{0,1},{1,2},{2,3},{3,4},{4,5},{5,6},{6,7},{7,8},{8,9},{9,10},{10,1... | collective-permute-start | bytes 196616 | tf_op jit(solution)/shard_map/ppermute | solution.py:687
  6.4 1.9 %collective-permute-start.1 = (f32[4,32,128]{2,1,0:T(8,128)S(1)}, f32[4,32,128]{2,1,0:T(8,128)S(1)}, u32[]{:S(2)}, u32[]{:S(2)}) collective-permute-start(f32[4,32,128]{2,1,0:T(8,128)S(1)} %pad_maximum_fusion.1), channel_id=1, source_target_pairs={{1,0},{2,1},{3,2},{4,3},{5,4},{6,5},{7,6},{8,7},{9,8},{10,9},{11,1... | collective-permute-start | bytes 196616 | tf_op jit(solution)/shard_map/ppermute | solution.py:688
  8.3 0.7 pad_add_fusion
  9.1 0.7 copy.24
  9.8 10.5 %all-to-all-start = ((s32[128,1,20]{2,1,0:T(1,128)}), s32[128,1,20]{2,1,0:T(1,128)S(1)}, u32[]{:S(2)}, u32[]{:S(2)}) async-start(s32[128,1,20]{2,1,0:T(1,128)} %bitcast.7), calls=%async_computation | async-start | bytes 131072 | tf_op jit(solution)/shard_map/all_to_all | solution.py:677
  20.4 0.0 copy-start.2
  20.4 0.8 copy-done.2
  21.2 0.0 copy-start.3
  21.2 2.0 %copy-done.3 = f32[8,286,286]{2,0,1:T(8,128)S(1)} copy-done((f32[8,286,286]{2,0,1:T(8,128)S(1)}, f32[8,286,286]{2,0,1:T(8,128)}, u32[]{:S(2)}) %copy-start.3) | copy-done | bytes 2617496
  23.2 6.0 %upward.1 = (f32[3,128,128]{2,1,0:T(8,128)S(1)}, f32[3,16,128]{2,1,0:T(8,128)S(1)}, f32[3,128]{1,0:T(4,128)S(1)}) custom-call(s32[1]{0:T(128)} %bitcast.dev_ref, f32[3,128,128]{2,1,0:T(8,128)S(1)} %bitcast.31, f32[128,128]{1,0:T(8,128)S(1)} %bitcast.36, f32[2288,286]{1,0:T(8,128)S(1)} %bitcast.37), custom_call_target="tpu_custom_call" | custom-call | flops 8000000000 | bytes 3000000 | tf_op jit(solution)/shard_map/upward/pallas_call | solution.py:566
  29.3 0.0 copy-done
  29.3 0.6 all-to-all-done
  29.9 0.0 collective-permute-done.before_ref
  29.9 0.0 copy-start.11
  29.9 0.0 collective-permute-done.1.after_ref
  29.9 0.0 copy-start.12
  29.9 3.2 %pack.1 = f32[6144,128]{1,0:T(8,128)} custom-call(s32[128,20]{1,0:T(8,128)S(1)} %bitcast.34, f32[3,128,128]{2,1,0:T(8,128)S(1)} %get-tuple-element.15.lt_ref, f32[3,16,128]{2,1,0:T(8,128)S(1)} %get-tuple-element.16.pt_ref, f32[3,128]{1,0:T(4,128)S(1)} %get-tuple-element.18.lift_ref), custom_call_target="tpu_custom_call" | custom-call | flops 1000000000 | bytes 4000000 | tf_op jit(solution)/shard_map/pack/pallas_call | solution.py:585
  33.1 0.0 copy-start.9
  33.1 0.0 copy-start.10
  33.1 0.0 copy-done.11
  33.1 0.0 copy-done.12
  33.1 9.6 %all-to-all-start.1 = ((f32[128,48,128]{2,1,0:T(8,128)}), f32[128,48,128]{2,1,0:T(8,128)}, u32[]{:S(2)}, u32[]{:S(2)}) async-start(f32[128,48,128]{2,1,0:T(8,128)} %bitcast.12), calls=%async_computation.1 | async-start | bytes 6291456 | tf_op jit(solution)/shard_map/all_to_all | solution.py:694
  42.7 0.0 copy-done.9
  42.7 0.1 copy.22
  42.8 0.1 reshape.56.lists_ref
  42.9 0.0 copy-done.10
  42.9 0.1 copy.23
  43.0 0.1 reshape.57.class_ref
  43.1 0.0 copy-start.1
  43.1 0.0 copy-start.4
  43.2 0.0 copy-start.5
  43.2 0.0 copy-start.6
  43.2 0.0 copy-start.7
  43.2 34.8 %near.1.near_ref = f32[128,128]{1,0:T(8,128)} custom-call(s32[1]{0:T(128)} %bitcast.dev_ref, s32[27,128]{1,0:T(8,128)} %bitcast.45, s32[27,128]{1,0:T(8,128)} %bitcast.46, f32[3,128,128]{2,1,0:T(8,128)} %bitcast.32, f32[128,128]{1,0:T(8,128)} %bitcast.35, f32[4,32,128]{2,1,0:T(8,128)} %copy-done.11, f32[4,32,128]{2,1,0:T(8,128)} %copy-done.12), custom_call_target="tpu_custom_call" | custom-call | flops 30000001024 | bytes 1000000 | tf_op jit(solution)/shard_map/near/pallas_call | solution.py:597
  78.0 6.3 %all-to-all-done.1 = f32[128,48,128]{2,1,0:T(8,128)} async-done(((f32[128,48,128]{2,1,0:T(8,128)}), f32[128,48,128]{2,1,0:T(8,128)}, u32[]{:S(2)}, u32[]{:S(2)}) %all-to-all-start.1) | async-done | bytes 3145760 | tf_op jit(solution)/shard_map/all_to_all | solution.py:694
  84.3 0.0 copy-done.1
  84.3 0.0 copy-done.4
  84.3 0.0 copy-done.5
  84.3 0.0 copy-done.6
  84.4 0.0 copy-done.7
  84.4 0.0 copy-start.8
  84.4 0.8 copy-done.8
  85.2 29.6 %far.1 = f32[128,128]{1,0:T(8,128)} custom-call(s32[1]{0:T(128)} %bitcast.dev_ref, s32[224]{0:T(256)S(1)} %reshape.56.lists_ref, s32[224]{0:T(256)S(1)} %reshape.57.class_ref, s32[189,128]{1,0:T(8,128)S(1)} %bitcast.38, s32[189,128]{1,0:T(8,128)S(1)} %bitcast.39, s32[16,189]{1,0:T(8,128)S(1)} %copy-done.6, s32[16,189]{1,0:T(8,128)S(1)} %copy-done.7, ...), custom_call_target="tpu_custom_call" | custom-call | flops 20000000000 | bytes 20000000 | tf_op jit(solution)/shard_map/far/pallas_call | solution.py:622
  (3 shorter events, 0.0 us)
Async XLA Ops:
  1.0 28.3 %copy-start = (f32[1,3,128,128]{3,2,1,0:T(8,128)}, f32[1,3,128,128]{3,2,1,0:T(8,128)S(1)}, u32[]{:S(2)}) copy-start(f32[1,3,128,128]{3,2,1,0:T(8,128)S(1)} %copy.27) | copy-start | bytes 589828
  1.8 28.1 %collective-permute-start = (f32[4,32,128]{2,1,0:T(8,128)S(1)}, f32[4,32,128]{2,1,0:T(8,128)S(1)}, u32[]{:S(2)}, u32[]{:S(2)}) collective-permute-start(f32[4,32,128]{2,1,0:T(8,128)S(1)} %pad_maximum_fusion), channel_id=1, source_target_pairs={{0,1},{1,2},{2,3},{3,4},{4,5},{5,6},{6,7},{7,8},{8,9},{9,10},{10,1... | collective-permute-start | bytes 196616 | tf_op jit(solution)/shard_map/ppermute | solution.py:687
  6.4 23.5 %collective-permute-start.1 = (f32[4,32,128]{2,1,0:T(8,128)S(1)}, f32[4,32,128]{2,1,0:T(8,128)S(1)}, u32[]{:S(2)}, u32[]{:S(2)}) collective-permute-start(f32[4,32,128]{2,1,0:T(8,128)S(1)} %pad_maximum_fusion.1), channel_id=1, source_target_pairs={{1,0},{2,1},{3,2},{4,3},{5,4},{6,5},{7,6},{8,7},{9,8},{10,9},{11,1... | collective-permute-start | bytes 196616 | tf_op jit(solution)/shard_map/ppermute | solution.py:688
  9.8 20.1 %all-to-all-start = ((s32[128,1,20]{2,1,0:T(1,128)}), s32[128,1,20]{2,1,0:T(1,128)S(1)}, u32[]{:S(2)}, u32[]{:S(2)}) async-start(s32[128,1,20]{2,1,0:T(1,128)} %bitcast.7), calls=%async_computation | async-start | bytes 131072 | tf_op jit(solution)/shard_map/all_to_all | solution.py:677
  20.4 0.8 copy-start.2
  21.2 2.0 %copy-start.3 = (f32[8,286,286]{2,0,1:T(8,128)S(1)}, f32[8,286,286]{2,0,1:T(8,128)}, u32[]{:S(2)}) copy-start(f32[8,286,286]{2,0,1:T(8,128)} %param.27) | copy-start | bytes 7852420
  29.9 3.2 %copy-start.11 = (f32[4,32,128]{2,1,0:T(8,128)}, f32[4,32,128]{2,1,0:T(8,128)S(1)}, u32[]{:S(2)}) copy-start(f32[4,32,128]{2,1,0:T(8,128)S(1)} %collective-permute-done.before_ref) | copy-start | bytes 196612
  29.9 3.2 %copy-start.12 = (f32[4,32,128]{2,1,0:T(8,128)}, f32[4,32,128]{2,1,0:T(8,128)S(1)}, u32[]{:S(2)}) copy-start(f32[4,32,128]{2,1,0:T(8,128)S(1)} %collective-permute-done.1.after_ref) | copy-start | bytes 196612
  33.1 9.6 %copy-start.9 = (s32[32,7]{0,1:T(8,128)S(1)}, s32[32,7]{0,1:T(8,128)}, u32[]{:S(2)}) copy-start(s32[32,7]{0,1:T(8,128)} %param.25) | copy-start | bytes 2692
  33.1 9.8 %copy-start.10 = (s32[32,7]{0,1:T(8,128)S(1)}, s32[32,7]{0,1:T(8,128)}, u32[]{:S(2)}) copy-start(s32[32,7]{0,1:T(8,128)} %param.26) | copy-start | bytes 2692
  33.1 51.2 %all-to-all-start.1 = ((f32[128,48,128]{2,1,0:T(8,128)}), f32[128,48,128]{2,1,0:T(8,128)}, u32[]{:S(2)}, u32[]{:S(2)}) async-start(f32[128,48,128]{2,1,0:T(8,128)} %bitcast.12), calls=%async_computation.1 | async-start | bytes 6291456 | tf_op jit(solution)/shard_map/all_to_all | solution.py:694
  43.1 41.2 %copy-start.1 = (f32[1,3,128,128]{3,2,1,0:T(8,128)S(1)}, f32[1,3,128,128]{3,2,1,0:T(8,128)}, u32[]{:S(2)}) copy-start(f32[1,3,128,128]{3,2,1,0:T(8,128)} %copy-done) | copy-start | bytes 589828
  43.1 41.2 %copy-start.4 = (s32[128,189]{0,1:T(8,128)S(1)}, s32[128,189]{0,1:T(8,128)}, u32[]{:S(2)}) copy-start(s32[128,189]{0,1:T(8,128)} %param.19) | copy-start | bytes 290308
  43.2 41.2 %copy-start.5 = (s32[128,189]{0,1:T(8,128)S(1)}, s32[128,189]{0,1:T(8,128)}, u32[]{:S(2)}) copy-start(s32[128,189]{0,1:T(8,128)} %param.20) | copy-start | bytes 290308
  43.2 41.2 %copy-start.6 = (s32[16,189]{1,0:T(8,128)S(1)}, s32[16,189]{1,0:T(8,128)}, u32[]{:S(2)}) copy-start(s32[16,189]{1,0:T(8,128)} %parent_ref.1) | copy-start | bytes 36292
  43.2 41.2 %copy-start.7 = (s32[16,189]{1,0:T(8,128)S(1)}, s32[16,189]{1,0:T(8,128)}, u32[]{:S(2)}) copy-start(s32[16,189]{1,0:T(8,128)} %parent_class_ref.1) | copy-start | bytes 36292
  84.4 0.8 copy-start.8

commit v7 on v6

--- a/solution.py
+++ b/solution.py
@@ -365,25 +365,41 @@
     return jnp.where(slots < 0, -1, code), jnp.where(own, slots, lax.div(ghost, capacity))
 
 
-def far_kernel(dev_ref, lists_ref, class_ref, leaf_ref, leaf_class_ref, parent_ref, parent_class_ref,
-               lt_ref, pt_ref, pos_ref, near_ref, arrived_ref, down_hbm, far_hbm, out_ref,
-               src, src_parent, even, odd, even_parent, grouped, code_scr, low_scr, turned, column, loc,
-               result, down_ref, stored_down, far_ref, stored_far, sems):
+def count(code_ref, low_ref, first, capacity, table_ref):
+    blocks = capacity + 1
+    for t in range(16):
+        rows = pl.ds(first + t, 1)
+        table = count_rows(code_ref[rows, :], low_ref[rows, :], 16 * blocks)
+        for b in range(blocks):
+            table_ref[16 * t : 16 * t + 16, 128 * b : 128 * b + 128] = table[16 * b : 16 * b + 16]
+
+
+def counts_kernel(leaf_ref, leaf_class_ref, parent_ref, parent_class_ref, parent_table_ref, code_ref,
+                  low_ref, turned):
+    width = leaf_ref.shape[0]
+    code_ref[...] = jnp.full_like(code_ref, -1)
+    low_ref[...] = jnp.full_like(low_ref, -1)
+    for part, rows in zip(
+        encode(leaf_ref[...], leaf_class_ref[...], LEAF, CAP_L), (code_ref, low_ref)
+    ):
+        turned[...] = jnp.full_like(turned, -1.0)
+        turned[:width, :] = part.astype(F32)
+        rows[0:128, 0:128] = turned[0:128, :].T.astype(jnp.int32)
+        rows[0:128, 128:256] = turned[128:256, :].T.astype(jnp.int32)
+    for part, rows in zip(
+        encode(parent_ref[...], parent_class_ref[...], 16, CAP_P), (code_ref, low_ref)
+    ):
+        rows[128:144, :width] = part
+    count(code_ref, low_ref, 128, CAP_P, parent_table_ref)
+
+
+def far_kernel(dev_ref, lists_ref, class_ref, code_ref, low_ref, parent_table_ref, lt_ref, pt_ref,
+               pos_ref, near_ref, arrived_ref, down_hbm, far_hbm, out_ref,
+               src, src_parent, even, odd, grouped, column, loc, result, down_ref, stored_down,
+               far_ref, stored_far, sems):
     far_copies = pieces(far_hbm, stored_far, sems, 0)
     down_copies = pieces(down_hbm, stored_down, sems, 4)
-    start(far_copies)
-    start(down_copies)
     lane = lax.broadcasted_iota(jnp.int32, (128, 128), 1)
-
-    def count(first, capacity, table_ref):
-        blocks = capacity + 1
-        for t in range(16):
-            rows = pl.ds(first + t, 1)
-            table = count_rows(code_scr[rows, :], low_scr[rows, :], 16 * blocks)
-            for b in range(blocks):
-                table_ref[16 * t : 16 * t + 16, 128 * b : 128 * b + 128] = table[
-                    16 * b : 16 * b + 16
-                ]
 
     def place(ref, row, parts):
         count = parts[0].shape[0]
@@ -408,22 +424,9 @@
         part = pltpu.roll(part, 128 - 32 * p, 1) if p else part
         return jnp.where(lane < 32, part, 0.0)
 
-    width = leaf_ref.shape[0]
-    code_scr[...] = jnp.full_like(code_scr, -1)
-    low_scr[...] = jnp.full_like(low_scr, -1)
-    for part, scratch in zip(
-        encode(leaf_ref[...], leaf_class_ref[...], LEAF, CAP_L), (code_scr, low_scr)
-    ):
-        turned[...] = jnp.full_like(turned, -1.0)
-        turned[:width, :] = part.astype(F32)
-        scratch[0:128, 0:128] = turned[0:128, :].T.astype(jnp.int32)
-        scratch[0:128, 128:256] = turned[128:256, :].T.astype(jnp.int32)
-    for part, scratch in zip(
-        encode(parent_ref[...], parent_class_ref[...], 16, CAP_P), (code_scr, low_scr)
-    ):
-        scratch[128:144, :width] = part
-    count(128, CAP_P, even_parent)
-    count(0, CAP_L, even)
+    start(far_copies)
+    start(down_copies)
+    count(code_ref, low_ref, 0, CAP_L, even)
     place(src, 0, [lt_ref[h] for h in range(3)])
     for c in range(CAP_L):
         place(
@@ -439,7 +442,7 @@
             128 * (c + 1),
             [arrived_ref[pl.ds(32 + 2 * c, 128, stride=ROWS), :], arrived_ref[pl.ds(33 + 2 * c, 128, stride=ROWS), :], arrived_tail(44, c)],
         )
-    collect(nn(even_parent[...], src_parent[...]), 2048, 256)
+    collect(nn(parent_table_ref[...], src_parent[...]), 2048, 256)
     mine = dev_ref[0] // 4
     operator = lax.broadcasted_iota(jnp.int32, (16, 128), 0)
     cell = lax.broadcasted_iota(jnp.int32, (16, 128), 1) // 4
@@ -455,9 +458,9 @@
 
     def two_blocks(step, carry):
         row = pl.multiple_of(step * 512, 512)
-        count(32 * step + 16, CAP_L, odd)
+        count(code_ref, low_ref, 32 * step + 16, CAP_L, odd)
         collect(nn(even[...], src[...]), row, 256)
-        count(jnp.minimum(32 * step + 32, 112), CAP_L, even)
+        count(code_ref, low_ref, jnp.minimum(32 * step + 32, 112), CAP_L, even)
         collect(nn(odd[...], src[...]), row + 256, 256)
         return carry
 
@@ -617,23 +620,36 @@
     )(dev, near_leaves, near_offsets, pos, chg, before, after)
 
 
-def far_call(dev, lists, classes, leaves, leaf_class, parents, parent_class, lt, pt, pos, near, arrived,
-             down_shift, far_shift):
+def counts_call(leaves, leaf_class, parents, parent_class):
+    return pl.pallas_call(
+        counts_kernel,
+        out_shape=(
+            shape(256, 640, dtype=BF16),
+            shape(144, 256, dtype=jnp.int32),
+            shape(144, 256, dtype=jnp.int32),
+        ),
+        in_specs=[VMEM] * 4,
+        out_specs=(VMEM,) * 3,
+        scratch_shapes=[pltpu.VMEM((256, 128), F32)],
+        compiler_params=limits(40),
+        cost_estimate=cost(4 * 10**9, 10**6),
+        name="counts",
+    )(leaves, leaf_class, parents, parent_class)
+
+
+def far_call(dev, lists, classes, code, low, parent_table, lt, pt, pos, near, arrived, down_shift,
+             far_shift):
     return pl.pallas_call(
         far_kernel,
         out_shape=shape(128, 128),
-        in_specs=[SMEM] * 3 + [VMEM] * 9 + [HBM] * 2,
+        in_specs=[SMEM] * 3 + [VMEM] * 8 + [HBM] * 2,
         out_specs=VMEM,
         scratch_shapes=[
             pltpu.VMEM((2176, 640), BF16),
             pltpu.VMEM((640, 640), BF16),
             pltpu.VMEM((256, 2176), BF16),
             pltpu.VMEM((256, 2176), BF16),
-            pltpu.VMEM((256, 640), BF16),
             pltpu.VMEM((3, 16 * TARGETS, 128), F32),
-            pltpu.VMEM((144, 256), jnp.int32),
-            pltpu.VMEM((144, 256), jnp.int32),
-            pltpu.VMEM((256, 128), F32),
             pltpu.VMEM((384, 128), F32),
             pltpu.VMEM((384, 128), F32),
             pltpu.VMEM((128, 128), F32),
@@ -646,8 +662,8 @@
         compiler_params=limits(52),
         cost_estimate=cost(20 * 10**9, 20 * 10**6),
         name="far",
-    )(dev, lists, classes, leaves, leaf_class, parents, parent_class, lt, pt, pos, near, arrived,
-      down_shift, far_shift)
+    )(dev, lists, classes, code, low, parent_table, lt, pt, pos, near, arrived, down_shift,
+      far_shift)
 
 
 def by_rows(operators):
@@ -690,14 +706,18 @@
     before, after, asked, lt = lax.optimization_barrier((before, after, asked, lt))
     outgoing = pack_call(asked, lt, pt, lift)
     outgoing = outgoing.reshape(LEAF, ROWS, 128)
-    near_leaves, outgoing = lax.optimization_barrier((near_leaves, outgoing))
+    near_leaves, far_leaves, outgoing = lax.optimization_barrier(
+        (near_leaves, far_leaves, outgoing)
+    )
     arrived = lax.all_to_all(outgoing, AXES, split_axis=0, concat_axis=0, tiled=True)
     arrived = arrived.reshape(LEAF * ROWS, 128)
     near = near_call(dev, near_leaves.T, near_offsets.T, pos, chg, before, after)
+    parent_table, code, low = counts_call(
+        far_leaves.T, far_leaf_class.T, far_parents, far_parent_class
+    )
     potential = far_call(
-        dev, coarse_lists.reshape(-1), coarse_class.reshape(-1), far_leaves.T, far_leaf_class.T,
-        far_parents, far_parent_class, lt, pt, pos, near, arrived,
-        by_rows(down_shift), by_rows(far_shift),
+        dev, coarse_lists.reshape(-1), coarse_class.reshape(-1), code, low, parent_table, lt, pt, pos,
+        near, arrived, by_rows(down_shift), by_rows(far_shift),
     )
     return potential.reshape(-1)
 

time: 116 us -> 116 us (level)
    pallas_call x1, Pallas kernels: 34.8 us -> 33.3 us  [near_call(): pl.pallas_call(near_kernel, out_shape=shape(128, 128), in_specs=[SMEM] +...]
    all_to_all x1, waiting for transfers between devices: 6.3 us -> 7.62 us  [per_device(): lax.all_to_all(outgoing, AXES, split_axis=0, concat_axis=0, tiled=True)]
  transfers between devices with their start and end apart: 4 -> 4, of which waited for: 2 -> 1; matrix products, arithmetic and copies ran while one was open for 2% -> 2% of each run, Pallas kernels for 36% -> 35%
where the time goes in v7:
time: 116 us; the launch traced here: 115 us
  Pallas kernels  72.8 us (63%)
  starting transfers between devices  27.2 us (23%)
  waiting for transfers between devices  7.62 us (7%)
  local copies, waits for them, and re-layouts  6.54 us (6%)
    pallas_call x1, Pallas kernels, near_call(): pl.pallas_call(near_kernel, out_shape=shape(128, 128), in_specs=[SMEM] +...  33.3 us
    pallas_call x1, Pallas kernels, far_call(): pl.pallas_call(far_kernel, out_shape=shape(128, 128), in_specs=[SMEM] * 3...  29.6 us
    all_to_all x1, starting transfers between devices, per_device(): asked = lax.all_to_all(plans, AXES, split_axis=0, concat_axis=0, tiled=True)  11.5 us
    all_to_all x1, starting transfers between devices, per_device(): lax.all_to_all(outgoing, AXES, split_axis=0, concat_axis=0, tiled=True)  10.3 us
    all_to_all x1, waiting for transfers between devices, per_device(): lax.all_to_all(outgoing, AXES, split_axis=0, concat_axis=0, tiled=True)  7.62 us
    pallas_call x1, Pallas kernels, upward_call(): pl.pallas_call(upward_kernel, out_shape=(shape(3, 128, 128), shape(3, 16,...  6.05 us
    unnamed x29, local copies, waits for them, and re-layouts  4.85 us
    ppermute x1, starting transfers between devices, per_device(): before = lax.ppermute(rims[0], AXES, up)  3.54 us
  transfers between devices with their start and end apart: 4, of which 1 were waited for; matrix products, arithmetic and copies ran while one was open for 2% of the time, Pallas kernels for 35%

profile of v7, /device:TPU:1, one launch (start us, length us, event | category | flops | bytes accessed | tf_op | source)
XLA Modules:
  0.0 115.3 jit_solution(9949006545708391347)
XLA Ops:
  0.0 0.7 pad_add_fusion
  0.7 0.7 copy.24
  1.5 11.5 %all-to-all-start = ((s32[128,1,20]{2,1,0:T(1,128)}), s32[128,1,20]{2,1,0:T(1,128)S(1)}, u32[]{:S(2)}, u32[]{:S(2)}) async-start(s32[128,1,20]{2,1,0:T(1,128)} %bitcast.5), calls=%async_computation | async-start | bytes 131072 | tf_op jit(solution)/shard_map/all_to_all | solution.py:693
  13.0 0.7 slice_bitcast_fusion
  13.7 1.0 copy.27
  14.7 0.0 copy-start
  14.7 3.5 %collective-permute-start = (f32[4,32,128]{2,1,0:T(8,128)S(1)}, f32[4,32,128]{2,1,0:T(8,128)S(1)}, u32[]{:S(2)}, u32[]{:S(2)}) collective-permute-start(f32[4,32,128]{2,1,0:T(8,128)S(1)} %pad_maximum_fusion), channel_id=1, source_target_pairs={{0,1},{1,2},{2,3},{3,4},{4,5},{5,6},{6,7},{7,8},{8,9},{9,10},{10,1... | collective-permute-start | bytes 196616 | tf_op jit(solution)/shard_map/ppermute | solution.py:703
  18.3 1.9 %collective-permute-start.1 = (f32[4,32,128]{2,1,0:T(8,128)S(1)}, f32[4,32,128]{2,1,0:T(8,128)S(1)}, u32[]{:S(2)}, u32[]{:S(2)}) collective-permute-start(f32[4,32,128]{2,1,0:T(8,128)S(1)} %pad_maximum_fusion.1), channel_id=1, source_target_pairs={{1,0},{2,1},{3,2},{4,3},{5,4},{6,5},{7,6},{8,7},{9,8},{10,9},{11,1... | collective-permute-start | bytes 196616 | tf_op jit(solution)/shard_map/ppermute | solution.py:704
  20.2 0.0 copy-start.2
  20.2 0.8 copy-done.2
  21.1 0.0 copy-start.3
  21.1 2.0 %copy-done.3 = f32[8,286,286]{2,0,1:T(8,128)S(1)} copy-done((f32[8,286,286]{2,0,1:T(8,128)S(1)}, f32[8,286,286]{2,0,1:T(8,128)}, u32[]{:S(2)}) %copy-start.3) | copy-done | bytes 2617496
  23.1 0.0 copy-start.9
  23.1 0.0 copy-start.10
  23.1 6.0 %upward.1 = (f32[3,128,128]{2,1,0:T(8,128)S(1)}, f32[3,16,128]{2,1,0:T(8,128)S(1)}, f32[3,128]{1,0:T(4,128)S(1)}) custom-call(s32[1]{0:T(128)} %bitcast.dev_ref, f32[3,128,128]{2,1,0:T(8,128)S(1)} %bitcast.31, f32[128,128]{1,0:T(8,128)S(1)} %bitcast.36, f32[2288,286]{1,0:T(8,128)S(1)} %bitcast.37), custom_call_target="tpu_custom_call" | custom-call | flops 8000000000 | bytes 3000000 | tf_op jit(solution)/shard_map/upward/pallas_call | solution.py:569
  29.1 0.0 copy-done
  29.1 0.0 copy-done.9
  29.1 0.1 copy.22
  29.2 0.1 reshape.56.lists_ref
  29.3 0.0 copy-done.10
  29.3 0.1 copy.23
  29.4 0.1 reshape.57.class_ref
  29.5 0.0 all-to-all-done
  29.5 0.0 collective-permute-done.before_ref
  29.6 0.0 copy-start.11
  29.6 0.0 collective-permute-done.1.after_ref
  29.6 0.0 copy-start.12
  29.6 3.2 %pack.1 = f32[6144,128]{1,0:T(8,128)} custom-call(s32[128,20]{1,0:T(8,128)S(1)} %bitcast.34, f32[3,128,128]{2,1,0:T(8,128)S(1)} %get-tuple-element.20.lt_ref, f32[3,16,128]{2,1,0:T(8,128)S(1)} %get-tuple-element.21.pt_ref, f32[3,128]{1,0:T(4,128)S(1)} %get-tuple-element.22.lift_ref), custom_call_target="tpu_custom_call" | custom-call | flops 1000000000 | bytes 4000000 | tf_op jit(solution)/shard_map/pack/pallas_call | solution.py:588
  32.8 0.0 copy-start.4
  32.8 0.0 copy-start.5
  32.8 0.0 copy-start.6
  32.8 0.0 copy-start.7
  32.8 0.0 copy-done.11
  32.8 0.0 copy-done.12
  32.8 10.3 %all-to-all-start.1 = ((f32[128,48,128]{2,1,0:T(8,128)}), f32[128,48,128]{2,1,0:T(8,128)}, u32[]{:S(2)}, u32[]{:S(2)}) async-start(f32[128,48,128]{2,1,0:T(8,128)} %bitcast.10), calls=%async_computation.1 | async-start | bytes 6291456 | tf_op jit(solution)/shard_map/all_to_all | solution.py:712
  43.1 0.0 copy-done.4
  43.1 0.0 copy-done.5
  43.1 0.0 copy-done.6
  43.1 0.0 copy-done.7
  43.1 0.6 counts.1
  43.7 0.0 copy-start.1
  43.7 33.3 %near.1.near_ref = f32[128,128]{1,0:T(8,128)} custom-call(s32[1]{0:T(128)} %bitcast.dev_ref, s32[27,128]{1,0:T(8,128)} %bitcast.45, s32[27,128]{1,0:T(8,128)} %bitcast.46, f32[3,128,128]{2,1,0:T(8,128)} %bitcast.32, f32[128,128]{1,0:T(8,128)} %bitcast.35, f32[4,32,128]{2,1,0:T(8,128)} %copy-done.11, f32[4,32,128]{2,1,0:T(8,128)} %copy-done.12), custom_call_target="tpu_custom_call" | custom-call | flops 30000001024 | bytes 1000000 | tf_op jit(solution)/shard_map/near/pallas_call | solution.py:600
  77.1 7.6 %all-to-all-done.1 = f32[128,48,128]{2,1,0:T(8,128)} async-done(((f32[128,48,128]{2,1,0:T(8,128)}), f32[128,48,128]{2,1,0:T(8,128)}, u32[]{:S(2)}, u32[]{:S(2)}) %all-to-all-start.1) | async-done | bytes 3145760 | tf_op jit(solution)/shard_map/all_to_all | solution.py:712
  84.7 0.0 copy-done.1
  84.7 0.0 copy-start.8
  84.7 0.8 copy-done.8
  85.5 29.6 %far.1 = f32[128,128]{1,0:T(8,128)} custom-call(s32[1]{0:T(128)} %bitcast.dev_ref, s32[224]{0:T(256)S(1)} %reshape.56.lists_ref, s32[224]{0:T(256)S(1)} %reshape.57.class_ref, s32[144,256]{1,0:T(8,128)S(1)} %get-tuple-element.24.code_ref, s32[144,256]{1,0:T(8,128)S(1)} %get-tuple-element.25.low_ref, bf16[256,640]{1,0:T(8,128)(2,1)S(1)} %get-tuple-element.26.parent_table_ref, ...), custom_call_target="tpu_custom_call" | custom-call | flops 20000000000 | bytes 20000000 | tf_op jit(solution)/shard_map/far/pallas_call | solution.py:642
  (3 shorter events, 0.0 us)
Async XLA Ops:
  1.5 28.1 %all-to-all-start = ((s32[128,1,20]{2,1,0:T(1,128)}), s32[128,1,20]{2,1,0:T(1,128)S(1)}, u32[]{:S(2)}, u32[]{:S(2)}) async-start(s32[128,1,20]{2,1,0:T(1,128)} %bitcast.5), calls=%async_computation | async-start | bytes 131072 | tf_op jit(solution)/shard_map/all_to_all | solution.py:693
  14.7 14.4 %copy-start = (f32[1,3,128,128]{3,2,1,0:T(8,128)}, f32[1,3,128,128]{3,2,1,0:T(8,128)S(1)}, u32[]{:S(2)}) copy-start(f32[1,3,128,128]{3,2,1,0:T(8,128)S(1)} %copy.27) | copy-start | bytes 589828
  14.7 14.8 %collective-permute-start = (f32[4,32,128]{2,1,0:T(8,128)S(1)}, f32[4,32,128]{2,1,0:T(8,128)S(1)}, u32[]{:S(2)}, u32[]{:S(2)}) collective-permute-start(f32[4,32,128]{2,1,0:T(8,128)S(1)} %pad_maximum_fusion), channel_id=1, source_target_pairs={{0,1},{1,2},{2,3},{3,4},{4,5},{5,6},{6,7},{7,8},{8,9},{9,10},{10,1... | collective-permute-start | bytes 196616 | tf_op jit(solution)/shard_map/ppermute | solution.py:703
  18.3 11.3 %collective-permute-start.1 = (f32[4,32,128]{2,1,0:T(8,128)S(1)}, f32[4,32,128]{2,1,0:T(8,128)S(1)}, u32[]{:S(2)}, u32[]{:S(2)}) collective-permute-start(f32[4,32,128]{2,1,0:T(8,128)S(1)} %pad_maximum_fusion.1), channel_id=1, source_target_pairs={{1,0},{2,1},{3,2},{4,3},{5,4},{6,5},{7,6},{8,7},{9,8},{10,9},{11,1... | collective-permute-start | bytes 196616 | tf_op jit(solution)/shard_map/ppermute | solution.py:704
  20.2 0.8 copy-start.2
  21.1 2.0 %copy-start.3 = (f32[8,286,286]{2,0,1:T(8,128)S(1)}, f32[8,286,286]{2,0,1:T(8,128)}, u32[]{:S(2)}) copy-start(f32[8,286,286]{2,0,1:T(8,128)} %param.27) | copy-start | bytes 7852420
  23.1 6.1 %copy-start.9 = (s32[32,7]{0,1:T(8,128)S(1)}, s32[32,7]{0,1:T(8,128)}, u32[]{:S(2)}) copy-start(s32[32,7]{0,1:T(8,128)} %param.25) | copy-start | bytes 2692
  23.1 6.3 %copy-start.10 = (s32[32,7]{0,1:T(8,128)S(1)}, s32[32,7]{0,1:T(8,128)}, u32[]{:S(2)}) copy-start(s32[32,7]{0,1:T(8,128)} %param.26) | copy-start | bytes 2692
  29.6 3.2 %copy-start.11 = (f32[4,32,128]{2,1,0:T(8,128)}, f32[4,32,128]{2,1,0:T(8,128)S(1)}, u32[]{:S(2)}) copy-start(f32[4,32,128]{2,1,0:T(8,128)S(1)} %collective-permute-done.before_ref) | copy-start | bytes 196612
  29.6 3.2 %copy-start.12 = (f32[4,32,128]{2,1,0:T(8,128)}, f32[4,32,128]{2,1,0:T(8,128)S(1)}, u32[]{:S(2)}) copy-start(f32[4,32,128]{2,1,0:T(8,128)S(1)} %collective-permute-done.1.after_ref) | copy-start | bytes 196612
  32.8 10.3 %copy-start.4 = (s32[128,189]{0,1:T(8,128)S(1)}, s32[128,189]{0,1:T(8,128)}, u32[]{:S(2)}) copy-start(s32[128,189]{0,1:T(8,128)} %param.19) | copy-start | bytes 290308
  32.8 10.3 %copy-start.5 = (s32[128,189]{0,1:T(8,128)S(1)}, s32[128,189]{0,1:T(8,128)}, u32[]{:S(2)}) copy-start(s32[128,189]{0,1:T(8,128)} %param.20) | copy-start | bytes 290308
  32.8 10.3 %copy-start.6 = (s32[16,189]{1,0:T(8,128)S(1)}, s32[16,189]{1,0:T(8,128)}, u32[]{:S(2)}) copy-start(s32[16,189]{1,0:T(8,128)} %parent_ref.1) | copy-start | bytes 36292
  32.8 10.3 %copy-start.7 = (s32[16,189]{1,0:T(8,128)S(1)}, s32[16,189]{1,0:T(8,128)}, u32[]{:S(2)}) copy-start(s32[16,189]{1,0:T(8,128)} %parent_class_ref.1) | copy-start | bytes 36292
  32.8 51.9 %all-to-all-start.1 = ((f32[128,48,128]{2,1,0:T(8,128)}), f32[128,48,128]{2,1,0:T(8,128)}, u32[]{:S(2)}, u32[]{:S(2)}) async-start(f32[128,48,128]{2,1,0:T(8,128)} %bitcast.10), calls=%async_computation.1 | async-start | bytes 6291456 | tf_op jit(solution)/shard_map/all_to_all | solution.py:712
  43.7 41.0 %copy-start.1 = (f32[1,3,128,128]{3,2,1,0:T(8,128)S(1)}, f32[1,3,128,128]{3,2,1,0:T(8,128)}, u32[]{:S(2)}) copy-start(f32[1,3,128,128]{3,2,1,0:T(8,128)} %copy-done) | copy-start | bytes 589828
  84.7 0.8 copy-start.8
